TPU v7x, 32 devices: a whole 2x2x4 slice. The times are simulated.
32 devices in a mesh: section: 2 (over core), dp: 4 (over y, x), fsdp: 4 (over z).
Axes of the slice: x: 2, y: 2, z: 4, core: 2. Of those that a mesh axis runs over, the one named last changes fastest.
Arguments:
- token_ids: int32 [32, 128], P(('dp', 'fsdp')), may hold values from 0 to 31999
- next_ids: int32 [32, 128], P(('dp', 'fsdp')), may hold values from 0 to 31999
- seq_lengths: int32 [32], replicated, may hold values from 32 to 128, as said below
- embedding: float32 [32000, 768], P('fsdp'), may hold values from -6 to 6
- embedding_mom: float32 [32000, 768], P('fsdp'), may hold values from -2.9802322e-07 to 2.9802322e-07
- embedding_sec: float32 [32000, 768], P('fsdp'), may hold values from 3.6747965e-15 to 1.4699186e-14
- head_table: float32 [768, 32000], P(None, 'fsdp')
- head_mom: float32 [768, 32000], P(None, 'fsdp'), may hold values from -1.9073486e-06 to 1.9073486e-06
- head_sec: float32 [768, 32000], P(None, 'fsdp'), may hold values from 7.349593e-14 to 2.9398372e-13
- w_qkv: float32 [2, 768, 2304], P('section', 'fsdp'), may hold values from -0.21875 to 0.21875
- qkv_mom: float32 [2, 768, 2304], P('section', 'fsdp'), may hold values from -1.9073486e-06 to 1.9073486e-06
- qkv_sec: float32 [2, 768, 2304], P('section', 'fsdp'), may hold values from 7.349593e-14 to 2.9398372e-13
- w_out: float32 [2, 768, 768], P('section', 'fsdp'), may hold values from -0.875 to 0.875
- out_mom: float32 [2, 768, 768], P('section', 'fsdp'), may hold values from -1.9073486e-06 to 1.9073486e-06
- out_sec: float32 [2, 768, 768], P('section', 'fsdp'), may hold values from 7.349593e-14 to 2.9398372e-13
- w_gateup: float32 [2, 768, 6144], P('section', 'fsdp'), may hold values from -0.21875 to 0.21875
- gateup_mom: float32 [2, 768, 6144], P('section', 'fsdp'), may hold values from -1.9073486e-06 to 1.9073486e-06
- gateup_sec: float32 [2, 768, 6144], P('section', 'fsdp'), may hold values from 7.349593e-14 to 2.9398372e-13
- w_down: float32 [2, 3072, 768], P('section', 'fsdp'), may hold values from -0.109375 to 0.109375
- down_mom: float32 [2, 3072, 768], P('section', 'fsdp'), may hold values from -1.9073486e-06 to 1.9073486e-06
- down_sec: float32 [2, 3072, 768], P('section', 'fsdp'), may hold values from 7.349593e-14 to 2.9398372e-13
- gains: float32 [2, 3, 768], P('section', None, 'fsdp')
- gains_mom: float32 [2, 3, 768], P('section', None, 'fsdp'), may hold values from -9.536743e-06 to 9.536743e-06
- gains_sec: float32 [2, 3, 768], P('section', None, 'fsdp'), may hold values from 1.9108942e-12 to 7.349593e-12
Outputs:
- loss_sum: float32 [], replicated
- token_count: float32 [], replicated
- grad_norm: float32 [], replicated
- new_embedding: float32 [32000, 768], P('fsdp')
- new_embedding_mom: float32 [32000, 768], P('fsdp')
- new_embedding_sec: float32 [32000, 768], P('fsdp')
- embedding_bf16: bfloat16 [32000, 768], P('fsdp')
- new_head: float32 [768, 32000], P(None, 'fsdp')
- new_head_mom: float32 [768, 32000], P(None, 'fsdp')
- new_head_sec: float32 [768, 32000], P(None, 'fsdp')
- head_bf16: bfloat16 [768, 32000], P(None, 'fsdp')
- new_qkv: float32 [2, 768, 2304], P('section', 'fsdp')
- new_qkv_mom: float32 [2, 768, 2304], P('section', 'fsdp')
- new_qkv_sec: float32 [2, 768, 2304], P('section', 'fsdp')
- qkv_bf16: bfloat16 [2, 768, 2304], P('section', 'fsdp')
- new_out: float32 [2, 768, 768], P('section', 'fsdp')
- new_out_mom: float32 [2, 768, 768], P('section', 'fsdp')
- new_out_sec: float32 [2, 768, 768], P('section', 'fsdp')
- out_bf16: bfloat16 [2, 768, 768], P('section', 'fsdp')
- new_gateup: float32 [2, 768, 6144], P('section', 'fsdp')
- new_gateup_mom: float32 [2, 768, 6144], P('section', 'fsdp')
- new_gateup_sec: float32 [2, 768, 6144], P('section', 'fsdp')
- gateup_bf16: bfloat16 [2, 768, 6144], P('section', 'fsdp')
- new_down: float32 [2, 3072, 768], P('section', 'fsdp')
- new_down_mom: float32 [2, 3072, 768], P('section', 'fsdp')
- new_down_sec: float32 [2, 3072, 768], P('section', 'fsdp')
- down_bf16: bfloat16 [2, 3072, 768], P('section', 'fsdp')
- new_gains: float32 [2, 3, 768], P('section', None, 'fsdp')
- new_gains_mom: float32 [2, 3, 768], P('section', None, 'fsdp')
- new_gains_sec: float32 [2, 3, 768], P('section', None, 'fsdp')
Inputs may be any that keep to these rules, and one draw needn't show every extreme that they name: Positions p < seq_lengths[i] of row i are real tokens, the rest padding; some row has all 128 positions real.
All inputs are finite; a program needn't handle non-finite values.
Results may differ from a plain program's by a relative error of at most 0.028.
The roundings to bfloat16 on the way count: a program that leaves them out, or rounds other values in their place, can miss the bound.
Values may be sent and summed in bfloat16 or wider, within the bound.
A program may use at most 704 MiB of HBM per device.

v0:
```python
import math

import jax
import jax.numpy as jnp
from jax import lax
from jax.sharding import PartitionSpec as P

D = 768
HEADS = 12
HEAD_DIM = 64
FF = 3072
ROW = 128
MB = 2
STEP_COUNT = 10


EPS = 1e-05
MTP_WEIGHT = 0.3
CLIP = 0.01
BETA1 = 0.9
BETA2 = 0.95
ADAM_EPS = 1e-08


def joined(value, axis, join):
    pieces = jax.tree.map(lambda part: lax.all_gather(part, axis), value)
    head = jax.tree.map(lambda part: part[0], pieces)
    tail = jax.tree.map(lambda part: part[1:], pieces)
    running, _ = lax.scan(lambda running, share: (join(running, share), None), head, tail)
    return running


def from_partner(block, axis, distance):
    count = lax.axis_size(axis)
    route = []
    for low in range(count):
        high = low | 1 << distance
        if high != low and high < count:
            route += [(low, high), (high, low)]
    return lax.ppermute(block, axis, route)


def norm_fwd(values, scale_gain):
    inverse = lax.rsqrt(jnp.mean(values * values, axis=-1, keepdims=True) + EPS)
    return values * inverse * scale_gain


def norm_back(values, scale_gain, upstream):
    _, pullback = jax.vjp(norm_fwd, values, scale_gain)
    return pullback(upstream)


def rope_tables(row_count, head_width):
    half_width = head_width // 2
    position = jnp.arange(row_count, dtype=jnp.float32)[:, None]
    frequency = 10000.0 ** (-jnp.arange(half_width, dtype=jnp.float32) / half_width)
    angles = position * frequency[None, :]
    return (jnp.cos(angles), jnp.sin(angles))


def rotate(values, cosine, sine_table):
    half_width = values.shape[-1] // 2
    first, second = (values[..., :half_width], values[..., half_width:])
    return jnp.concatenate(
        [first * cosine - second * sine_table, second * cosine + first * sine_table], axis=-1
    )


def contract_rows(left, right):
    return lax.dot_general(
        left, right, (((0,), (0,)), ((), ())), preferred_element_type=jnp.float32
    )


def contract_cols(left, right):
    return lax.dot_general(
        left, right, (((1,), (1,)), ((), ())), preferred_element_type=jnp.float32
    )


def swiglu(gate_up):
    return jax.nn.silu(gate_up[:, :FF]) * gate_up[:, FF:]


def layer_fwd(inputs, weights):
    w_qkv, w_out, w_gateup, w_down, attn_gain, ffn_gain = weights
    row_count = inputs.shape[0]
    normed = norm_fwd(inputs, attn_gain).astype(jnp.bfloat16)
    packed = jnp.dot(normed, w_qkv, preferred_element_type=jnp.float32)
    split = packed.reshape(row_count, 3, HEADS, HEAD_DIM).transpose(1, 2, 0, 3)
    cosine, sine_table = rope_tables(row_count, HEAD_DIM)
    queries = rotate(split[0], cosine, sine_table).astype(jnp.bfloat16)
    keys_rot = rotate(split[1], cosine, sine_table).astype(jnp.bfloat16)
    values_low = split[2].astype(jnp.bfloat16)
    scores = jnp.einsum(
        "hqd,hkd->hqk", queries, keys_rot, preferred_element_type=jnp.float32
    ) * HEAD_DIM ** (-0.5)
    position = jnp.arange(row_count)
    causal = position[:, None] >= position[None, :]
    scores = jnp.where(causal[None], scores, -1e30)
    shifted = jnp.exp(scores - jnp.max(scores, axis=-1, keepdims=True))
    probs = shifted / jnp.sum(shifted, axis=-1, keepdims=True)
    probs_low = probs.astype(jnp.bfloat16)
    mixed = jnp.einsum("hqk,hkd->hqd", probs_low, values_low, preferred_element_type=jnp.float32)
    mixed_low = mixed.transpose(1, 0, 2).reshape(row_count, D).astype(jnp.bfloat16)
    after_attn = inputs + jnp.dot(mixed_low, w_out, preferred_element_type=jnp.float32)
    normed_ffn = norm_fwd(after_attn, ffn_gain).astype(jnp.bfloat16)
    gate_up = jnp.dot(normed_ffn, w_gateup, preferred_element_type=jnp.float32)
    hidden = swiglu(gate_up).astype(jnp.bfloat16)
    output = after_attn + jnp.dot(hidden, w_down, preferred_element_type=jnp.float32)
    saved = (
        normed,
        queries,
        keys_rot,
        values_low,
        probs,
        probs_low,
        mixed_low,
        after_attn,
        normed_ffn,
        gate_up,
        hidden,
    )
    return (output, saved)


def layer_back(inputs, weights, saved, upstream):
    w_qkv, w_out, w_gateup, w_down, attn_gain, ffn_gain = weights
    (
        normed,
        queries,
        keys_rot,
        values_low,
        probs,
        probs_low,
        mixed_low,
        after_attn,
        normed_ffn,
        gate_up,
        hidden,
    ) = saved
    row_count = inputs.shape[0]
    upstream_low = upstream.astype(jnp.bfloat16)
    grad_down = contract_rows(hidden, upstream_low)
    grad_hidden = contract_cols(upstream_low, w_down)
    _, pullback = jax.vjp(swiglu, gate_up)
    grad_gu = pullback(grad_hidden)[0].astype(jnp.bfloat16)
    grad_gateup = contract_rows(normed_ffn, grad_gu)
    grad_nffn = contract_cols(grad_gu, w_gateup)
    back_ffn, grad_ffn_gain = norm_back(after_attn, ffn_gain, grad_nffn)
    grad_after = upstream + back_ffn
    after_low = grad_after.astype(jnp.bfloat16)
    grad_out = contract_rows(mixed_low, after_low)
    grad_mixed = contract_cols(after_low, w_out).astype(jnp.bfloat16)
    grad_mixed = grad_mixed.reshape(row_count, HEADS, HEAD_DIM).transpose(1, 0, 2)
    grad_probs = jnp.einsum(
        "hqd,hkd->hqk", grad_mixed, values_low, preferred_element_type=jnp.float32
    )
    grad_values = jnp.einsum(
        "hqk,hqd->hkd", probs_low, grad_mixed, preferred_element_type=jnp.float32
    )
    grad_scores = probs * (grad_probs - jnp.sum(probs * grad_probs, axis=-1, keepdims=True))
    grad_scores = grad_scores.astype(jnp.bfloat16)
    scale_attn = HEAD_DIM ** (-0.5)
    grad_query = (
        jnp.einsum("hqk,hkd->hqd", grad_scores, keys_rot, preferred_element_type=jnp.float32)
        * scale_attn
    )
    grad_key = (
        jnp.einsum("hqk,hqd->hkd", grad_scores, queries, preferred_element_type=jnp.float32)
        * scale_attn
    )
    cosine, sine_table = rope_tables(row_count, HEAD_DIM)
    grad_query = rotate(grad_query, cosine, -sine_table)
    grad_key = rotate(grad_key, cosine, -sine_table)
    grad_packed = jnp.stack([grad_query, grad_key, grad_values]).transpose(2, 0, 1, 3)
    grad_packed = grad_packed.reshape(row_count, 3 * D).astype(jnp.bfloat16)
    grad_qkv = contract_rows(normed, grad_packed)
    grad_normed = contract_cols(grad_packed, w_qkv)
    back_attn, grad_attn_gain = norm_back(inputs, attn_gain, grad_normed)
    grad_inputs = grad_after + back_attn
    return (
        grad_inputs,
        (grad_qkv, grad_out, grad_gateup, grad_down),
        (grad_attn_gain, grad_ffn_gain),
    )


def combine_stats(first_part, second_part):
    high_a, total_a, picked_a = first_part
    high_b, total_b, picked_b = second_part
    highest = jnp.maximum(high_a, high_b)
    summed = total_a * jnp.exp(high_a - highest) + total_b * jnp.exp(high_b - highest)
    return (highest, summed, picked_a + picked_b)


def head_pass(rows_low, targets, weights_tok, head_low, vocab_start, token_total):
    gathered = lax.all_gather(rows_low, "fsdp", axis=0, tiled=True)
    total_rows = gathered.shape[0]
    block = math.gcd(total_rows, 2048)
    blocks_n = total_rows // block
    local_vocab = head_low.shape[1]
    columns = jnp.arange(local_vocab, dtype=jnp.int32)
    row_blocks = gathered.reshape(blocks_n, block, D)
    local_targets = (targets - vocab_start).reshape(blocks_n, block)

    def block_stats(pair):
        piece, target_blk = pair
        logits = jnp.dot(piece, head_low, preferred_element_type=jnp.float32)
        highest = jnp.max(logits, axis=-1)
        summed = jnp.sum(jnp.exp(logits - highest[:, None]), axis=-1)
        picked = jnp.sum(jnp.where(columns[None, :] == target_blk[:, None], logits, 0.0), axis=-1)
        return (highest, summed, picked)

    highs, sums_exp, picks = lax.map(block_stats, (row_blocks, local_targets))
    merged = joined(
        (highs.reshape(-1), sums_exp.reshape(-1), picks.reshape(-1)), "fsdp", combine_stats
    )
    lse = merged[0] + jnp.log(merged[1])
    loss_part = jnp.sum((lse - merged[2]) * weights_tok)
    factor = (weights_tok / token_total).reshape(blocks_n, block)

    def block_grads(quad):
        piece, target_blk, lse_blk, factor_blk = quad
        logits = jnp.dot(piece, head_low, preferred_element_type=jnp.float32)
        onehot = (columns[None, :] == target_blk[:, None]).astype(jnp.float32)
        return ((jnp.exp(logits - lse_blk[:, None]) - onehot) * factor_blk[:, None]).astype(
            jnp.bfloat16
        )

    grads_low = lax.map(
        block_grads, (row_blocks, local_targets, lse.reshape(blocks_n, block), factor)
    )
    grads_low = grads_low.reshape(total_rows, local_vocab)
    grad_head = contract_rows(gathered, grads_low)
    piece = grads_low
    grad_rows = lax.psum_scatter(
        contract_cols(piece, head_low), "fsdp", scatter_dimension=0, tiled=True
    )
    return (loss_part, grad_head, grad_rows)


def adam_update(weight, grad, first_mom, second_mom, rate, decay):
    mom_new = BETA1 * first_mom + (1.0 - BETA1) * grad
    sec_new = BETA2 * second_mom + (1.0 - BETA2) * grad * grad
    mom_hat = mom_new / (1.0 - BETA1**STEP_COUNT)
    sec_hat = sec_new / (1.0 - BETA2**STEP_COUNT)
    weight_new = weight - rate * (mom_hat / (jnp.sqrt(sec_hat) + ADAM_EPS) + decay * weight)
    return (weight_new, mom_new, sec_new)


def per_device(
    token_ids,
    next_ids,
    seq_lengths,
    embedding,
    embedding_mom,
    embedding_sec,
    head_table,
    head_mom,
    head_sec,
    w_qkv,
    qkv_mom,
    qkv_sec,
    w_out,
    out_mom,
    out_sec,
    w_gateup,
    gateup_mom,
    gateup_sec,
    w_down,
    down_mom,
    down_sec,
    gains,
    gains_mom,
    gains_sec,
):
    groups = lax.axis_size("fsdp")
    replicas_n = lax.axis_size("dp")
    first = lax.axis_index("section") == 0
    first_f = first.astype(jnp.float32)
    token_total = jnp.sum(seq_lengths).astype(jnp.float32)
    my_tokens = jnp.concatenate([token_ids.reshape(-1), next_ids.reshape(-1)])
    group_all = lax.all_gather(my_tokens, "fsdp", axis=0, tiled=True)
    table_low = embedding.astype(jnp.bfloat16)
    vocab_rows = table_low.shape[0]
    vocab_start = lax.axis_index("fsdp") * vocab_rows
    local = group_all.reshape(groups, -1) - vocab_start
    inside = (local >= 0) & (local < vocab_rows)
    found = jnp.take(table_low, jnp.clip(local, 0, vocab_rows - 1), axis=0)
    found = jnp.where(inside[..., None], found, jnp.zeros((), jnp.bfloat16))
    arrived = lax.all_to_all(found, "fsdp", split_axis=0, concat_axis=0, tiled=True)
    looked = jnp.sum(arrived, axis=0, dtype=jnp.float32)
    inputs_all = looked[: MB * ROW].reshape(MB, ROW, D)
    next_embed = looked[MB * ROW :].reshape(MB, ROW, D)
    gathered_w = (
        lax.all_gather(w_qkv[0].astype(jnp.bfloat16), "fsdp", axis=0, tiled=True),
        lax.all_gather(w_out[0].astype(jnp.bfloat16), "fsdp", axis=0, tiled=True),
        lax.all_gather(w_gateup[0].astype(jnp.bfloat16), "fsdp", axis=0, tiled=True),
        lax.all_gather(w_down[0].astype(jnp.bfloat16), "fsdp", axis=0, tiled=True),
        lax.all_gather(gains[0].astype(jnp.bfloat16), "fsdp", axis=1, tiled=True),
    )
    gains_full = gathered_w[4].astype(jnp.float32)
    layer_weights = (
        gathered_w[0],
        gathered_w[1],
        gathered_w[2],
        gathered_w[3],
        gains_full[0],
        gains_full[1],
    )
    head_gain = gains_full[2]
    head_low = head_table.astype(jnp.bfloat16)
    incoming = jnp.zeros((ROW, D), jnp.bfloat16)
    saved_in, saved_out, received = ([], [], [])
    for tick_index in range(MB + 1):
        slot = min(tick_index, MB - 1)
        layer_in = jnp.where(first, inputs_all[slot], incoming.astype(jnp.float32))
        layer_result, _ = layer_fwd(layer_in, layer_weights)
        final_state = norm_fwd(layer_result, head_gain)
        outgoing = jnp.where(first, layer_result, final_state).astype(jnp.bfloat16)
        saved_in.append(layer_in.astype(jnp.bfloat16))
        saved_out.append(layer_result)
        incoming = from_partner(outgoing, "section", 0)
        received.append(incoming)
    lengths_here = lax.dynamic_index_in_dim(
        seq_lengths.reshape(replicas_n, groups, MB), lax.axis_index("dp"), 0, keepdims=False
    )
    group_next = group_all.reshape(groups, 2, MB, ROW)[:, 1]
    positions = jnp.arange(ROW, dtype=jnp.int32)
    loss_acc = jnp.zeros((), jnp.float32)
    grad_head = jnp.zeros(head_table.shape, jnp.float32)
    head_gain_grad = jnp.zeros((D,), jnp.float32)
    back_send, next_grads, main_grads = ([], [], [])
    for slot in range(MB):
        state = jnp.where(first, received[slot + 1].astype(jnp.float32), saved_out[slot + 1])
        merged_in = state + next_embed[slot] * first_f
        head_in = norm_fwd(merged_in, head_gain)
        targets_main = group_next[:, slot]
        shifted = jnp.concatenate([targets_main[:, 1:], targets_main[:, :1]], axis=1)
        targets = jnp.where(first, shifted, targets_main)
        limit = lengths_here[:, slot] - first.astype(jnp.int32)
        weights_tok = (positions[None, :] < limit[:, None]).astype(jnp.float32) * jnp.where(
            first, MTP_WEIGHT, 1.0
        )
        loss_part, grad_part, grad_in = head_pass(
            head_in.astype(jnp.bfloat16),
            targets.reshape(-1),
            weights_tok.reshape(-1),
            head_low,
            vocab_start,
            token_total,
        )
        loss_acc = loss_acc + loss_part
        grad_head = grad_head + grad_part
        merged_grad, gain_grad = norm_back(merged_in, head_gain, grad_in)
        head_gain_grad = head_gain_grad + gain_grad * first_f
        back_send.append(merged_grad.astype(jnp.bfloat16))
        next_grads.append(merged_grad)
        main_grads.append(grad_in)
    send_prev = jnp.zeros((ROW, D), jnp.bfloat16)
    layer_acc = None
    attn_gain_acc = jnp.zeros((D,), jnp.float32)
    ffn_gain_acc = jnp.zeros((D,), jnp.float32)
    input_grads = [None] * MB
    for tick_index in range(MB + 1):
        later = min(tick_index, MB - 1)
        earlier = max(tick_index - 1, 0)
        payload = jnp.where(first, back_send[later], send_prev)
        arrived = from_partner(payload, "section", 0).astype(jnp.float32)
        layer_in = jnp.where(first, saved_in[earlier], saved_in[later + 1]).astype(jnp.float32)
        layer_result, saved = layer_fwd(layer_in, layer_weights)
        top_grad, top_gain = norm_back(layer_result, head_gain, main_grads[later] + arrived)
        upstream = jnp.where(first, arrived, top_grad)
        valid = jnp.where(first, 1.0 if tick_index >= 1 else 0.0, 1.0 if tick_index < MB else 0.0)
        grad_inputs, grads, gain_parts = layer_back(layer_in, layer_weights, saved, upstream)
        if layer_acc is None:
            layer_acc = [item * valid for item in grads]
        else:
            layer_acc = [total + item * valid for total, item in zip(layer_acc, grads)]
        attn_gain_acc = attn_gain_acc + gain_parts[0] * valid
        ffn_gain_acc = ffn_gain_acc + gain_parts[1] * valid
        head_gain_grad = head_gain_grad + top_gain * valid * (1.0 - first_f)
        send_prev = grad_inputs.astype(jnp.bfloat16)
        if tick_index >= 1:
            input_grads[tick_index - 1] = grad_inputs
    token_grads = (
        jnp.concatenate([jnp.stack(input_grads), jnp.stack(next_grads)]).reshape(-1, D) * first_f
    )
    local = group_all - vocab_start
    inside = (local >= 0) & (local < vocab_rows)
    target_slot = jnp.where(inside, local, vocab_rows)
    grad_table = jax.ops.segment_sum(
        lax.all_gather(token_grads, "fsdp", axis=0, tiled=True),
        target_slot,
        num_segments=vocab_rows + 1,
    )[:vocab_rows]
    gains_grad = jnp.stack([attn_gain_acc, ffn_gain_acc, head_gain_grad])
    shards = (
        lax.psum_scatter(layer_acc[0], "fsdp", scatter_dimension=0, tiled=True),
        lax.psum_scatter(layer_acc[1], "fsdp", scatter_dimension=0, tiled=True),
        lax.psum_scatter(layer_acc[2], "fsdp", scatter_dimension=0, tiled=True),
        lax.psum_scatter(layer_acc[3], "fsdp", scatter_dimension=0, tiled=True),
        lax.psum_scatter(gains_grad, "fsdp", scatter_dimension=1, tiled=True),
    )
    shards = lax.psum((shards[0], shards[1], shards[2], shards[3], shards[4]), "dp")
    grad_table, grad_head, loss_total = lax.psum(
        (grad_table, grad_head, loss_acc), ("section", "dp")
    )
    squares = jnp.zeros((), jnp.float32)
    for item in shards:
        squares = squares + jnp.sum(item * item)
    squares = squares + first_f * (
        jnp.sum(grad_table * grad_table) + jnp.sum(grad_head * grad_head)
    )
    grad_norm = jnp.sqrt(lax.psum(squares, ("section", "fsdp")))
    clip_scale = CLIP / jnp.maximum(grad_norm, CLIP)
    params = (embedding, head_table, w_qkv[0], w_out[0], w_gateup[0], w_down[0], gains[0])
    grads_all = (grad_table, grad_head, shards[0], shards[1], shards[2], shards[3], shards[4])
    moments = (
        (embedding_mom, embedding_sec),
        (head_mom, head_sec),
        (qkv_mom[0], qkv_sec[0]),
        (out_mom[0], out_sec[0]),
        (gateup_mom[0], gateup_sec[0]),
        (down_mom[0], down_sec[0]),
        (gains_mom[0], gains_sec[0]),
    )
    rates = (0.6, 0.03, 0.03, 0.12, 0.03, 0.03, 0.6)
    decays = (0.1, 0.1, 0.1, 0.1, 0.1, 0.1, 0.0)
    outputs = [loss_total, token_total, grad_norm]
    for index in range(7):
        weight_new, mom_new, sec_new = adam_update(
            params[index],
            grads_all[index] * clip_scale,
            moments[index][0],
            moments[index][1],
            rates[index],
            decays[index],
        )
        if index >= 2:
            weight_new, mom_new, sec_new = (weight_new[None], mom_new[None], sec_new[None])
        outputs.extend([weight_new, mom_new, sec_new])
        if index < 6:
            outputs.append(weight_new.astype(jnp.bfloat16))
    return tuple(outputs)


def solution(mesh):
    placed = (
        P(("dp", "fsdp"), None),
        P(("dp", "fsdp"), None),
        P(),
        P("fsdp", None),
        P("fsdp", None),
        P("fsdp", None),
        P(None, "fsdp"),
        P(None, "fsdp"),
        P(None, "fsdp"),
        P("section", "fsdp", None),
        P("section", "fsdp", None),
        P("section", "fsdp", None),
        P("section", "fsdp", None),
        P("section", "fsdp", None),
        P("section", "fsdp", None),
        P("section", "fsdp", None),
        P("section", "fsdp", None),
        P("section", "fsdp", None),
        P("section", "fsdp", None),
        P("section", "fsdp", None),
        P("section", "fsdp", None),
        P("section", None, "fsdp"),
        P("section", None, "fsdp"),
        P("section", None, "fsdp"),
    )
    return jax.shard_map(
        per_device,
        mesh=mesh,
        in_specs=placed,
        out_specs=(
            P(),
            P(),
            P(),
            P("fsdp", None),
            P("fsdp", None),
            P("fsdp", None),
            P("fsdp", None),
            P(None, "fsdp"),
            P(None, "fsdp"),
            P(None, "fsdp"),
            P(None, "fsdp"),
            P("section", "fsdp", None),
            P("section", "fsdp", None),
            P("section", "fsdp", None),
            P("section", "fsdp", None),
            P("section", "fsdp", None),
            P("section", "fsdp", None),
            P("section", "fsdp", None),
            P("section", "fsdp", None),
            P("section", "fsdp", None),
            P("section", "fsdp", None),
            P("section", "fsdp", None),
            P("section", "fsdp", None),
            P("section", "fsdp", None),
            P("section", "fsdp", None),
            P("section", "fsdp", None),
            P("section", "fsdp", None),
            P("section", None, "fsdp"),
            P("section", None, "fsdp"),
            P("section", None, "fsdp"),
        ),
        check_vma=False,
    )
```

profile of v0, /device:TPU:0, one launch (start us, length us, event | category | flops | bytes accessed | tf_op | source)
XLA Modules:
  0.0 2566.3 jit_solution(1695704149145596049)
XLA Ops:
  42.1 14.6 gather_fusion
  79.0 94.5 %all-gather.7 = bf16[4,192,3]{1,2,0:T(4,128)(2,1)S(1)} all-gather(bf16[1,192,3]{1,2,0:T(4,128)(2,1)S(1)} %bitcast.575), channel_id=1, replica_groups=mesh['section'=2,'dp'=4,'fsdp'=4] {'fsdp'}, dimensions={0}, use_global_device_ids=true | all-gather | bytes 5760 | tf_op jit(solution)/shard_map/all_gather | solution.py:301
  192.2 137.6 %all-gather.24.cloned.1.call-done = bf16[768,6144]{1,0:T(8,128)(2,1)} async-done(((bf16[192,6144]{1,0:T(8,128)(2,1)}), bf16[768,6144]{1,0:T(8,128)(2,1)}) %all-gather.24.cloned.1.call-update) | async-done | bytes 9437200 | tf_op jit(solution)/shard_map/all_gather | solution.py:299
  336.6 82.8 %all-gather.26.cloned.1.call-done = bf16[3072,768]{1,0:T(8,128)(2,1)} async-done(((bf16[768,768]{1,0:T(8,128)(2,1)}), bf16[3072,768]{1,0:T(8,128)(2,1)}) %all-gather.26.cloned.1.call-update) | async-done | bytes 4718608 | tf_op jit(solution)/shard_map/all_gather | solution.py:300
  472.3 17.8 all_gather.55
  552.7 14.9 fusion.361
  603.4 18.1 all_gather.51
  672.5 14.9 fusion.360
  705.3 16.1 reduce-scatter.10.cloned.1.call-done
  834.8 20.6 multiply_add_fusion.4
  856.7 17.2 fusion.359
  875.3 25.7 convolution_add_fusion
  909.7 24.3 scatter_custom_fusion
  934.1 17.0 slice.517
  958.9 125.9 %reduce-scatter.14.cloned.1.call-done = f32[192,2304]{1,0:T(8,128)} async-done(((f32[768,2304]{1,0:T(8,128)}), f32[192,2304]{1,0:T(8,128)}) %reduce-scatter.14.cloned.1.call-update) | async-done | bytes 1769488 | tf_op jit(solution)/shard_map/reduce_scatter | solution.py:400
  1084.8 164.6 %reduce-scatter.20.cloned.1.call-done = f32[768,768]{1,0:T(8,128)} async-done(((f32[3072,768]{1,0:T(8,128)}), f32[768,768]{1,0:T(8,128)}) %reduce-scatter.20.cloned.1.call-update) | async-done | bytes 2359312 | tf_op jit(solution)/shard_map/reduce_scatter | solution.py:403
  1249.4 317.6 %reduce-scatter.18.cloned.1.call-done = f32[192,6144]{1,0:T(8,128)} async-done(((f32[768,6144]{1,0:T(8,128)}), f32[192,6144]{1,0:T(8,128)}) %reduce-scatter.18.cloned.1.call-update) | async-done | bytes 4718608 | tf_op jit(solution)/shard_map/reduce_scatter | solution.py:402
  1568.3 23.2 reduce-scatter.22.cloned.1.call-done
  1603.0 559.8 %all-reduce.11.cloned.1.call-done = (f32[8000,768]{1,0:T(8,128)}, f32[768,8000]{0,1:T(8,128)}) async-done(((f32[8000,768]{1,0:T(8,128)}, f32[768,8000]{0,1:T(8,128)}), (f32[8000,768]{1,0:T(8,128)}, f32[768,8000]{0,1:T(8,128)})) %all-reduce.11.cloned.1.call-update) | async-done | bytes 49152016 | tf_op jit(solution)/shard_map/psum | solution.py:407
  2187.2 169.7 %all-reduce.13.cloned.1.call-done = (f32[192,2304]{1,0:T(8,128)}, f32[192,768]{1,0:T(8,128)}, f32[192,6144]{1,0:T(8,128)}, f32[768,768]{1,0:T(8,128)}) async-done(((f32[192,2304]{1,0:T(8,128)}, f32[192,768]{1,0:T(8,128)}, f32[192,6144]{1,0:T(8,128)}, f32[768,768]{1,0:T(8,128)}), (f32[192,2304]{1,0:T(8,128)}, f32[192,768]{1,0:T(8,128)}, f32[192,6144]{1,0:T(8,128)}, ...) | async-done | bytes 9437200 | tf_op jit(solution)/shard_map/psum | solution.py:406
  2370.1 14.8 psum.63
  2384.9 17.9 psum.71
  2405.3 61.8 %fusion.364 = (bf16[8000,768]{1,0:T(8,128)(2,1)}, f32[8000,768]{1,0:T(8,128)}, f32[8000,768]{1,0:T(8,128)}, f32[8000,768]{1,0:T(8,128)}) fusion(f32[8000,768]{1,0:T(8,128)} %param.31, f32[8000,768]{1,0:T(8,128)} %get-tuple-element.327, f32[]{:T(128)S(6)} %div.573, f32[8000,768]{1,0:T(8,128)} %param.32, f32[8000,768]{1,0:T(8,128)} %param.33), kind=kLoop, calls=%fused_computation.639 | loop fusion | flops 104448000 | bytes 184320000 | tf_op jit(solution)/shard_map/convert_element_type | solution.py:445
  2467.1 61.8 %fusion.362 = (bf16[768,8000]{0,1:T(8,128)(2,1)}, f32[768,8000]{0,1:T(8,128)}, f32[768,8000]{0,1:T(8,128)}, f32[768,8000]{0,1:T(8,128)}) fusion(f32[768,8000]{0,1:T(8,128)} %param.34, f32[768,8000]{0,1:T(8,128)} %get-tuple-element.328, f32[]{:T(128)S(6)} %div.573, f32[768,8000]{0,1:T(8,128)} %param.35, f32[768,8000]{0,1:T(8,128)} %param.36), kind=kLoop, calls=%fused_computation.638 | loop fusion | flops 104448000 | bytes 184320000 | tf_op jit(solution)/shard_map/convert_element_type | solution.py:445
  (869 shorter events, 513.9 us)
Async XLA Ops:
  7.2 172.3 %all-gather.20.cloned.1.call-start = ((), (), s32[]{:S(2)}) async-start(), calls=%async_computation.8 | async-start | bytes 4423680 | tf_op jit(solution)/shard_map/all_gather | solution.py:297
  9.8 180.5 %all-gather.22.cloned.1.call-start = ((), (), s32[]{:S(2)}) async-start(), calls=%async_computation.9 | async-start | bytes 1474560 | tf_op jit(solution)/shard_map/all_gather | solution.py:298
  10.7 319.1 %all-gather.24.cloned.1.call-start = ((), (), s32[]{:S(2)}) async-start(), calls=%async_computation.10 | async-start | bytes 11796480 | tf_op jit(solution)/shard_map/all_gather | solution.py:299
  58.8 118.5 %all-to-all-start = ((bf16[4,512,768]{2,1,0:T(8,128)(2,1)}), bf16[4,512,768]{2,1,0:T(8,128)(2,1)S(1)}, u32[]{:S(2)}, u32[]{:S(2)}) async-start(bf16[4,512,768]{2,1,0:T(8,128)(2,1)} %select_select_fusion), calls=%async_computation | async-start | bytes 6291456 | tf_op jit(solution)/shard_map/all_to_all | solution.py:292
  62.6 356.8 %all-gather.26.cloned.1.call-start = ((), (), s32[]{:S(2)}) async-start(), calls=%async_computation.11 | async-start | bytes 5898240 | tf_op jit(solution)/shard_map/all_gather | solution.py:300
  65.4 536.3 %reduce-scatter.12.cloned.1.call-start = ((), (), s32[]{:S(2)}) async-start(), calls=%async_computation.13 | async-start | bytes 1966080 | tf_op jit(solution)/shard_map/reduce_scatter | solution.py:237
  175.8 336.2 %copy-start.170 = (s32[512]{0:T(512)}, s32[512]{0:T(512)S(1)}, u32[]{:S(2)}) copy-start(s32[512]{0:T(512)S(1)} %fusion.250) | copy-start | bytes 6148
  424.0 1.5 collective-permute-start
  444.4 1.8 collective-permute-start.1
  467.5 1.5 collective-permute-start.2
  567.6 153.7 %reduce-scatter.10.cloned.1.call-start = ((), (), s32[]{:S(2)}) async-start(), calls=%async_computation.12 | async-start | bytes 1966080 | tf_op jit(solution)/shard_map/reduce_scatter | solution.py:237
  573.0 168.6 %copy-start.206 = (f32[12,128]{1,0:T(8,128)}, f32[12,128]{1,0:T(8,128)S(1)}, u32[]{:S(2)}) copy-start(f32[12,128]{1,0:T(8,128)S(1)} %get-tuple-element.497) | copy-start | bytes 18436
  575.0 163.3 %copy-start.11 = (f32[128,768]{1,0:T(8,128)}, f32[128,768]{1,0:T(8,128)S(1)}, u32[]{:S(2)}) copy-start(f32[128,768]{1,0:T(8,128)S(1)} %get-tuple-element.500) | copy-start | bytes 1179652
  687.4 222.3 %all-gather.28.cloned.1.call-start = ((), (), s32[]{:S(2)}) async-start(), calls=%async_computation.18 | async-start | bytes 7864320 | tf_op jit(solution)/shard_map/all_gather | solution.py:394
  724.4 1.5 collective-permute-start.3
  748.2 1.4 collective-permute-start.4
  770.9 1.5 collective-permute-start.5
  795.3 163.6 %reduce-scatter.16.cloned.1.call-start = ((), (), s32[]{:S(2)}) async-start(), calls=%async_computation.15 | async-start | bytes 2949120 | tf_op jit(solution)/shard_map/reduce_scatter | solution.py:401
  798.3 286.5 %reduce-scatter.14.cloned.1.call-start = ((), (), s32[]{:S(2)}) async-start(), calls=%async_computation.14 | async-start | bytes 8847360 | tf_op jit(solution)/shard_map/reduce_scatter | solution.py:400
  805.5 443.9 %reduce-scatter.20.cloned.1.call-start = ((), (), s32[]{:S(2)}) async-start(), calls=%async_computation.17 | async-start | bytes 11796480 | tf_op jit(solution)/shard_map/reduce_scatter | solution.py:403
  815.0 752.0 %reduce-scatter.18.cloned.1.call-start = ((), (), s32[]{:S(2)}) async-start(), calls=%async_computation.16 | async-start | bytes 23592960 | tf_op jit(solution)/shard_map/reduce_scatter | solution.py:402
  855.5 736.0 %reduce-scatter.22.cloned.1.call-start = ((), (), s32[]{:S(2)}) async-start(), calls=%async_computation.19 | async-start | bytes 491520
  875.0 1287.7 %all-reduce.11.cloned.1.call-start = ((), (), s32[]{:S(2)}) async-start(), calls=%async_computation.20 | async-start | bytes 98304000 | tf_op jit(solution)/shard_map/psum | solution.py:407
  951.1 1405.9 %all-reduce.13.cloned.1.call-start = ((), (), s32[]{:S(2)}) async-start(), calls=%async_computation.21 | async-start | bytes 18874368 | tf_op jit(solution)/shard_map/psum | solution.py:406
  (265 other events, 2015.9 us)
Sparse Core Ops, SparseCore 0:
  10.2 99.1 all-gather.19
  111.5 51.0 all-gather.21
  164.8 164.9 all-gather.23
  331.7 87.5 all-gather.25
  567.8 33.8 reduce-scatter.11
  687.5 33.8 reduce-scatter.9
  795.4 114.2 all-gather.27
  912.6 46.2 reduce-scatter.15
  961.8 122.9 reduce-scatter.13
  1087.6 161.7 reduce-scatter.19
  1252.4 314.5 reduce-scatter.17
  1569.8 21.6 reduce-scatter.21
  1596.1 566.6 all-reduce.10
  2166.5 190.3 all-reduce.12
where the time goes:
time: 2570 us
  waiting for transfers between devices  1630 us (63%)
  other arithmetic  294 us (11%)
  matrix products  281 us (11%)
  blocking collectives  258 us (10%)
  local copies, waits for them, and re-layouts  73.2 us (3%)
  between operations  27.7 us (1%)
    psum x1, waiting for transfers between devices, per_device(): lax.psum((grad_table, grad_head, loss_acc), ('section', 'dp'))  560 us
    reduce_scatter x1, waiting for transfers between devices, per_device(): lax.psum_scatter(layer_acc[2], 'fsdp', scatter_dimension=0, tiled=True)  318 us
    psum x1, waiting for transfers between devices, per_device(): lax.psum((shards[0], shards[1], shards[2], shards[3], shards[4]), 'dp')  170 us
    reduce_scatter x1, waiting for transfers between devices, per_device(): lax.psum_scatter(layer_acc[3], 'fsdp', scatter_dimension=0, tiled=True)  165 us
    convert_element_type x6, other arithmetic, per_device(): outputs.append(weight_new.astype(jnp.bfloat16))  152 us
    all_gather x1, waiting for transfers between devices, per_device(): lax.all_gather(w_gateup[0].astype(jnp.bfloat16), 'fsdp', axis=0, tiled=True)  138 us
    reduce_scatter x1, waiting for transfers between devices, per_device(): lax.psum_scatter(layer_acc[0], 'fsdp', scatter_dimension=0, tiled=True)  126 us
    dot_general x14, matrix products, contract_rows(): lax.dot_general(left, right, (((0,), (0,)), ((), ())), preferred_element_...  99.5 us
  transfers between devices with their start and end apart: 21, of which 17 were waited for; matrix products, arithmetic and copies ran while one was open for 11% of the time, Pallas kernels for 0%

commit v1 on v0

v1 whole, which is shorter than its diff:
```python
import functools
import math

import jax
import jax.numpy as jnp
from jax import lax
from jax.experimental import pallas as pl
from jax.experimental.pallas import tpu as pltpu
from jax.sharding import PartitionSpec as P

D = 768
HEADS = 12
HEAD_DIM = 64
FF = 3072
ROW = 128
MB = 2
STEP_COUNT = 10
SHARE = 4


EPS = 1e-05
MTP_WEIGHT = 0.3
CLIP = 0.01
BETA1 = 0.9
BETA2 = 0.95
ADAM_EPS = 1e-08
LOW = jnp.bfloat16
WIDE = jnp.float32

MESH = pl.DeviceIdType.MESH

def weights_kernel(planes, replicas, units, rows, *refs):
    n = len(rows)
    own, full = refs[:n], refs[n:2*n]
    send, recv, local = refs[2*n:]
    z = lax.axis_index("fsdp")
    i = lax.axis_index("dp")
    half = replicas // 2
    low, top = i % 2, i // half
    q = top * 2 + low
    xn = i + 1 - 2 * low
    yn = (i + half) % replicas
    qx = top * 2 + 1 - low
    qy = (1 - top) * 2 + low
    barrier = pltpu.get_barrier_semaphore()
    for step in range(1, planes):
        pl.semaphore_signal(barrier, inc=1, device_id={"fsdp": (z + step) % planes}, device_id_type=MESH)
    pl.semaphore_signal(barrier, inc=1, device_id={"dp": xn}, device_id_type=MESH)
    pl.semaphore_signal(barrier, inc=1, device_id={"dp": yn}, device_id_type=MESH)
    pl.semaphore_wait(barrier, planes + 1)
    keep = []
    for m in range(n):
        c = pltpu.make_async_copy(own[m], full[m].at[pl.ds(pl.multiple_of(z * rows[m], 16), rows[m]), :], local.at[m])
        c.start()
        keep.append(c)
    per = 3 * (planes - 1) + (planes - 1)
    def cp(src, dst, k, dev):
        return pltpu.make_async_remote_copy(src_ref=src, dst_ref=dst, send_sem=send.at[k], recv_sem=recv.at[k], device_id=dev, device_id_type=MESH)
    def block(m, plane, quarter, cols):
        r = rows[m] // 4
        return full[m].at[pl.ds(pl.multiple_of(plane * rows[m] + quarter * r, 16), r), pl.ds(cols[0], cols[1])]
    first, second, third = [], [], []
    for u, (m, cols, order) in enumerate(units):
        r = rows[m] // 4
        group = []
        for step in range(1, planes):
            src = own[m].at[pl.ds(pl.multiple_of(q * r, 16), r), pl.ds(cols[0], cols[1])]
            c = cp(src, block(m, z, q, cols), u * per + step - 1, {"fsdp": (z + step) % planes})
            c.start()
            group.append(c)
        first.append(group)
    def phase2(u):
        m, cols, order = units[u]
        base = u * per + planes - 1
        group = []
        for step in range(1, planes):
            first[u][step - 1].wait_recv()
            b = block(m, (z + planes - step) % planes, q, cols)
            c = cp(b, b, base + step - 1, {"dp": xn if order == 0 else yn})
            c.start()
            group.append(c)
        second.append(group)
    def phase3(u):
        m, cols, order = units[u]
        base = u * per + 2 * (planes - 1)
        group = []
        for step in range(1, planes):
            second[u][step - 1].wait_recv()
            for w, quarter in enumerate((q, qx if order == 0 else qy)):
                b = block(m, (z + planes - step) % planes, quarter, cols)
                c = cp(b, b, base + 2 * (step - 1) + w, {"dp": yn if order == 0 else xn})
                c.start()
                group.append(c)
        third.append(group)
    total = len(units)
    for u in range(total):
        phase2(u)
        if u >= 1:
            phase3(u - 1)
    phase3(total - 1)
    for u in range(total):
        for c in third[u]:
            c.wait_recv()
    for u in range(total):
        for c in first[u] + second[u] + third[u]:
            c.wait_send()
    for c in keep:
        c.wait()

def gather_weights(planes, replicas, shards):
    rows = [w.shape[0] for w in shards]
    if any(r % (SHARE * 16) for r in rows):
        return [lax.all_gather(w, "fsdp", axis=0, tiled=True) for w in shards]
    units = []
    for m, w in enumerate(shards):
        width = w.shape[1]
        parts = 4 if width > 4096 else 2
        step = width // parts
        for p in range(parts):
            units.append((m, (p * step, step), p % 2))
    copies = len(units) * 4 * (planes - 1)
    return pl.pallas_call(
        functools.partial(weights_kernel, planes, replicas, units, rows),
        out_shape=[jax.ShapeDtypeStruct((planes * w.shape[0], w.shape[1]), w.dtype) for w in shards],
        in_specs=[pl.BlockSpec(memory_space=pl.ANY)] * len(shards),
        out_specs=[pl.BlockSpec(memory_space=pl.ANY)] * len(shards),
        scratch_shapes=[pltpu.SemaphoreType.DMA((copies,)), pltpu.SemaphoreType.DMA((copies,)), pltpu.SemaphoreType.DMA((len(shards),))],
        compiler_params=pltpu.CompilerParams(collective_id=1, has_side_effects=True),
        name="gather_weights",
    )(*shards)


def norm_fwd(values, scale_gain):
    inverse = lax.rsqrt(jnp.mean(values * values, axis=-1, keepdims=True) + EPS)
    return values * inverse * scale_gain


def norm_back(values, scale_gain, upstream):
    _, pullback = jax.vjp(norm_fwd, values, scale_gain)
    return pullback(upstream)


def rope_tables(row_count, head_width):
    half_width = head_width // 2
    position = jnp.arange(row_count, dtype=jnp.float32)[:, None]
    frequency = 10000.0 ** (-jnp.arange(half_width, dtype=jnp.float32) / half_width)
    angles = position * frequency[None, :]
    return (jnp.cos(angles), jnp.sin(angles))


def rotate(values, cosine, sine_table):
    half_width = values.shape[-1] // 2
    first, second = (values[..., :half_width], values[..., half_width:])
    return jnp.concatenate(
        [first * cosine - second * sine_table, second * cosine + first * sine_table], axis=-1
    )


def contract_rows(left, right):
    return lax.dot_general(
        left, right, (((0,), (0,)), ((), ())), preferred_element_type=jnp.float32
    )


def contract_cols(left, right):
    return lax.dot_general(
        left, right, (((1,), (1,)), ((), ())), preferred_element_type=jnp.float32
    )


def swiglu(gate_up):
    return jax.nn.silu(gate_up[:, :FF]) * gate_up[:, FF:]


def shift(block, axis, distance):
    count = lax.axis_size(axis)
    return lax.ppermute(block, axis, [(i, (i + distance) % count) for i in range(count)])


def swap(block, axis, mask):
    count = lax.axis_size(axis)
    return lax.ppermute(block, axis, [(i, i ^ mask) for i in range(count)])


def pick(array, index, axis=0):
    return lax.dynamic_index_in_dim(array, index, axis, keepdims=False)


def layer_fwd(inputs, weights):
    w_qkv, w_out, w_gateup, w_down, attn_gain, ffn_gain = weights
    normed = norm_fwd(inputs, attn_gain).astype(LOW)
    packed = jnp.dot(normed, w_qkv, preferred_element_type=WIDE)
    split = packed.reshape(MB, ROW, 3, HEADS, HEAD_DIM).transpose(2, 0, 3, 1, 4)
    split = split.reshape(3, MB * HEADS, ROW, HEAD_DIM)
    cosine, sine_table = rope_tables(ROW, HEAD_DIM)
    queries = rotate(split[0], cosine, sine_table).astype(LOW)
    keys_rot = rotate(split[1], cosine, sine_table).astype(LOW)
    values_low = split[2].astype(LOW)
    scores = jnp.einsum(
        "hqd,hkd->hqk", queries, keys_rot, preferred_element_type=WIDE
    ) * HEAD_DIM ** (-0.5)
    position = jnp.arange(ROW)
    causal = position[:, None] >= position[None, :]
    scores = jnp.where(causal[None], scores, -1e30)
    shifted = jnp.exp(scores - jnp.max(scores, axis=-1, keepdims=True))
    probs = shifted / jnp.sum(shifted, axis=-1, keepdims=True)
    probs_low = probs.astype(LOW)
    mixed = jnp.einsum("hqk,hkd->hqd", probs_low, values_low, preferred_element_type=WIDE)
    mixed = mixed.reshape(MB, HEADS, ROW, HEAD_DIM).transpose(0, 2, 1, 3)
    mixed_low = mixed.reshape(MB * ROW, D).astype(LOW)
    after_attn = inputs + jnp.dot(mixed_low, w_out, preferred_element_type=WIDE)
    normed_ffn = norm_fwd(after_attn, ffn_gain).astype(LOW)
    gate_up = jnp.dot(normed_ffn, w_gateup, preferred_element_type=WIDE)
    hidden = swiglu(gate_up).astype(LOW)
    output = after_attn + jnp.dot(hidden, w_down, preferred_element_type=WIDE)
    saved = (
        normed,
        queries,
        keys_rot,
        values_low,
        probs,
        probs_low,
        mixed_low,
        after_attn,
        normed_ffn,
        gate_up,
        hidden,
    )
    return (output, saved)


def layer_back(inputs, weights, saved, upstream):
    w_qkv, w_out, w_gateup, w_down, attn_gain, ffn_gain = weights
    (
        normed,
        queries,
        keys_rot,
        values_low,
        probs,
        probs_low,
        mixed_low,
        after_attn,
        normed_ffn,
        gate_up,
        hidden,
    ) = saved
    upstream_low = upstream.astype(LOW)
    grad_hidden = contract_cols(upstream_low, w_down)
    _, pullback = jax.vjp(swiglu, gate_up)
    grad_gu = pullback(grad_hidden)[0].astype(LOW)
    grad_nffn = contract_cols(grad_gu, w_gateup)
    back_ffn, grad_ffn_gain = norm_back(after_attn, ffn_gain, grad_nffn)
    grad_after = upstream + back_ffn
    after_low = grad_after.astype(LOW)
    grad_mixed = contract_cols(after_low, w_out).astype(LOW)
    grad_mixed = grad_mixed.reshape(MB, ROW, HEADS, HEAD_DIM).transpose(0, 2, 1, 3)
    grad_mixed = grad_mixed.reshape(MB * HEADS, ROW, HEAD_DIM)
    grad_probs = jnp.einsum("hqd,hkd->hqk", grad_mixed, values_low, preferred_element_type=WIDE)
    grad_values = jnp.einsum("hqk,hqd->hkd", probs_low, grad_mixed, preferred_element_type=WIDE)
    grad_scores = probs * (grad_probs - jnp.sum(probs * grad_probs, axis=-1, keepdims=True))
    grad_scores = grad_scores.astype(LOW)
    scale_attn = HEAD_DIM ** (-0.5)
    grad_query = (
        jnp.einsum("hqk,hkd->hqd", grad_scores, keys_rot, preferred_element_type=WIDE)
        * scale_attn
    )
    grad_key = (
        jnp.einsum("hqk,hqd->hkd", grad_scores, queries, preferred_element_type=WIDE)
        * scale_attn
    )
    cosine, sine_table = rope_tables(ROW, HEAD_DIM)
    grad_query = rotate(grad_query, cosine, -sine_table)
    grad_key = rotate(grad_key, cosine, -sine_table)
    grad_packed = jnp.stack([grad_query, grad_key, grad_values]).astype(LOW)
    grad_packed = grad_packed.reshape(3, MB, HEADS, ROW, HEAD_DIM).transpose(1, 3, 0, 2, 4)
    grad_packed = grad_packed.reshape(MB * ROW, 3 * D)
    grad_normed = contract_cols(grad_packed, w_qkv)
    back_attn, grad_attn_gain = norm_back(inputs, attn_gain, grad_normed)
    grad_inputs = grad_after + back_attn
    return (
        grad_inputs,
        (grad_packed, after_low, grad_gu, upstream_low),
        (grad_attn_gain, grad_ffn_gain),
    )


def plane_masks(replicas):
    return (0, 1, replicas // 2, 1 + replicas // 2)


def plane_rank(replicas):
    index = lax.axis_index("dp")
    return (index // (replicas // 2)) * 2 + index % 2


def everyone(block, replicas):
    return jnp.concatenate(
        [block] + [swap(block, "dp", mask) for mask in plane_masks(replicas)[1:]], axis=0
    )


def quarters(block, replicas):
    rank = plane_rank(replicas)
    width = block.shape[1] // SHARE
    pieces = []
    for offset, mask in enumerate(plane_masks(replicas)):
        piece = lax.dynamic_slice_in_dim(block, (rank ^ offset) * width, width, 1)
        pieces.append(swap(piece, "dp", mask) if mask else piece)
    return jnp.concatenate(pieces, axis=0)


def rows_to_owner(partial):
    planes = lax.axis_size("fsdp")
    me = lax.axis_index("fsdp")
    blocks = partial.reshape((planes, partial.shape[0] // planes) + partial.shape[1:])
    total = pick(blocks, me).astype(WIDE)
    for step in range(1, planes):
        total = total + shift(pick(blocks, (me + step) % planes), "fsdp", step).astype(WIDE)
    return total


def other_replicas(total, replicas):
    mask = 2
    while mask < replicas // 2:
        total = total + swap(total.astype(LOW), "dp", mask).astype(WIDE)
        mask *= 2
    return total


def columns_from_plane(piece, replicas):
    rank = plane_rank(replicas)
    height, width = piece.shape
    full = jnp.zeros((height, SHARE * width), piece.dtype)
    for offset, mask in enumerate(plane_masks(replicas)):
        block = swap(piece, "dp", mask) if mask else piece
        full = lax.dynamic_update_slice_in_dim(full, block, (rank ^ offset) * width, 1)
    return full


def bit_of(axis, mask):
    return (lax.axis_index(axis) // mask) % 2


def halve(block, axis, mask):
    bit = bit_of(axis, mask)
    pair = block.reshape((2, block.shape[0] // 2) + block.shape[1:])
    theirs = swap(pick(pair, 1 - bit), axis, mask)
    return (pick(pair, bit).astype(WIDE) + theirs.astype(WIDE)).astype(LOW)


def double(block, axis, mask):
    theirs = swap(block, axis, mask)
    bit = bit_of(axis, mask)
    return jnp.where(
        bit == 0,
        jnp.concatenate([block, theirs], axis=0),
        jnp.concatenate([theirs, block], axis=0),
    )


def mask_orders(replicas):
    masks = [1 << k for k in range(replicas.bit_length() - 1)]
    return (masks, masks[::-1])


def reduce_shared(block, replicas):
    mine = halve(block, "section", 1)
    pieces = []
    for part, order in zip(jnp.split(mine, 2, axis=0), mask_orders(replicas)):
        for mask in order:
            part = halve(part, "dp", mask)
        pieces.append(part)
    return pieces


def gather_shared(pieces, replicas):
    parts = []
    for part, order in zip(pieces, mask_orders(replicas)):
        for mask in order[::-1]:
            part = double(part, "dp", mask)
        parts.append(part)
    return double(jnp.concatenate(parts, axis=0), "section", 1)


def head_pass(rows_low, targets, weights_tok, head_low, vocab_start, token_total):
    planes = lax.axis_size("fsdp")
    gathered = jnp.concatenate(
        [rows_low] + [shift(rows_low, "fsdp", step) for step in range(1, planes)], axis=0
    )
    local_vocab = head_low.shape[1]
    columns = jnp.arange(local_vocab, dtype=jnp.int32)
    local_targets = targets - vocab_start
    hit = columns[None, :] == local_targets[:, None]
    logits = jnp.dot(gathered, head_low, preferred_element_type=WIDE)
    highest = jnp.max(logits, axis=-1)
    summed = jnp.sum(jnp.exp(logits - highest[:, None]), axis=-1)
    picked = jnp.sum(jnp.where(hit, logits, 0.0), axis=-1)
    stats = jnp.stack([highest, summed, picked]).reshape(3, planes, -1)
    parts = [stats] + [
        jnp.roll(shift(stats, "fsdp", step), step, axis=1) for step in range(1, planes)
    ]
    parts = jnp.stack(parts)
    peak = jnp.max(parts[:, 0], axis=0)
    total = jnp.sum(parts[:, 1] * jnp.exp(parts[:, 0] - peak[None]), axis=0)
    lse = (peak + jnp.log(total)).reshape(-1)
    loss_part = jnp.sum((lse - jnp.sum(parts[:, 2], axis=0).reshape(-1)) * weights_tok)
    factor = weights_tok / token_total
    onehot = hit.astype(WIDE)
    grads_low = ((jnp.exp(logits - lse[:, None]) - onehot) * factor[:, None]).astype(LOW)
    grad_head = contract_rows(gathered, grads_low).astype(LOW)
    partial = contract_cols(grads_low, head_low).reshape(planes, -1, D)
    grad_rows = partial[0]
    for step in range(1, planes):
        grad_rows = grad_rows + shift(partial[step].astype(LOW), "fsdp", planes - step).astype(WIDE)
    return (loss_part, grad_head, grad_rows)


def adam_update(weight, grad, first_mom, second_mom, rate, decay):
    mom_new = BETA1 * first_mom + (1.0 - BETA1) * grad
    sec_new = BETA2 * second_mom + (1.0 - BETA2) * grad * grad
    mom_hat = mom_new / (1.0 - BETA1**STEP_COUNT)
    sec_hat = sec_new / (1.0 - BETA2**STEP_COUNT)
    weight_new = weight - rate * (mom_hat / (jnp.sqrt(sec_hat) + ADAM_EPS) + decay * weight)
    return (weight_new, mom_new, sec_new)


def per_device(
    token_ids,
    next_ids,
    seq_lengths,
    embedding,
    embedding_mom,
    embedding_sec,
    head_table,
    head_mom,
    head_sec,
    w_qkv,
    qkv_mom,
    qkv_sec,
    w_out,
    out_mom,
    out_sec,
    w_gateup,
    gateup_mom,
    gateup_sec,
    w_down,
    down_mom,
    down_sec,
    gains,
    gains_mom,
    gains_sec,
):
    planes = lax.axis_size("fsdp")
    replicas = lax.axis_size("dp")
    first = lax.axis_index("section") == 0
    first_f = first.astype(WIDE)
    me = lax.axis_index("fsdp")
    token_total = jnp.sum(seq_lengths).astype(WIDE)
    tokens = MB * ROW

    my_ids = jnp.stack([token_ids.reshape(-1), next_ids.reshape(-1)])
    rel_ids = jnp.stack([my_ids] + [shift(my_ids, "fsdp", step) for step in range(1, planes)])
    my_kind = jnp.where(first, rel_ids[:, 0], rel_ids[:, 1])
    vocab_rows = embedding.shape[0]
    vocab_start = me * vocab_rows
    local = my_kind - vocab_start
    inside = (local >= 0) & (local < vocab_rows)
    found = jnp.take(embedding, jnp.clip(local, 0, vocab_rows - 1), axis=0)
    found = jnp.where(inside[..., None], found, 0.0).astype(LOW)
    looked = found[0].astype(WIDE)
    for step in range(1, planes):
        looked = looked + shift(found[step], "fsdp", planes - step).astype(WIDE)
    next_embed = swap(looked.astype(LOW), "section", 1).astype(WIDE)

    full = gather_weights(
        planes,
        replicas,
        [w_qkv[0].astype(LOW), w_out[0].astype(LOW), w_gateup[0].astype(LOW), w_down[0].astype(LOW)],
    )
    gains_full = lax.all_gather(gains[0].astype(LOW), "fsdp", axis=1, tiled=True).astype(WIDE)
    layer_weights = (full[0], full[1], full[2], full[3], gains_full[0], gains_full[1])
    head_gain = gains_full[2]
    head_low = head_table.astype(LOW)

    first_out, _ = layer_fwd(looked, layer_weights)
    middle = swap(first_out.astype(LOW), "section", 1).astype(WIDE)
    layer_in = jnp.where(first, looked, middle)
    layer_out, saved = layer_fwd(layer_in, layer_weights)
    final_state = norm_fwd(layer_out, head_gain)
    arrived = swap(final_state.astype(LOW), "section", 1).astype(WIDE)
    merged_in = jnp.where(first, arrived + next_embed, layer_out)
    head_in = norm_fwd(merged_in, head_gain)

    lengths = seq_lengths.reshape(replicas, planes, MB)[lax.axis_index("dp")]
    rel_planes = (me - jnp.arange(planes)) % planes
    lengths = jnp.take(lengths, rel_planes, axis=0)
    targets_main = rel_ids[:, 1].reshape(planes, MB, ROW)
    shifted = jnp.concatenate([targets_main[..., 1:], targets_main[..., :1]], axis=-1)
    targets = jnp.where(first, shifted, targets_main)
    limit = lengths - first.astype(jnp.int32)
    positions = jnp.arange(ROW, dtype=jnp.int32)
    weights_tok = (positions < limit[..., None]).astype(WIDE) * jnp.where(first, MTP_WEIGHT, 1.0)
    loss_part, grad_head, grad_in = head_pass(
        head_in.astype(LOW),
        targets.reshape(-1),
        weights_tok.reshape(-1),
        head_low,
        vocab_start,
        token_total,
    )
    head_pieces = reduce_shared(grad_head, replicas)

    merged_grad, mtp_gain = norm_back(merged_in, head_gain, grad_in)
    merged_low = merged_grad.astype(LOW)
    sent = swap(merged_low, "section", 1).astype(WIDE)
    top_grad, top_gain = norm_back(layer_out, head_gain, grad_in + sent)
    head_gain_grad = jnp.where(first, mtp_gain, top_gain)
    below, _, _ = layer_back(layer_in, layer_weights, saved, top_grad)
    upstream = jnp.where(first, swap(below.astype(LOW), "section", 1).astype(WIDE), top_grad)
    grad_inputs, right, gain_parts = layer_back(layer_in, layer_weights, saved, upstream)

    left = (saved[0], saved[6], saved[8], saved[10])
    shards = []
    for a_side, b_side in zip(left, right):
        a_all = everyone(a_side, replicas)
        b_all = quarters(b_side, replicas)
        part = contract_rows(a_all, b_all).astype(LOW)
        shards.append(other_replicas(rows_to_owner(part), replicas).astype(LOW))
    gains_grad = jnp.stack([gain_parts[0], gain_parts[1], head_gain_grad])
    gains_grad = lax.psum(
        lax.psum_scatter(gains_grad, "fsdp", scatter_dimension=1, tiled=True), "dp"
    )

    row_grads = jnp.where(first, grad_inputs.astype(LOW), sent.astype(LOW))
    rel_grads = jnp.stack([row_grads] + [shift(row_grads, "fsdp", step) for step in range(1, planes)])
    slot = jnp.where(inside, local, vocab_rows)
    grad_table = jnp.zeros((vocab_rows, D), WIDE)
    grad_table = grad_table.at[slot.reshape(-1)].add(
        rel_grads.reshape(-1, D).astype(WIDE), mode="drop"
    )
    table_pieces = reduce_shared(grad_table.astype(LOW), replicas)

    def square(item):
        wide = item.astype(WIDE)
        return jnp.sum(wide * wide)

    squares = jnp.zeros((), WIDE)
    for item in shards:
        squares = squares + square(item) * (SHARE / replicas)
    for item in head_pieces + table_pieces:
        squares = squares + square(item)
    squares = squares + square(gains_grad) / replicas
    totals = lax.psum(jnp.stack([squares, loss_part / planes]), ("section", "dp", "fsdp"))
    grad_norm = jnp.sqrt(totals[0])
    loss_total = totals[1]
    clip_scale = CLIP / jnp.maximum(grad_norm, CLIP)

    grad_table = gather_shared(table_pieces, replicas).astype(WIDE)
    grad_head = gather_shared(head_pieces, replicas).astype(WIDE)
    layer_grads = [columns_from_plane(item, replicas).astype(WIDE) for item in shards]
    params = (embedding, head_table, w_qkv[0], w_out[0], w_gateup[0], w_down[0], gains[0])
    grads_all = (grad_table, grad_head, *layer_grads, gains_grad)
    moments = (
        (embedding_mom, embedding_sec),
        (head_mom, head_sec),
        (qkv_mom[0], qkv_sec[0]),
        (out_mom[0], out_sec[0]),
        (gateup_mom[0], gateup_sec[0]),
        (down_mom[0], down_sec[0]),
        (gains_mom[0], gains_sec[0]),
    )
    rates = (0.6, 0.03, 0.03, 0.12, 0.03, 0.03, 0.6)
    decays = (0.1, 0.1, 0.1, 0.1, 0.1, 0.1, 0.0)
    outputs = [loss_total, token_total, grad_norm]
    for index in range(7):
        weight_new, mom_new, sec_new = adam_update(
            params[index],
            grads_all[index] * clip_scale,
            moments[index][0],
            moments[index][1],
            rates[index],
            decays[index],
        )
        if index >= 2:
            weight_new, mom_new, sec_new = (weight_new[None], mom_new[None], sec_new[None])
        outputs.extend([weight_new, mom_new, sec_new])
        if index < 6:
            outputs.append(weight_new.astype(LOW))
    return tuple(outputs)


def solution(mesh):
    placed = (
        P(("dp", "fsdp"), None),
        P(("dp", "fsdp"), None),
        P(),
        P("fsdp", None),
        P("fsdp", None),
        P("fsdp", None),
        P(None, "fsdp"),
        P(None, "fsdp"),
        P(None, "fsdp"),
        P("section", "fsdp", None),
        P("section", "fsdp", None),
        P("section", "fsdp", None),
        P("section", "fsdp", None),
        P("section", "fsdp", None),
        P("section", "fsdp", None),
        P("section", "fsdp", None),
        P("section", "fsdp", None),
        P("section", "fsdp", None),
        P("section", "fsdp", None),
        P("section", "fsdp", None),
        P("section", "fsdp", None),
        P("section", None, "fsdp"),
        P("section", None, "fsdp"),
        P("section", None, "fsdp"),
    )
    return jax.shard_map(
        per_device,
        mesh=mesh,
        in_specs=placed,
        out_specs=(
            P(),
            P(),
            P(),
            P("fsdp", None),
            P("fsdp", None),
            P("fsdp", None),
            P("fsdp", None),
            P(None, "fsdp"),
            P(None, "fsdp"),
            P(None, "fsdp"),
            P(None, "fsdp"),
            P("section", "fsdp", None),
            P("section", "fsdp", None),
            P("section", "fsdp", None),
            P("section", "fsdp", None),
            P("section", "fsdp", None),
            P("section", "fsdp", None),
            P("section", "fsdp", None),
            P("section", "fsdp", None),
            P("section", "fsdp", None),
            P("section", "fsdp", None),
            P("section", "fsdp", None),
            P("section", "fsdp", None),
            P("section", "fsdp", None),
            P("section", "fsdp", None),
            P("section", "fsdp", None),
            P("section", "fsdp", None),
            P("section", None, "fsdp"),
            P("section", None, "fsdp"),
            P("section", None, "fsdp"),
        ),
        check_vma=False,
    )
```

time: 2570 us -> 1490 us (0.58)
  waiting for transfers between devices: 1630 us -> 331 us
  Pallas kernels: 0 us -> 193 us
  blocking collectives: 258 us -> 72.3 us
  local copies, waits for them, and re-layouts: 73.2 us -> 223 us
  starting transfers between devices: 6.2 us -> 141 us
  matrix products: 281 us -> 163 us
  other arithmetic: 294 us -> 331 us
    psum x2 -> x0, waiting for transfers between devices: 730 us -> none  [the longest x1 560 us: per_device(): lax.psum((grad_table, grad_head, loss_acc), ('section', 'dp'))]
    reduce_scatter x6 -> x0, waiting for transfers between devices: 638 us -> none  [the longest x1 318 us: per_device(): lax.psum_scatter(layer_acc[2], 'fsdp', scatter_dimension=0, tiled=True)]
    ppermute x6 -> x91, waiting for transfers between devices: 4.94 us -> 331 us  [the longest x61 205 us: swap(): return lax.ppermute(block, axis, [(i, i ^ mask) for i in range(count)])]
    all_gather x5 -> x0, waiting for transfers between devices: 229 us -> none  [the longest x1 138 us: per_device(): lax.all_gather(w_gateup[0].astype(jnp.bfloat16), 'fsdp', axis=0, tiled=True)]
    all_gather x10 -> x1, blocking collectives: 216 us -> 11.9 us  [per_device(): lax.all_gather(gains[0].astype(LOW), 'fsdp', axis=1, tiled=True)]
    pallas_call x0 -> x1, Pallas kernels: none -> 193 us  [gather_weights(): pl.pallas_call(functools.partial(weights_kernel, planes, replicas, units,...]
    ppermute x6 -> x91, starting transfers between devices: 1.11 us -> 141 us  [the longest x30 81.6 us: shift(): lax.ppermute(block, axis, [(i, (i + distance) % count) for i in range(cou...]
    dot_general x14 -> x5, matrix products: 99.5 us -> 40.2 us  [contract_rows(): lax.dot_general(left, right, (((0,), (0,)), ((), ())), preferred_element_...]
  transfers between devices with their start and end apart: 21 -> 92, of which waited for: 17 -> 32; matrix products, arithmetic and copies ran while one was open for 11% -> 35% of each run, Pallas kernels for 0% -> 13%
where the time goes in v1:
time: 1490 us; the launch traced here: 1480 us
  other arithmetic  331 us (22%)
  waiting for transfers between devices  331 us (22%)
  local copies, waits for them, and re-layouts  223 us (15%)
  Pallas kernels  193 us (13%)
  matrix products  163 us (11%)
  starting transfers between devices  141 us (9%)
  blocking collectives  72.3 us (5%)
  between operations  26.5 us (2%)
    ppermute x61, waiting for transfers between devices, swap(): return lax.ppermute(block, axis, [(i, i ^ mask) for i in range(count)])  205 us
    pallas_call x1, Pallas kernels, gather_weights(): pl.pallas_call(functools.partial(weights_kernel, planes, replicas, units,...  193 us
    convert_element_type x6, other arithmetic, per_device(): outputs.append(weight_new.astype(LOW))  166 us
    ppermute x30, waiting for transfers between devices, shift(): lax.ppermute(block, axis, [(i, (i + distance) % count) for i in range(cou...  126 us
    ppermute x30, starting transfers between devices, shift(): lax.ppermute(block, axis, [(i, (i + distance) % count) for i in range(cou...  81.6 us
    ppermute x61, starting transfers between devices, swap(): return lax.ppermute(block, axis, [(i, i ^ mask) for i in range(count)])  59.8 us
    dot_general x9, matrix products, contract_cols(): lax.dot_general(left, right, (((1,), (1,)), ((), ())), preferred_element_...  57.9 us
    dynamic_update_slice x15, local copies, waits for them, and re-layouts, columns_from_plane(): lax.dynamic_update_slice_in_dim(full, block, (rank ^ offset) * width, 1)  42.9 us
  transfers between devices with their start and end apart: 92, of which 32 were waited for; matrix products, arithmetic and copies ran while one was open for 35% of the time, Pallas kernels for 13%

profile of v1, /device:TPU:0, one launch (start us, length us, event | category | flops | bytes accessed | tf_op | source)
XLA Modules:
  0.0 1482.5 jit_solution(16330878306975695921)
XLA Ops:
  52.9 193.0 %gather_weights.1 = (bf16[768,2304]{1,0:T(8,128)(2,1)}, bf16[768,768]{1,0:T(8,128)(2,1)}, bf16[768,6144]{1,0:T(8,128)(2,1)}, bf16[3072,768]{1,0:T(8,128)(2,1)}) custom-call(bf16[192,2304]{1,0:T(8,128)(2,1)} %bitcast_convert_fusion.2.refs_0_, bf16[192,768]{1,0:T(8,128)(2,1)} %bitcast_convert_fusion.3.refs_1_, bf16[192,6144]{1,0:T(8,128)(2,1)} %bitcast_convert_fusion.refs_2_, ...), custom_call_target="tpu_custom_call" | custom-call | tf_op jit(solution)/shard_map/gather_weights/pallas_call | solution.py:122
  324.6 26.5 %collective-permute-done.13 = bf16[256,768]{1,0:T(8,128)(2,1)} collective-permute-done((bf16[256,768]{1,0:T(8,128)(2,1)}, bf16[256,768]{1,0:T(8,128)(2,1)}, u32[]{:S(2)}, u32[]{:S(2)}) %collective-permute-start.13) | collective-permute-done | bytes 393248 | tf_op jit(solution)/shard_map/ppermute | solution.py:177
  351.1 25.8 %fusion.263 = (f32[1024]{0:T(1024)S(1)}, f32[1024,8000]{0,1:T(8,128)}) fusion(f32[768,8000]{0,1:T(8,128)} %param.30, bf16[256,768]{1,0:T(8,128)(2,1)} %collective-permute-done.14, bf16[256,768]{1,0:T(8,128)(2,1)} %collective-permute-done.13, bf16[256,768]{1,0:T(8,128)(2,1)} %collective-permute-done.12, bf16[256,768]{1,0:T(8,128)(2,1)} %multiply_convert_fusion.4), kind=kOutput, calls=%fused_computation.518 | convolution fusion | flops 12603538432 | bytes 58920960 | tf_op jit(solution)/shard_map/dot_general | solution.py:394
  376.9 14.8 select_reduce_fusion
  400.2 26.7 %fusion.264 = (bf16[1024,768]{1,0:T(8,128)(2,1)}, f32[1024,768]{1,0:T(8,128)}) fusion(f32[768,8000]{0,1:T(8,128)} %param.30, f32[1024,8000]{0,1:T(8,128)} %get-tuple-element.387, f32[1024]{0:T(1024)S(1)} %bitcast.549, f32[1024]{0:T(1024)S(1)} %bitcast.552, s32[1024]{0:T(1024)S(1)} %select_subtract_fusion), kind=kOutput, calls=%fused_computation.519 | convolution fusion | flops 12638994432 | bytes 62074880 | tf_op jit(solution)/shard_map/dot_general | solution.py:166
  443.9 13.3 collective-permute-done.19
  462.9 25.4 %convolution_convert_fusion = bf16[768,8000]{0,1:T(8,128)(2,1)} fusion(bf16[256,768]{1,0:T(8,128)(2,1)} %collective-permute-done.14, bf16[256,768]{1,0:T(8,128)(2,1)} %collective-permute-done.13, bf16[256,768]{1,0:T(8,128)(2,1)} %collective-permute-done.12, bf16[256,768]{1,0:T(8,128)(2,1)} %multiply_convert_fusion.4, f32[1024,8000]{0,1:T(8,128)} %get-tuple-element.387, ...), kind=kOutput, calls=%fused_computation.19 | convolution fusion | flops 12644499456 | bytes 46641152 | tf_op jit(solution)/shard_map/dot_general | solution.py:160
  488.3 23.8 %reshape.728 = bf16[2,384,8000]{1,0,2:T(2,128)(2,1)} reshape(bf16[768,8000]{0,1:T(8,128)(2,1)} %convolution_convert_fusion) | data formatting | bytes 24576000 | tf_op jit(solution)/shard_map/reshape | solution.py:346
  540.8 27.0 %constant_dynamic-slice_fusion.1 = (bf16[1,384,8000]{1,0,2:T(2,128)(2,1)}, bf16[1,384,8000]{1,0,2:T(2,128)(2,1)}) fusion(bf16[2,384,8000]{1,0,2:T(2,128)(2,1)S(1)} %bitcast.470, s32[]{:T(128)S(6)} %select_n.553, s32[]{:T(128)S(6)} %select_n.554), kind=kLoop, calls=%fused_computation.378 | loop fusion | bytes 24576008 | tf_op jit(solution)/shard_map/jit(dynamic_index_in_dim)/dynamic_slice | solution.py:186
  628.2 40.9 %collective-permute-done.39 = bf16[256,768]{1,0:T(8,128)(2,1)} collective-permute-done((bf16[256,768]{1,0:T(8,128)(2,1)}, bf16[256,768]{1,0:T(8,128)(2,1)}, u32[]{:S(2)}, u32[]{:S(2)}) %collective-permute-start.39) | collective-permute-done | bytes 393248 | tf_op jit(solution)/shard_map/ppermute | solution.py:182
  747.8 20.6 %psum.14 = f32[3,192]{1,0:T(4,128)S(1)} all-reduce(f32[3,192]{1,0:T(4,128)S(1)} %copy.420), channel_id=1, replica_groups=mesh['section'=2,'dp'=4,'fsdp'=4] {'dp'}, use_global_device_ids=true, to_apply=%region_38.39 | all-reduce | flops 576 | bytes 4608 | tf_op jit(solution)/shard_map/psum | solution.py:530
  811.1 26.2 %collective-permute-done.53 = bf16[768,192]{1,0:T(8,128)(2,1)S(1)} collective-permute-done((bf16[768,192]{1,0:T(8,128)(2,1)S(1)}, bf16[768,192]{1,0:T(8,128)(2,1)S(1)}, u32[]{:S(2)}, u32[]{:S(2)}) %collective-permute-start.53) | collective-permute-done | bytes 294944 | tf_op jit(solution)/shard_map/ppermute | solution.py:177
  839.9 13.0 collective-permute-start.27
  864.5 17.6 %scatter_custom_fusion = f32[8000,768]{1,0:T(8,128)} fusion(s32[1024]{0:T(1024)S(1)} %bitcast.551, f32[]{:T(128)} %constant.451.clone.1, bf16[1024,768]{1,0:T(8,128)(2,1)S(1)} %bitcast.487), kind=kCustom, calls=%fused_computation.26 | custom fusion | flops 1572864 | bytes 26148868 | tf_op jit(solution)/shard_map/scatter-add | solution.py:538
  882.1 13.2 convert_element_type.600
  911.7 12.9 collective-permute-done.45
  1020.9 41.9 %collective-permute-done.59 = bf16[96,8000]{1,0:T(8,128)(2,1)S(1)} collective-permute-done((bf16[96,8000]{1,0:T(8,128)(2,1)S(1)}, bf16[96,8000]{1,0:T(8,128)(2,1)S(1)}, u32[]{:S(2)}, u32[]{:S(2)}) %collective-permute-start.59) | collective-permute-done | bytes 1536032 | tf_op jit(solution)/shard_map/ppermute | solution.py:182
  1110.9 25.6 %collective-permute-done.65 = bf16[1000,768]{1,0:T(8,128)(2,1)} collective-permute-done((bf16[1000,768]{1,0:T(8,128)(2,1)}, bf16[1000,768]{1,0:T(8,128)(2,1)}, u32[]{:S(2)}, u32[]{:S(2)}) %collective-permute-start.65) | collective-permute-done | bytes 1536032 | tf_op jit(solution)/shard_map/ppermute | solution.py:182
  1156.7 35.4 %collective-permute-done.66 = bf16[500,768]{1,0:T(8,128)(2,1)} collective-permute-done((bf16[500,768]{1,0:T(8,128)(2,1)}, bf16[500,768]{1,0:T(8,128)(2,1)}, u32[]{:S(2)}, u32[]{:S(2)}) %collective-permute-start.66) | collective-permute-done | bytes 768032 | tf_op jit(solution)/shard_map/ppermute | solution.py:182
  1221.5 39.9 %psum.15 = f32[2]{0:T(128)S(1)} all-reduce(f32[2]{0:T(128)S(1)} %pad_maximum_fusion.21), channel_id=1, replica_groups=mesh['section'=2,'dp'=4,'fsdp'=4] {'section','dp','fsdp'}, use_global_device_ids=true, to_apply=%region_42.43 | all-reduce | flops 2 | bytes 16 | tf_op jit(solution)/shard_map/psum | solution.py:553
  1266.0 14.0 convert_bitcast_fusion
  1307.6 13.6 collective-permute-done.72
  1332.0 67.3 %fusion.233 = (bf16[768,8000]{0,1:T(8,128)(2,1)}, f32[768,8000]{0,1:T(8,128)}, f32[768,8000]{0,1:T(8,128)}, f32[768,8000]{0,1:T(8,128)}) fusion(f32[768,8000]{0,1:T(8,128)} %param.30, f32[]{:T(128)S(6)} %div.359, bf16[192,8000]{0,1:T(8,128)(2,1)} %copy.399, bf16[192,8000]{0,1:T(8,128)(2,1)} %copy.398, bf16[384,8000]{0,1:T(8,128)(2,1)} %collective-permute-done.78, ...), kind=kLoop, calls=%fused_computation.505 | loop fusion | flops 190464000 | bytes 172032000 | tf_op jit(solution)/shard_map/convert_element_type | solution.py:588
  1399.2 74.0 %fusion.235 = (bf16[8000,768]{1,0:T(8,128)(2,1)}, f32[8000,768]{1,0:T(8,128)}, f32[8000,768]{1,0:T(8,128)}, f32[8000,768]{1,0:T(8,128)}) fusion(f32[8000,768]{1,0:T(8,128)} %param.27, f32[]{:T(128)S(6)} %div.359, bf16[2000,768]{1,0:T(8,128)(2,1)S(1)} %maximum_select_fusion.5, bf16[2000,768]{1,0:T(8,128)(2,1)} %copy-done.1, ...), kind=kLoop, calls=%fused_computation.506 | loop fusion | flops 190464000 | bytes 172032000 | tf_op jit(solution)/shard_map/convert_element_type | solution.py:588
  (646 shorter events, 623.8 us)
Async XLA Ops:
  7.2 739.7 %reduce-scatter.4.cloned.1.call-start = ((), (), s32[]{:S(2)}) async-start(), calls=%async_computation.1 | async-start | bytes 491520
  48.9 197.9 %collective-permute-start.5 = (bf16[256,768]{1,0:T(8,128)(2,1)S(1)}, bf16[256,768]{1,0:T(8,128)(2,1)S(1)}, u32[]{:S(2)}, u32[]{:S(2)}) collective-permute-start(bf16[256,768]{1,0:T(8,128)(2,1)S(1)} %get-tuple-element.312), channel_id=1, source_target_pairs={{0,1},{1,2},{2,3},{3,0},{4,5},{5,6},{6,7},{7,4},{8,9},{9,10},{10,1... | collective-permute-start | bytes 1179656 | tf_op jit(solution)/shard_map/ppermute | solution.py:177
  49.9 196.8 %collective-permute-start.4 = (bf16[256,768]{1,0:T(8,128)(2,1)S(1)}, bf16[256,768]{1,0:T(8,128)(2,1)}, u32[]{:S(2)}, u32[]{:S(2)}) collective-permute-start(bf16[256,768]{1,0:T(8,128)(2,1)S(1)} %get-tuple-element.313), channel_id=1, source_target_pairs={{0,2},{1,3},{2,0},{3,1},{4,6},{5,7},{6,4},{7,5},{8,10},{9,11},{10,... | collective-permute-start | bytes 1179656 | tf_op jit(solution)/shard_map/ppermute | solution.py:177
  51.0 196.4 %collective-permute-start.3 = (bf16[256,768]{1,0:T(8,128)(2,1)S(1)}, bf16[256,768]{1,0:T(8,128)(2,1)}, u32[]{:S(2)}, u32[]{:S(2)}) collective-permute-start(bf16[256,768]{1,0:T(8,128)(2,1)S(1)} %get-tuple-element.311), channel_id=1, source_target_pairs={{0,3},{1,0},{2,1},{3,2},{4,7},{5,4},{6,5},{7,6},{8,11},{9,8},{10,9... | collective-permute-start | bytes 1179656 | tf_op jit(solution)/shard_map/ppermute | solution.py:177
  433.1 167.8 %collective-permute-start.9 = (bf16[256,768]{1,0:T(8,128)(2,1)}, bf16[256,768]{1,0:T(8,128)(2,1)}, u32[]{:S(2)}, u32[]{:S(2)}) collective-permute-start(bf16[256,768]{1,0:T(8,128)(2,1)} %multiply_convert_fusion.7), channel_id=1, source_target_pairs={{0,12},{4,8},{8,4},{12,0},{1,13},{5,9},{9,5},{13,1},{2,14},{6,10},... | collective-permute-start | bytes 1179656 | tf_op jit(solution)/shard_map/ppermute | solution.py:182
  435.4 167.0 %collective-permute-start.31 = (bf16[256,768]{0,1:T(8,128)(2,1)}, bf16[256,768]{0,1:T(8,128)(2,1)}, u32[]{:S(2)}, u32[]{:S(2)}) collective-permute-start(bf16[256,768]{0,1:T(8,128)(2,1)} %bitcast.464), channel_id=1, source_target_pairs={{0,12},{4,8},{8,4},{12,0},{1,13},{5,9},{9,5},{13,1},{2,14},{6,10},... | collective-permute-start | bytes 1179656 | tf_op jit(solution)/shard_map/ppermute | solution.py:182
  443.4 160.8 %collective-permute-start.30 = (bf16[256,768]{0,1:T(8,128)(2,1)}, bf16[256,768]{0,1:T(8,128)(2,1)}, u32[]{:S(2)}, u32[]{:S(2)}) collective-permute-start(bf16[256,768]{0,1:T(8,128)(2,1)} %bitcast.464), channel_id=1, source_target_pairs={{0,8},{4,12},{8,0},{12,4},{1,9},{5,13},{9,1},{13,5},{2,10},{6,14},... | collective-permute-start | bytes 1179656 | tf_op jit(solution)/shard_map/ppermute | solution.py:182
  457.2 147.5 %collective-permute-start.29 = (bf16[256,768]{0,1:T(8,128)(2,1)}, bf16[256,768]{0,1:T(8,128)(2,1)}, u32[]{:S(2)}, u32[]{:S(2)}) collective-permute-start(bf16[256,768]{0,1:T(8,128)(2,1)} %bitcast.464), channel_id=1, source_target_pairs={{0,4},{4,0},{8,12},{12,8},{1,5},{5,1},{9,13},{13,9},{2,6},{6,2},{1... | collective-permute-start | bytes 1179656 | tf_op jit(solution)/shard_map/ppermute | solution.py:182
  610.5 321.1 %collective-permute-start.56 = (bf16[384,8000]{0,1:T(8,128)(2,1)}, bf16[384,8000]{0,1:T(8,128)(2,1)}, u32[]{:S(2)}, u32[]{:S(2)}) collective-permute-start(bf16[384,8000]{0,1:T(8,128)(2,1)} %bitcast.462), channel_id=1, source_target_pairs={{0,16},{16,0},{1,17},{17,1},{2,18},{18,2},{3,19},{19,3},{4,20},{20... | collective-permute-start | bytes 18432008 | tf_op jit(solution)/shard_map/ppermute | solution.py:182
  618.9 85.7 %collective-permute-start.49 = (bf16[256,3072]{1,0:T(8,128)(2,1)}, bf16[256,3072]{1,0:T(8,128)(2,1)}, u32[]{:S(2)}, u32[]{:S(2)}) collective-permute-start(bf16[256,3072]{1,0:T(8,128)(2,1)} %copy-done.55), channel_id=1, source_target_pairs={{0,12},{4,8},{8,4},{12,0},{1,13},{5,9},{9,5},{13,1},{2,14},{6,10},... | collective-permute-start | bytes 4718600 | tf_op jit(solution)/shard_map/ppermute | solution.py:182
  619.7 86.6 %collective-permute-start.48 = (bf16[256,3072]{1,0:T(8,128)(2,1)}, bf16[256,3072]{1,0:T(8,128)(2,1)}, u32[]{:S(2)}, u32[]{:S(2)}) collective-permute-start(bf16[256,3072]{1,0:T(8,128)(2,1)} %copy-done.55), channel_id=1, source_target_pairs={{0,8},{4,12},{8,0},{12,4},{1,9},{5,13},{9,1},{13,5},{2,10},{6,14},... | collective-permute-start | bytes 4718600 | tf_op jit(solution)/shard_map/ppermute | solution.py:182
  627.4 79.1 %collective-permute-start.47 = (bf16[256,3072]{1,0:T(8,128)(2,1)}, bf16[256,3072]{1,0:T(8,128)(2,1)}, u32[]{:S(2)}, u32[]{:S(2)}) collective-permute-start(bf16[256,3072]{1,0:T(8,128)(2,1)} %copy-done.55), channel_id=1, source_target_pairs={{0,4},{4,0},{8,12},{12,8},{1,5},{5,1},{9,13},{13,9},{2,6},{6,2},{1... | collective-permute-start | bytes 4718600 | tf_op jit(solution)/shard_map/ppermute | solution.py:182
  730.9 71.7 %collective-permute-start.43 = (bf16[256,1536]{1,0:T(8,128)(2,1)}, bf16[256,1536]{1,0:T(8,128)(2,1)}, u32[]{:S(2)}, u32[]{:S(2)}) collective-permute-start(bf16[256,1536]{1,0:T(8,128)(2,1)} %get-tuple-element.293), channel_id=1, source_target_pairs={{0,12},{4,8},{8,4},{12,0},{1,13},{5,9},{9,5},{13,1},{2,14},{6,10},... | collective-permute-start | bytes 2359304 | tf_op jit(solution)/shard_map/ppermute | solution.py:182
  732.4 70.2 %collective-permute-start.42 = (bf16[256,1536]{1,0:T(8,128)(2,1)}, bf16[256,1536]{1,0:T(8,128)(2,1)}, u32[]{:S(2)}, u32[]{:S(2)}) collective-permute-start(bf16[256,1536]{1,0:T(8,128)(2,1)} %get-tuple-element.294), channel_id=1, source_target_pairs={{0,8},{4,12},{8,0},{12,4},{1,9},{5,13},{9,1},{13,5},{2,10},{6,14},... | collective-permute-start | bytes 2359304 | tf_op jit(solution)/shard_map/ppermute | solution.py:182
  734.0 69.2 %collective-permute-start.41 = (bf16[256,1536]{1,0:T(8,128)(2,1)}, bf16[256,1536]{1,0:T(8,128)(2,1)}, u32[]{:S(2)}, u32[]{:S(2)}) collective-permute-start(bf16[256,1536]{1,0:T(8,128)(2,1)} %get-tuple-element.295), channel_id=1, source_target_pairs={{0,4},{4,0},{8,12},{12,8},{1,5},{5,1},{9,13},{13,9},{2,6},{6,2},{1... | collective-permute-start | bytes 2359304 | tf_op jit(solution)/shard_map/ppermute | solution.py:182
  855.5 69.1 %collective-permute-start.45 = (bf16[192,1536]{1,0:T(8,128)(2,1)}, bf16[192,1536]{1,0:T(8,128)(2,1)}, u32[]{:S(2)}, u32[]{:S(2)}) collective-permute-start(bf16[192,1536]{1,0:T(8,128)(2,1)} %get-tuple-element.300), channel_id=1, source_target_pairs={{0,2},{1,3},{2,0},{3,1},{4,6},{5,7},{6,4},{7,5},{8,10},{9,11},{10,... | collective-permute-start | bytes 1769480 | tf_op jit(solution)/shard_map/ppermute | solution.py:177
  857.5 68.5 %collective-permute-start.44 = (bf16[192,1536]{1,0:T(8,128)(2,1)}, bf16[192,1536]{1,0:T(8,128)(2,1)}, u32[]{:S(2)}, u32[]{:S(2)}) collective-permute-start(bf16[192,1536]{1,0:T(8,128)(2,1)} %get-tuple-element.298), channel_id=1, source_target_pairs={{0,1},{1,2},{2,3},{3,0},{4,5},{5,6},{6,7},{7,4},{8,9},{9,10},{10,1... | collective-permute-start | bytes 1769480 | tf_op jit(solution)/shard_map/ppermute | solution.py:177
  990.3 74.9 %collective-permute-start.64 = (bf16[4000,768]{1,0:T(8,128)(2,1)}, bf16[4000,768]{1,0:T(8,128)(2,1)}, u32[]{:S(2)}, u32[]{:S(2)}) collective-permute-start(bf16[4000,768]{1,0:T(8,128)(2,1)} %dynamic-slice_bitcast_fusion), channel_id=1, source_target_pairs={{0,16},{16,0},{1,17},{17,1},{2,18},{18,2},{3,19},{19,3},{4,20},{20... | collective-permute-start | bytes 18432008 | tf_op jit(solution)/shard_map/ppermute | solution.py:182
  1000.6 88.5 %collective-permute-start.86 = (bf16[192,1536]{1,0:T(8,128)(2,1)}, bf16[192,1536]{1,0:T(8,128)(2,1)}, u32[]{:S(2)}, u32[]{:S(2)}) collective-permute-start(bf16[192,1536]{1,0:T(8,128)(2,1)} %get-tuple-element.236), channel_id=1, source_target_pairs={{0,8},{4,12},{8,0},{12,4},{1,9},{5,13},{9,1},{13,5},{2,10},{6,14},... | collective-permute-start | bytes 1769480 | tf_op jit(solution)/shard_map/ppermute | solution.py:182
  1001.7 217.9 %collective-permute-start.87 = (bf16[192,1536]{1,0:T(8,128)(2,1)}, bf16[192,1536]{1,0:T(8,128)(2,1)}, u32[]{:S(2)}, u32[]{:S(2)}) collective-permute-start(bf16[192,1536]{1,0:T(8,128)(2,1)} %get-tuple-element.236), channel_id=1, source_target_pairs={{0,12},{4,8},{8,4},{12,0},{1,13},{5,9},{9,5},{13,1},{2,14},{6,10},... | collective-permute-start | bytes 1769480 | tf_op jit(solution)/shard_map/ppermute | solution.py:182
  1019.8 73.6 %collective-permute-start.58 = (bf16[48,8000]{1,0:T(8,128)(2,1)}, bf16[48,8000]{1,0:T(8,128)(2,1)}, u32[]{:S(2)}, u32[]{:S(2)}) collective-permute-start(bf16[48,8000]{1,0:T(8,128)(2,1)} %dynamic-slice_bitcast_fusion.8), channel_id=1, source_target_pairs={{0,8},{4,12},{8,0},{12,4},{1,9},{5,13},{9,1},{13,5},{2,10},{6,14},... | collective-permute-start | bytes 2304008 | tf_op jit(solution)/shard_map/ppermute | solution.py:182
  1109.8 89.7 %collective-permute-start.77 = (bf16[96,8000]{1,0:T(8,128)(2,1)}, bf16[96,8000]{1,0:T(8,128)(2,1)}, u32[]{:S(2)}, u32[]{:S(2)}) collective-permute-start(bf16[96,8000]{1,0:T(8,128)(2,1)} %maximum_select_fusion.7), channel_id=1, source_target_pairs={{0,8},{4,12},{8,0},{12,4},{1,9},{5,13},{9,1},{13,5},{2,10},{6,14},... | collective-permute-start | bytes 4608008 | tf_op jit(solution)/shard_map/ppermute | solution.py:182
  1219.6 112.3 %collective-permute-start.78 = (bf16[384,8000]{0,1:T(8,128)(2,1)}, bf16[384,8000]{0,1:T(8,128)(2,1)}, u32[]{:S(2)}, u32[]{:S(2)}) collective-permute-start(bf16[384,8000]{0,1:T(8,128)(2,1)} %copy.397), channel_id=1, source_target_pairs={{0,16},{16,0},{1,17},{17,1},{2,18},{18,2},{3,19},{19,3},{4,20},{20... | collective-permute-start | bytes 18432008 | tf_op jit(solution)/shard_map/ppermute | solution.py:182
  1331.9 67.3 %collective-permute-start.73 = (bf16[4000,768]{1,0:T(8,128)(2,1)}, bf16[4000,768]{1,0:T(8,128)(2,1)}, u32[]{:S(2)}, u32[]{:S(2)}) collective-permute-start(bf16[4000,768]{1,0:T(8,128)(2,1)} %pad_maximum_fusion.1), channel_id=1, source_target_pairs={{0,16},{16,0},{1,17},{17,1},{2,18},{18,2},{3,19},{19,3},{4,20},{20... | collective-permute-start | bytes 18432008 | tf_op jit(solution)/shard_map/ppermute | solution.py:182
  (171 other events, 3285.1 us)
Sparse Core Ops, SparseCore 0:
  688.4 20.9 reduce-scatter.3

commit v2 on v1

--- a/solution.py
+++ b/solution.py
@@ -284,118 +284,185 @@
     )
 
 
-def plane_masks(replicas):
-    return (0, 1, replicas // 2, 1 + replicas // 2)
-
-
-def plane_rank(replicas):
-    index = lax.axis_index("dp")
-    return (index // (replicas // 2)) * 2 + index % 2
-
-
-def everyone(block, replicas):
-    return jnp.concatenate(
-        [block] + [swap(block, "dp", mask) for mask in plane_masks(replicas)[1:]], axis=0
-    )
-
-
-def quarters(block, replicas):
-    rank = plane_rank(replicas)
+def plane_rank():
+    return lax.axis_index("dp")
+
+
+def quarter(block, index):
     width = block.shape[1] // SHARE
-    pieces = []
-    for offset, mask in enumerate(plane_masks(replicas)):
-        piece = lax.dynamic_slice_in_dim(block, (rank ^ offset) * width, width, 1)
-        pieces.append(swap(piece, "dp", mask) if mask else piece)
-    return jnp.concatenate(pieces, axis=0)
-
-
-def rows_to_owner(partial):
-    planes = lax.axis_size("fsdp")
-    me = lax.axis_index("fsdp")
-    blocks = partial.reshape((planes, partial.shape[0] // planes) + partial.shape[1:])
-    total = pick(blocks, me).astype(WIDE)
-    for step in range(1, planes):
-        total = total + shift(pick(blocks, (me + step) % planes), "fsdp", step).astype(WIDE)
-    return total
-
-
-def other_replicas(total, replicas):
-    mask = 2
-    while mask < replicas // 2:
-        total = total + swap(total.astype(LOW), "dp", mask).astype(WIDE)
-        mask *= 2
-    return total
-
-
-def columns_from_plane(piece, replicas):
-    rank = plane_rank(replicas)
-    height, width = piece.shape
-    full = jnp.zeros((height, SHARE * width), piece.dtype)
-    for offset, mask in enumerate(plane_masks(replicas)):
-        block = swap(piece, "dp", mask) if mask else piece
-        full = lax.dynamic_update_slice_in_dim(full, block, (rank ^ offset) * width, 1)
+    return lax.dynamic_slice_in_dim(block, index * width, width, 1)
+
+
+def sub_quarter(block, planes, index):
+    rows, width = block.shape
+    split = block.reshape(rows, planes, SHARE, width // planes // SHARE)
+    return lax.dynamic_index_in_dim(split, index, 2, keepdims=False).reshape(rows, -1)
+
+
+def spread(make):
+    rank = plane_rank()
+    own = make(rank)
+    rows = own.shape[0]
+    full = lax.dynamic_update_slice(jnp.zeros((SHARE * rows, own.shape[1]), LOW), own, (0, 0))
+    for mask in range(1, SHARE):
+        piece = swap(make(rank ^ mask), "dp", mask)
+        full = lax.dynamic_update_slice(full, piece, (mask * rows, 0))
     return full
 
 
-def bit_of(axis, mask):
-    return (lax.axis_index(axis) // mask) % 2
-
-
-def halve(block, axis, mask):
-    bit = bit_of(axis, mask)
-    pair = block.reshape((2, block.shape[0] // 2) + block.shape[1:])
-    theirs = swap(pick(pair, 1 - bit), axis, mask)
-    return (pick(pair, bit).astype(WIDE) + theirs.astype(WIDE)).astype(LOW)
-
-
-def double(block, axis, mask):
-    theirs = swap(block, axis, mask)
-    bit = bit_of(axis, mask)
-    return jnp.where(
-        bit == 0,
-        jnp.concatenate([block, theirs], axis=0),
-        jnp.concatenate([theirs, block], axis=0),
-    )
-
-
-def mask_orders(replicas):
-    masks = [1 << k for k in range(replicas.bit_length() - 1)]
-    return (masks, masks[::-1])
-
-
-def reduce_shared(block, replicas):
-    mine = halve(block, "section", 1)
-    pieces = []
-    for part, order in zip(jnp.split(mine, 2, axis=0), mask_orders(replicas)):
-        for mask in order:
-            part = halve(part, "dp", mask)
-        pieces.append(part)
-    return pieces
-
-
-def gather_shared(pieces, replicas):
-    parts = []
-    for part, order in zip(pieces, mask_orders(replicas)):
-        for mask in order[::-1]:
-            part = double(part, "dp", mask)
-        parts.append(part)
-    return double(jnp.concatenate(parts, axis=0), "section", 1)
-
-
-def head_pass(rows_low, targets, weights_tok, head_low, vocab_start, token_total):
+def in_order(pieces, rank, axis):
+    low = rank % 2 == 0
+    top = rank // 2 == 0
+    pairs = []
+    for k in (0, 2):
+        pairs.append(
+            (jnp.where(low, pieces[k], pieces[k + 1]), jnp.where(low, pieces[k + 1], pieces[k]))
+        )
+    lower = [jnp.where(top, pairs[0][j], pairs[1][j]) for j in range(2)]
+    upper = [jnp.where(top, pairs[1][j], pairs[0][j]) for j in range(2)]
+    return jnp.concatenate(lower + upper, axis=axis)
+
+
+def relative_blocks():
+    s = lax.axis_index("section")
+    i = lax.axis_index("dp")
+    x, y = i % 2, i // 2
+    blocks = []
+    for es in (0, 1):
+        for kind in (0, 1):
+            for e1 in (0, 1):
+                for e2 in (0, 1):
+                    a, b = (x, y) if kind == 0 else (y, x)
+                    within = ((a + e1) % 2) * 2 + (b + e2) % 2
+                    blocks.append(((s + es) % 2) * 8 + kind * 4 + within)
+    return jnp.stack(blocks).astype(jnp.int32)
+
+
+TOKENS = 256
+
+
+def head_piece(vocab):
+    return -(-vocab // 256) * 16
+
+
+def table_block(vocab, base, h_ref):
+    inside = lax.broadcasted_iota(jnp.int32, h_ref.shape, 0) + base < vocab
+    return jnp.where(inside, h_ref[...], 0.0).astype(LOW)
+
+
+def head_scores(vocab, base, table, rows):
+    logits = contract_cols(table, rows)
+    index = lax.broadcasted_iota(jnp.int32, logits.shape, 0) + base
+    return jnp.where(index < vocab, logits, -1e30), index
+
+
+def head_stats_kernel(vocab, h_ref, rows_ref, target_ref, out):
+    step = pl.program_id(0)
+    base = step * h_ref.shape[0]
+    table = table_block(vocab, base, h_ref)
+
+    @pl.when(step == 0)
+    def _():
+        out[0:1, :] = jnp.full((1, out.shape[1]), -1e30, WIDE)
+        out[1:3, :] = jnp.zeros((2, out.shape[1]), WIDE)
+
+    for c in range(rows_ref.shape[0] // TOKENS):
+        span = slice(c * TOKENS, (c + 1) * TOKENS)
+        logits, index = head_scores(vocab, base, table, rows_ref[span, :])
+        before = out[0:1, span]
+        peak = jnp.maximum(before, jnp.max(logits, axis=0, keepdims=True))
+        summed = jnp.sum(jnp.exp(logits - peak), axis=0, keepdims=True)
+        picked = jnp.sum(jnp.where(index == target_ref[:, span], logits, 0.0), axis=0, keepdims=True)
+        out[0:1, span] = peak
+        out[1:2, span] = out[1:2, span] * jnp.exp(before - peak) + summed
+        out[2:3, span] += picked
+
+
+def once(shape):
+    return pl.BlockSpec(shape, lambda g, *_: (0,) * len(shape), pipeline_mode=pl.Buffered(1))
+
+
+def head_stats(head, rows, targets):
+    vocab, count = head.shape[0], rows.shape[0]
+    piece = head_piece(vocab)
+    return pl.pallas_call(
+        functools.partial(head_stats_kernel, vocab),
+        grid=(-(-vocab // piece),),
+        in_specs=[pl.BlockSpec((piece, D), lambda g: (g, 0)), once((count, D)), once((1, count))],
+        out_specs=pl.BlockSpec((8, count), lambda g: (0, 0)),
+        out_shape=jax.ShapeDtypeStruct((8, count), WIDE),
+        compiler_params=pltpu.CompilerParams(vmem_limit_bytes=50 << 20),
+        cost_estimate=pl.CostEstimate(
+            flops=2 * vocab * count * D, bytes_accessed=vocab * D * 4, transcendentals=vocab * count
+        ),
+        name="head_stats",
+    )(head, rows, targets)
+
+
+def head_grads_kernel(vocab, order, h_ref, rows_ref, target_ref, lse_ref, factor_ref, g_ref, c_ref, flipped, delta):
+    step = pl.program_id(0)
+    base = order[step] * h_ref.shape[0]
+    table = table_block(vocab, base, h_ref)
+    flipped[...] = table.astype(WIDE).T.astype(LOW)
+
+    @pl.when(step == 0)
+    def _():
+        c_ref[...] = jnp.zeros(c_ref.shape, WIDE)
+
+    for c in range(rows_ref.shape[0] // TOKENS):
+        span = slice(c * TOKENS, (c + 1) * TOKENS)
+        logits, index = head_scores(vocab, base, table, rows_ref[span, :])
+        onehot = (index == target_ref[:, span]).astype(WIDE)
+        delta[:, span] = (
+            (jnp.exp(logits - lse_ref[:, span]) - onehot) * factor_ref[:, span]
+        ).astype(LOW)
+    g_ref[...] = jnp.dot(delta[...], rows_ref[...], preferred_element_type=WIDE).astype(LOW)
+    for c in range(rows_ref.shape[0] // TOKENS):
+        span = slice(c * TOKENS, (c + 1) * TOKENS)
+        c_ref[:, span] += jnp.dot(flipped[...], delta[:, span], preferred_element_type=WIDE)
+
+
+def head_grads(head, rows, targets, lse, factor):
+    vocab, count = head.shape[0], rows.shape[0]
+    piece = head_piece(vocab)
+    return pl.pallas_call(
+        functools.partial(head_grads_kernel, vocab),
+        grid_spec=pltpu.PrefetchScalarGridSpec(
+            num_scalar_prefetch=1,
+            grid=(16,),
+            in_specs=[
+                pl.BlockSpec((piece, D), lambda g, order: (order[g], 0)),
+                once((count, D)),
+                once((1, count)),
+                once((1, count)),
+                once((1, count)),
+            ],
+            out_specs=[
+                pl.BlockSpec((piece, D), lambda g, order: (g, 0)),
+                pl.BlockSpec((D, count), lambda g, order: (0, 0)),
+            ],
+            scratch_shapes=[pltpu.VMEM((D, piece), LOW), pltpu.VMEM((piece, count), LOW)],
+        ),
+        out_shape=[
+            jax.ShapeDtypeStruct((16 * piece, D), LOW),
+            jax.ShapeDtypeStruct((D, count), WIDE),
+        ],
+        compiler_params=pltpu.CompilerParams(vmem_limit_bytes=56 << 20),
+        cost_estimate=pl.CostEstimate(
+            flops=6 * vocab * count * D, bytes_accessed=vocab * D * 8, transcendentals=vocab * count
+        ),
+        name="head_grads",
+    )(relative_blocks(), head, rows, targets, lse, factor)
+
+
+def head_pass(rows_low, targets, weights_tok, head, vocab_start, token_total):
     planes = lax.axis_size("fsdp")
     gathered = jnp.concatenate(
         [rows_low] + [shift(rows_low, "fsdp", step) for step in range(1, planes)], axis=0
     )
-    local_vocab = head_low.shape[1]
-    columns = jnp.arange(local_vocab, dtype=jnp.int32)
-    local_targets = targets - vocab_start
-    hit = columns[None, :] == local_targets[:, None]
-    logits = jnp.dot(gathered, head_low, preferred_element_type=WIDE)
-    highest = jnp.max(logits, axis=-1)
-    summed = jnp.sum(jnp.exp(logits - highest[:, None]), axis=-1)
-    picked = jnp.sum(jnp.where(hit, logits, 0.0), axis=-1)
-    stats = jnp.stack([highest, summed, picked]).reshape(3, planes, -1)
+    local = targets - vocab_start
+    local = jnp.where((local >= 0) & (local < head.shape[0]), local, -1)[None, :]
+    stats = head_stats(head, gathered, local)[:3].reshape(3, planes, -1)
     parts = [stats] + [
         jnp.roll(shift(stats, "fsdp", step), step, axis=1) for step in range(1, planes)
     ]
@@ -405,14 +472,22 @@
     lse = (peak + jnp.log(total)).reshape(-1)
     loss_part = jnp.sum((lse - jnp.sum(parts[:, 2], axis=0).reshape(-1)) * weights_tok)
     factor = weights_tok / token_total
-    onehot = hit.astype(WIDE)
-    grads_low = ((jnp.exp(logits - lse[:, None]) - onehot) * factor[:, None]).astype(LOW)
-    grad_head = contract_rows(gathered, grads_low).astype(LOW)
-    partial = contract_cols(grads_low, head_low).reshape(planes, -1, D)
+    grad_head, partial = head_grads(head, gathered, local, lse[None, :], factor[None, :])
+    partial = partial.T.reshape(planes, -1, D)
     grad_rows = partial[0]
     for step in range(1, planes):
         grad_rows = grad_rows + shift(partial[step].astype(LOW), "fsdp", planes - step).astype(WIDE)
-    return (loss_part, grad_head, grad_rows)
+    middle = grad_head.shape[0] // 2
+    return (loss_part, grad_head[:middle], grad_head[middle:], grad_rows)
+
+
+def add_low(one, other):
+    return (one.astype(WIDE) + other.astype(WIDE)).astype(LOW)
+
+
+def keep_half(block, mask):
+    half = block.shape[0] // 2
+    return add_low(block[:half], swap(block[half:], "dp", mask))
 
 
 def adam_update(weight, grad, first_mom, second_mom, rate, decay):
@@ -422,6 +497,408 @@
     sec_hat = sec_new / (1.0 - BETA2**STEP_COUNT)
     weight_new = weight - rate * (mom_hat / (jnp.sqrt(sec_hat) + ADAM_EPS) + decay * weight)
     return (weight_new, mom_new, sec_new)
+
+
+def exchange_kernel(planes, rows_ref, pa, pb, *refs):
+    n = (len(refs) - 7) // 2
+    parts, rows_all, head, slots = refs[:n], refs[n], refs[n + 1], refs[n + 2 : 2 * n + 2]
+    send, recv, core_send, core_recv, local = refs[2 * n + 2 :]
+    s = lax.axis_index("section")
+    i = lax.axis_index("dp")
+    z = lax.axis_index("fsdp")
+    x, y = i % 2, i // 2
+    xn, yn, diag = i + 1 - 2 * x, (i + 2) % 4, 3 - i
+    to_x, to_y, to_core = {"dp": xn}, {"dp": yn}, {"section": 1 - s}
+    barrier = pltpu.get_barrier_semaphore()
+    for device in [to_x, to_y, to_core] + [{"fsdp": (z + k) % planes} for k in range(1, planes)]:
+        pl.semaphore_signal(barrier, inc=1, device_id=device, device_id_type=MESH)
+    pl.semaphore_wait(barrier, planes + 2)
+    counts = [0, 0]
+    sent = []
+
+    def put(src, dst, device):
+        over = device is to_core
+        k = counts[over]
+        counts[over] += 1
+        copy = pltpu.make_async_remote_copy(
+            src_ref=src,
+            dst_ref=dst,
+            send_sem=(core_send if over else send).at[k],
+            recv_sem=(core_recv if over else recv).at[k],
+            device_id=device,
+            device_id_type=MESH,
+        )
+        copy.start()
+        sent.append(copy)
+        return copy
+
+    def take(*copies):
+        for copy in copies:
+            copy.wait_recv()
+
+    piece = pa.shape[0]
+    side = 4 * piece
+
+    def head_a(xx, yy, count):
+        return head.at[pl.ds(pl.multiple_of(s * 2 * side + xx * 2 * piece + yy * piece, 16), count)]
+
+    def head_b(xx, yy, count):
+        return head.at[
+            pl.ds(pl.multiple_of(s * 2 * side + side + yy * 2 * piece + xx * piece, 16), count)
+        ]
+
+    own = []
+    for k, (src, dst) in enumerate(
+        [(rows_ref, rows_all.at[s, i, z]), (pa, head_a(x, y, piece)), (pb, head_b(x, y, piece))]
+    ):
+        copy = pltpu.make_async_copy(src, dst, local.at[k])
+        copy.start()
+        own.append(copy)
+    near = [put(rows_ref, rows_all.at[s, i, z], {"fsdp": (z + k) % planes}) for k in range(1, planes)]
+    head1 = [put(pa, head_a(x, y, piece), to_y), put(pb, head_b(x, y, piece), to_x)]
+    reduce = []
+    for m in range(n):
+        height = slots[m].shape[1]
+        for k in range(1, planes):
+            target = (z + k) % planes
+            block = parts[m].at[pl.ds(pl.multiple_of(target * height, 16), height)]
+            reduce.append(put(block, slots[m].at[k - 1], {"fsdp": target}))
+    for copy in own:
+        copy.wait()
+    take(*near)
+    mid = planes // 2
+    early, late = pl.ds(0, mid), pl.ds(mid, planes - mid)
+    a1 = put(rows_all.at[s, i, early], rows_all.at[s, i, early], to_x)
+    b1 = put(rows_all.at[s, i, late], rows_all.at[s, i, late], to_y)
+    core = [put(rows_all.at[s, i], rows_all.at[s, i], to_core)]
+    take(*head1)
+    block = head_a(x, 0, 2 * piece)
+    ha = put(block, block, to_x)
+    block = head_b(0, y, 2 * piece)
+    hb = put(block, block, to_y)
+    take(a1, b1)
+    second = []
+    for who, span, device in ((i, early, to_y), (xn, early, to_y), (i, late, to_x), (yn, late, to_x)):
+        block = rows_all.at[s, who, span]
+        second.append(put(block, block, device))
+    for who, span in ((xn, early), (yn, late)):
+        block = rows_all.at[s, who, span]
+        core.append(put(block, block, to_core))
+    take(ha, hb)
+    block = head.at[pl.ds(pl.multiple_of(s * 2 * side, 16), 2 * side)]
+    core.append(put(block, block, to_core))
+    take(*second)
+    for who, span in ((yn, early), (diag, early), (xn, late), (diag, late)):
+        block = rows_all.at[s, who, span]
+        core.append(put(block, block, to_core))
+    take(*reduce)
+    take(*core)
+    for copy in sent:
+        copy.wait_send()
+
+
+def exchange(planes, row_grads, pieces, parts):
+    piece, vocab = pieces[0].shape
+    shape = jax.ShapeDtypeStruct
+    outs = [shape((2, 4, planes) + row_grads.shape, LOW), shape((16 * piece, vocab), LOW)]
+    outs += [shape((planes - 1, p.shape[0] // planes, p.shape[1]), LOW) for p in parts]
+    copies = (planes - 1) * (1 + len(parts)) + 2 + 2 + 2 + 4
+    anywhere = pl.BlockSpec(memory_space=pl.ANY)
+    result = pl.pallas_call(
+        functools.partial(exchange_kernel, planes),
+        out_shape=outs,
+        in_specs=[anywhere] * (3 + len(parts)),
+        out_specs=[anywhere] * len(outs),
+        scratch_shapes=[pltpu.SemaphoreType.DMA((copies,))] * 2
+        + [pltpu.SemaphoreType.DMA((8,))] * 2
+        + [pltpu.SemaphoreType.DMA((3,))],
+        compiler_params=pltpu.CompilerParams(collective_id=2, has_side_effects=True),
+        name="exchange",
+    )(row_grads, *pieces, *parts)
+    return result[0], result[1], result[2:]
+
+
+VOCAB_BLOCK = 400
+
+
+def chunk_of(lists):
+    return 32 if lists <= 64 else 16
+
+
+def start_chunks(lists, length, step, steps, starts, rows_hbm, buffer, sem):
+    chunk = chunk_of(lists)
+
+    def one(k, carry):
+        at = jnp.minimum(starts[k * steps + step] // 16 * 16, length - chunk)
+        src = rows_hbm.at[pl.ds(pl.multiple_of(k * length + at, 16), chunk)]
+        pltpu.make_async_copy(src, buffer.at[pl.ds(pl.multiple_of(k * chunk, 16), chunk)], sem).start()
+        return carry
+
+    lax.fori_loop(0, lists, one, 0)
+
+
+def block_grad(
+    lists, length, steps, step, starts, passes, bases, rows_hbm, ids_ref, near_ref, buffers, hot, wide_hot, grad, sems
+):
+    chunk = chunk_of(lists)
+    slot = step % 2
+    spare = buffers.at[2]
+
+    @pl.when(step == 0)
+    def _():
+        start_chunks(lists, length, 0, steps, starts, rows_hbm, buffers.at[0], sems.at[0])
+
+    @pl.when(step + 1 < steps)
+    def _():
+        start_chunks(lists, length, step + 1, steps, starts, rows_hbm, buffers.at[1 - slot], sems.at[1 - slot])
+
+    pltpu.make_async_copy(buffers.at[slot], buffers.at[slot], sems.at[slot]).wait()
+    lanes = lax.broadcasted_iota(jnp.int32, (chunk, VOCAB_BLOCK), 1) + bases[step]
+    within = lax.broadcasted_iota(jnp.int32, (chunk, VOCAB_BLOCK), 0)
+
+    def mark(shifted):
+        def one(k, carry):
+            begin = starts[k * steps + step] // 16 * 16 + shifted
+            at = jnp.minimum(begin, length - chunk)
+            ids = ids_ref[pl.ds(pl.multiple_of(k * length + at, 16), chunk), :]
+            same = (ids == lanes) & (within >= begin - at)
+            hot[pl.ds(pl.multiple_of(k * chunk, 16), chunk), :] = same.astype(WIDE).astype(LOW)
+            return carry
+
+        lax.fori_loop(0, lists, one, 0)
+
+    down = lax.broadcasted_iota(jnp.int32, (VOCAB_BLOCK, lists * chunk), 0) + bases[step]
+    wide_hot[...] = (down == near_ref[0]).astype(WIDE).astype(LOW)
+    grad[...] = jnp.dot(wide_hot[...], buffers[slot], preferred_element_type=WIDE)
+
+    def more(p, carry):
+        mark(p * chunk)
+
+        def one(k, inner):
+            begin = starts[k * steps + step] // 16 * 16 + p * chunk
+            at = jnp.minimum(begin, length - chunk)
+            src = rows_hbm.at[pl.ds(pl.multiple_of(k * length + at, 16), chunk)]
+            pltpu.make_async_copy(
+                src, spare.at[pl.ds(pl.multiple_of(k * chunk, 16), chunk)], sems.at[2]
+            ).start()
+            return inner
+
+        lax.fori_loop(0, lists, one, 0)
+        pltpu.make_async_copy(spare, spare, sems.at[2]).wait()
+        grad[...] += contract_rows(hot[...], spare[...])
+        return carry
+
+    lax.fori_loop(1, passes[step], more, 0)
+
+
+def table_square_kernel(lists, length, steps, starts, passes, bases, rows_hbm, ids_ref, near_ref, out, buffers, hot, wide_hot, grad, sems):
+    step = pl.program_id(0)
+    block_grad(lists, length, steps, step, starts, passes, bases, rows_hbm, ids_ref, near_ref, buffers, hot, wide_hot, grad, sems)
+    part = jnp.sum((grad[...] * grad[...]).reshape(-1, 8, D), axis=0)
+    part = jnp.where(passes[step] > 0, part, 0.0)
+
+    @pl.when(step == 0)
+    def _():
+        out[...] = part
+
+    @pl.when(step > 0)
+    def _():
+        out[...] += part
+
+
+def table_adam_kernel(
+    lists, length, steps, rate, decay, starts, passes, bases, clip, rows_hbm, ids_ref, near_ref, w, m, v, w_new, m_new, v_new, low, buffers, hot, wide_hot, grad, sems
+):
+    step = pl.program_id(0)
+    block_grad(lists, length, steps, step, starts, passes, bases, rows_hbm, ids_ref, near_ref, buffers, hot, wide_hot, grad, sems)
+    weight, mom, sec = adam_update(w[...], grad[...] * clip[0], m[...], v[...], rate, decay)
+    w_new[...] = weight
+    m_new[...] = mom
+    v_new[...] = sec
+    low[...] = weight.astype(LOW)
+
+
+def table_scratch(lists):
+    chunk = chunk_of(lists)
+    return [
+        pltpu.VMEM((3, lists * chunk, D), LOW),
+        pltpu.VMEM((lists * chunk, VOCAB_BLOCK), LOW),
+        pltpu.VMEM((VOCAB_BLOCK, lists * chunk), LOW),
+        pltpu.VMEM((VOCAB_BLOCK, D), WIDE),
+        pltpu.SemaphoreType.DMA((3,)),
+    ]
+
+
+def chunk_scalars(ids_sorted, bases):
+    chunk = chunk_of(ids_sorted.shape[0])
+    edges = bases[None, :, None]
+    starts = jnp.sum((ids_sorted[:, None, :] < edges).astype(jnp.int32), axis=-1)
+    ends = jnp.sum((ids_sorted[:, None, :] < edges + VOCAB_BLOCK).astype(jnp.int32), axis=-1)
+    passes = jnp.max((ends - starts // 16 * 16 + chunk - 1) // chunk, axis=0)
+    length = ids_sorted.shape[1]
+    begin = (starts // 16 * 16).T[:, :, None]
+    at = jnp.minimum(begin, length - chunk) + jnp.arange(chunk)[None, None, :]
+    near = jnp.sum(
+        jnp.where(
+            at[..., None] == jnp.arange(length)[None, None, None, :], ids_sorted[None, :, None, :], 0
+        ),
+        axis=-1,
+    )
+    near = jnp.where(at >= begin, near, -(1 << 30)).reshape(near.shape[0], 1, -1)
+    return starts.reshape(-1), jnp.maximum(passes, 1), near
+
+
+def table_square(ids_sorted, ids_column, rows_flat, rank, ranks, vocab_rows):
+    lists, length = ids_sorted.shape
+    total = vocab_rows // VOCAB_BLOCK
+    steps = -(-total // ranks)
+    blocks = rank + ranks * jnp.arange(steps, dtype=jnp.int32)
+    bases = blocks * VOCAB_BLOCK
+    starts, passes, near = chunk_scalars(ids_sorted, bases)
+    passes = jnp.where(blocks < total, passes, 0)
+    out = pl.pallas_call(
+        functools.partial(table_square_kernel, lists, length, steps),
+        grid_spec=pltpu.PrefetchScalarGridSpec(
+            num_scalar_prefetch=3,
+            grid=(steps,),
+            in_specs=[
+                pl.BlockSpec(memory_space=pl.ANY),
+                pl.BlockSpec(
+                    (lists * length, 1), lambda g, *_: (0, 0), pipeline_mode=pl.Buffered(1)
+                ),
+                pl.BlockSpec((1, 1, near.shape[2]), lambda g, *_: (g, 0, 0)),
+            ],
+            out_specs=pl.BlockSpec((8, D), lambda g, *_: (0, 0)),
+            scratch_shapes=table_scratch(lists),
+        ),
+        out_shape=jax.ShapeDtypeStruct((8, D), WIDE),
+        compiler_params=pltpu.CompilerParams(vmem_limit_bytes=56 << 20),
+        name="table_square",
+    )(starts, passes, bases, rows_flat, ids_column, near)
+    return jnp.sum(out)
+
+
+def table_adam(ids_sorted, ids_column, rows_flat, clip_scale, table, mom, sec, rate, decay):
+    lists, length = ids_sorted.shape
+    vocab_rows = table.shape[0]
+    steps = vocab_rows // VOCAB_BLOCK
+    bases = jnp.arange(steps, dtype=jnp.int32) * VOCAB_BLOCK
+    starts, passes, near = chunk_scalars(ids_sorted, bases)
+    block = pl.BlockSpec((VOCAB_BLOCK, D), lambda g, *_: (g, 0))
+    wide = jax.ShapeDtypeStruct(table.shape, WIDE)
+    return pl.pallas_call(
+        functools.partial(table_adam_kernel, lists, length, steps, rate, decay),
+        grid_spec=pltpu.PrefetchScalarGridSpec(
+            num_scalar_prefetch=4,
+            grid=(steps,),
+            in_specs=[
+                pl.BlockSpec(memory_space=pl.ANY),
+                pl.BlockSpec(
+                    (lists * length, 1), lambda g, *_: (0, 0), pipeline_mode=pl.Buffered(1)
+                ),
+                pl.BlockSpec((1, 1, near.shape[2]), lambda g, *_: (g, 0, 0)),
+                block,
+                block,
+                block,
+            ],
+            out_specs=[block] * 4,
+            scratch_shapes=table_scratch(lists),
+        ),
+        out_shape=[wide, wide, wide, jax.ShapeDtypeStruct(table.shape, LOW)],
+        compiler_params=pltpu.CompilerParams(vmem_limit_bytes=60 << 20),
+        cost_estimate=pl.CostEstimate(
+            flops=steps * 2 * VOCAB_BLOCK * lists * chunk_of(lists) * D,
+            bytes_accessed=table.size * 26,
+            transcendentals=table.size,
+        ),
+        name="table_adam",
+    )(starts, passes, bases, clip_scale.reshape(1), rows_flat, ids_column, near, table, mom, sec)
+
+
+HEAD_BLOCK = 512
+
+
+def head_adam_kernel(rate, decay, clip, grad, w, m, v, w_new, m_new, v_new, low):
+    scaled = grad[...].astype(WIDE) * clip[0]
+    weight, mom, sec = adam_update(w[...], scaled, m[...], v[...], rate, decay)
+    w_new[...] = weight
+    m_new[...] = mom
+    v_new[...] = sec
+    low[...] = weight.astype(LOW)
+
+
+def head_adam(grad, clip_scale, head, mom, sec, rate, decay):
+    vocab = head.shape[1]
+    block = pl.BlockSpec((HEAD_BLOCK, D), lambda g, *_: (g, 0))
+    wide = jax.ShapeDtypeStruct((vocab, D), WIDE)
+    results = pl.pallas_call(
+        functools.partial(head_adam_kernel, rate, decay),
+        grid_spec=pltpu.PrefetchScalarGridSpec(
+            num_scalar_prefetch=1,
+            grid=(-(-vocab // HEAD_BLOCK),),
+            in_specs=[block] * 4,
+            out_specs=[block] * 4,
+        ),
+        out_shape=[wide, wide, wide, jax.ShapeDtypeStruct((vocab, D), LOW)],
+        compiler_params=pltpu.CompilerParams(vmem_limit_bytes=56 << 20),
+        cost_estimate=pl.CostEstimate(
+            flops=head.size * 20, bytes_accessed=head.size * 28, transcendentals=head.size
+        ),
+        name="head_adam",
+    )(clip_scale.reshape(1), grad, head.T, mom.T, sec.T)
+    return [item.T for item in results]
+
+
+def small_gather_kernel(axes, sizes, *refs):
+    n = (len(refs) - 2) // 2
+    blocks, outs, send, recv = refs[:n], refs[n : 2 * n], refs[2 * n], refs[2 * n + 1]
+    mine = [lax.axis_index(axis) for axis in axes]
+    slot = 0
+    for index, size in zip(mine, sizes):
+        slot = slot * size + index
+    offsets = [()]
+    for size in sizes:
+        offsets = [o + (k,) for o in offsets for k in range(size)]
+    peers = [
+        {axis: (index + k) % size for axis, index, size, k in zip(axes, mine, sizes, offset)}
+        for offset in offsets[1:]
+    ]
+    barrier = pltpu.get_barrier_semaphore()
+    for peer in peers:
+        pl.semaphore_signal(barrier, inc=1, device_id=peer, device_id_type=MESH)
+    pl.semaphore_wait(barrier, len(peers))
+    copies = []
+    for m in range(n):
+        for k, peer in enumerate(peers):
+            copy = pltpu.make_async_remote_copy(
+                src_ref=blocks[m],
+                dst_ref=outs[m].at[slot],
+                send_sem=send.at[m * len(peers) + k],
+                recv_sem=recv.at[m * len(peers) + k],
+                device_id=peer,
+                device_id_type=MESH,
+            )
+            copy.start()
+            copies.append(copy)
+        outs[m][slot] = blocks[m][...]
+    for copy in copies:
+        copy.wait()
+
+
+def small_gather(blocks, axes, identity):
+    sizes = [lax.axis_size(axis) for axis in axes]
+    count = math.prod(sizes)
+    copies = (count - 1) * len(blocks)
+    whole = pl.BlockSpec(memory_space=pltpu.VMEM)
+    return pl.pallas_call(
+        functools.partial(small_gather_kernel, axes, sizes),
+        out_shape=[jax.ShapeDtypeStruct((count,) + b.shape, b.dtype) for b in blocks],
+        in_specs=[whole] * len(blocks),
+        out_specs=[whole] * len(blocks),
+        scratch_shapes=[pltpu.SemaphoreType.DMA((copies,))] * 2,
+        compiler_params=pltpu.CompilerParams(collective_id=identity, has_side_effects=True),
+        name=f"small_gather_{identity}",
+    )(*blocks)
 
 
 def per_device(
@@ -459,28 +936,45 @@
     tokens = MB * ROW
 
     my_ids = jnp.stack([token_ids.reshape(-1), next_ids.reshape(-1)])
-    rel_ids = jnp.stack([my_ids] + [shift(my_ids, "fsdp", step) for step in range(1, planes)])
+    ids_all, gains_all = small_gather([my_ids, gains[0]], ("dp", "fsdp"), 3)
+    ids_all = ids_all.reshape(replicas, planes, 2, tokens)
+    gains_full = gains_all[:planes].transpose(1, 0, 2).reshape(3, D)
+    gains_full = lax.optimization_barrier(gains_full.astype(LOW)).astype(WIDE)
+    group_ids = pick(ids_all, lax.axis_index("dp"))
+    rel_ids = jnp.stack([pick(group_ids, (me - step) % planes) for step in range(planes)])
     my_kind = jnp.where(first, rel_ids[:, 0], rel_ids[:, 1])
     vocab_rows = embedding.shape[0]
     vocab_start = me * vocab_rows
     local = my_kind - vocab_start
     inside = (local >= 0) & (local < vocab_rows)
     found = jnp.take(embedding, jnp.clip(local, 0, vocab_rows - 1), axis=0)
-    found = jnp.where(inside[..., None], found, 0.0).astype(LOW)
+    found = lax.optimization_barrier(jnp.where(inside[..., None], found, 0.0).astype(LOW))
     looked = found[0].astype(WIDE)
     for step in range(1, planes):
         looked = looked + shift(found[step], "fsdp", planes - step).astype(WIDE)
     next_embed = swap(looked.astype(LOW), "section", 1).astype(WIDE)
 
+    lists = ids_all.transpose(2, 0, 1, 3).reshape(-1, tokens) - vocab_start
+    place = jnp.arange(tokens)
+    before = (lists[:, None, :] < lists[:, :, None]) | (
+        (lists[:, None, :] == lists[:, :, None]) & (place[None, None, :] < place[None, :, None])
+    )
+    ranks = jnp.sum(before.astype(jnp.int32), axis=-1)
+    sorted_ids = jnp.sum(
+        jnp.where(ranks[:, None, :] == place[None, :, None], lists[:, None, :], 0), axis=-1
+    )
+    own_list = (
+        lax.axis_index("section") * replicas + lax.axis_index("dp")
+    ) * planes + me
+    arrange = (pick(ranks, own_list)[None, :] == place[:, None]).astype(LOW)
+
     full = gather_weights(
         planes,
         replicas,
         [w_qkv[0].astype(LOW), w_out[0].astype(LOW), w_gateup[0].astype(LOW), w_down[0].astype(LOW)],
     )
-    gains_full = lax.all_gather(gains[0].astype(LOW), "fsdp", axis=1, tiled=True).astype(WIDE)
     layer_weights = (full[0], full[1], full[2], full[3], gains_full[0], gains_full[1])
     head_gain = gains_full[2]
-    head_low = head_table.astype(LOW)
 
     first_out, _ = layer_fwd(looked, layer_weights)
     middle = swap(first_out.astype(LOW), "section", 1).astype(WIDE)
@@ -492,87 +986,125 @@
     head_in = norm_fwd(merged_in, head_gain)
 
     lengths = seq_lengths.reshape(replicas, planes, MB)[lax.axis_index("dp")]
-    rel_planes = (me - jnp.arange(planes)) % planes
-    lengths = jnp.take(lengths, rel_planes, axis=0)
+    lengths = jnp.stack([pick(lengths, (me - step) % planes) for step in range(planes)])
     targets_main = rel_ids[:, 1].reshape(planes, MB, ROW)
     shifted = jnp.concatenate([targets_main[..., 1:], targets_main[..., :1]], axis=-1)
     targets = jnp.where(first, shifted, targets_main)
     limit = lengths - first.astype(jnp.int32)
     positions = jnp.arange(ROW, dtype=jnp.int32)
     weights_tok = (positions < limit[..., None]).astype(WIDE) * jnp.where(first, MTP_WEIGHT, 1.0)
-    loss_part, grad_head, grad_in = head_pass(
+    left = [saved[0], saved[6], saved[8]]
+    left_all = spread(
+        lambda index: jnp.concatenate(left + [sub_quarter(saved[10], planes, index)], axis=1)
+    )
+    loss_part, mine, theirs, grad_in = head_pass(
         head_in.astype(LOW),
         targets.reshape(-1),
         weights_tok.reshape(-1),
-        head_low,
+        head_table.T,
         vocab_start,
         token_total,
     )
-    head_pieces = reduce_shared(grad_head, replicas)
-
+    sorted_ids, loss_part = lax.optimization_barrier((sorted_ids, loss_part))
     merged_grad, mtp_gain = norm_back(merged_in, head_gain, grad_in)
     merged_low = merged_grad.astype(LOW)
     sent = swap(merged_low, "section", 1).astype(WIDE)
     top_grad, top_gain = norm_back(layer_out, head_gain, grad_in + sent)
     head_gain_grad = jnp.where(first, mtp_gain, top_gain)
+    half = add_low(mine, swap(theirs, "section", 1))
+    top_grad, left_all = lax.optimization_barrier((top_grad, left_all))
     below, _, _ = layer_back(layer_in, layer_weights, saved, top_grad)
-    upstream = jnp.where(first, swap(below.astype(LOW), "section", 1).astype(WIDE), top_grad)
+    below, half = lax.optimization_barrier((below.astype(LOW), half))
+    side = half.shape[0] // 2
+    piece_a, piece_b = keep_half(half[:side], 1), keep_half(half[side:], 2)
+    upstream = jnp.where(first, swap(below, "section", 1).astype(WIDE), top_grad)
     grad_inputs, right, gain_parts = layer_back(layer_in, layer_weights, saved, upstream)
-
-    left = (saved[0], saved[6], saved[8], saved[10])
-    shards = []
-    for a_side, b_side in zip(left, right):
-        a_all = everyone(a_side, replicas)
-        b_all = quarters(b_side, replicas)
-        part = contract_rows(a_all, b_all).astype(LOW)
-        shards.append(other_replicas(rows_to_owner(part), replicas).astype(LOW))
+    grad_inputs, piece_a, piece_b = lax.optimization_barrier((grad_inputs, piece_a, piece_b))
+    piece_a, piece_b = keep_half(piece_a, 2), keep_half(piece_b, 1)
+
+    grad_packed, after_low, grad_gu, upstream_low = right
+    tops = spread(lambda index: upstream_low)
+    early = spread(lambda index: quarter(grad_gu, index))
+    late = spread(
+        lambda index: jnp.concatenate([quarter(after_low, index), quarter(grad_packed, index)], axis=1)
+    )
+    cut = D // SHARE
+    parts = [
+        contract_rows(left_all[:, 2 * D : 3 * D], early),
+        contract_rows(left_all[:, 3 * D :], tops),
+        contract_rows(left_all[:, :D], late[:, cut:]),
+        contract_rows(left_all[:, D : 2 * D], late[:, :cut]),
+    ]
+    parts = [part.astype(LOW) for part in parts]
     gains_grad = jnp.stack([gain_parts[0], gain_parts[1], head_gain_grad])
-    gains_grad = lax.psum(
-        lax.psum_scatter(gains_grad, "fsdp", scatter_dimension=1, tiled=True), "dp"
-    )
+    gains_grad = jnp.sum(small_gather([gains_grad], ("dp", "fsdp"), 4)[0], axis=0)
+    gains_grad = lax.dynamic_slice_in_dim(gains_grad, me * (D // planes), D // planes, 1)
 
     row_grads = jnp.where(first, grad_inputs.astype(LOW), sent.astype(LOW))
-    rel_grads = jnp.stack([row_grads] + [shift(row_grads, "fsdp", step) for step in range(1, planes)])
-    slot = jnp.where(inside, local, vocab_rows)
-    grad_table = jnp.zeros((vocab_rows, D), WIDE)
-    grad_table = grad_table.at[slot.reshape(-1)].add(
-        rel_grads.reshape(-1, D).astype(WIDE), mode="drop"
-    )
-    table_pieces = reduce_shared(grad_table.astype(LOW), replicas)
+    row_grads = jnp.dot(arrange, row_grads, preferred_element_type=WIDE).astype(LOW)
+    rows_all, grad_head, slots = exchange(planes, row_grads, (piece_a, piece_b), parts)
+    rows_flat = rows_all.reshape(-1, D)
+    ids_column = sorted_ids.reshape(-1, 1)
 
     def square(item):
         wide = item.astype(WIDE)
         return jnp.sum(wide * wide)
 
-    squares = jnp.zeros((), WIDE)
-    for item in shards:
-        squares = squares + square(item) * (SHARE / replicas)
-    for item in head_pieces + table_pieces:
+    shards = []
+    for part, slot in zip(parts, slots):
+        mine = pick(part.reshape((planes,) + slot.shape[1:]), me).astype(WIDE)
+        shards.append((mine + jnp.sum(slot.astype(WIDE), axis=0)).astype(LOW))
+    group = lax.axis_index("section") * replicas + lax.axis_index("dp")
+    squares = table_square(sorted_ids, ids_column, rows_flat, group, 2 * replicas, vocab_rows)
+    for item in shards + [piece_a, piece_b]:
         squares = squares + square(item)
     squares = squares + square(gains_grad) / replicas
-    totals = lax.psum(jnp.stack([squares, loss_part / planes]), ("section", "dp", "fsdp"))
+    totals = jnp.stack([squares, loss_part / planes])[:, None] * jnp.ones((1, 128), WIDE)
+    totals = jnp.sum(small_gather([totals], ("section", "dp", "fsdp"), 5)[0], axis=0)[:, 0]
     grad_norm = jnp.sqrt(totals[0])
     loss_total = totals[1]
     clip_scale = CLIP / jnp.maximum(grad_norm, CLIP)
 
-    grad_table = gather_shared(table_pieces, replicas).astype(WIDE)
-    grad_head = gather_shared(head_pieces, replicas).astype(WIDE)
-    layer_grads = [columns_from_plane(item, replicas).astype(WIDE) for item in shards]
-    params = (embedding, head_table, w_qkv[0], w_out[0], w_gateup[0], w_down[0], gains[0])
-    grads_all = (grad_table, grad_head, *layer_grads, gains_grad)
+    shards, clip_scale = lax.optimization_barrier((shards, clip_scale))
+    widths = [0, 2 * D, 3 * D, 3 * D + 3 * cut, 4 * D]
+    packed = jnp.concatenate(shards, axis=1)
+    rank = plane_rank()
+    others = [packed] + [swap(packed, "dp", mask) for mask in range(1, SHARE)]
+    layer_grads = [
+        in_order([other[:, lo:hi] for other in others], rank, 0 if index == 1 else 1).astype(WIDE)
+        for index, (lo, hi) in enumerate(zip(widths[:-1], widths[1:]))
+    ]
+    params = (w_qkv[0], w_out[0], w_gateup[0], w_down[0], gains[0])
+    grads_all = (
+        layer_grads[2],
+        layer_grads[3],
+        layer_grads[0],
+        layer_grads[1],
+        gains_grad,
+    )
     moments = (
-        (embedding_mom, embedding_sec),
-        (head_mom, head_sec),
         (qkv_mom[0], qkv_sec[0]),
         (out_mom[0], out_sec[0]),
         (gateup_mom[0], gateup_sec[0]),
         (down_mom[0], down_sec[0]),
         (gains_mom[0], gains_sec[0]),
     )
-    rates = (0.6, 0.03, 0.03, 0.12, 0.03, 0.03, 0.6)
-    decays = (0.1, 0.1, 0.1, 0.1, 0.1, 0.1, 0.0)
+    rates = (0.03, 0.12, 0.03, 0.03, 0.6)
+    decays = (0.1, 0.1, 0.1, 0.1, 0.0)
     outputs = [loss_total, token_total, grad_norm]
-    for index in range(7):
+    outputs += table_adam(
+        sorted_ids,
+        ids_column,
+        rows_flat,
+        clip_scale,
+        embedding,
+        embedding_mom,
+        embedding_sec,
+        0.6,
+        0.1,
+    )
+    outputs += head_adam(grad_head, clip_scale, head_table, head_mom, head_sec, 0.03, 0.1)
+    for index in range(5):
         weight_new, mom_new, sec_new = adam_update(
             params[index],
             grads_all[index] * clip_scale,
@@ -581,11 +1113,9 @@
             rates[index],
             decays[index],
         )
-        if index >= 2:
-            weight_new, mom_new, sec_new = (weight_new[None], mom_new[None], sec_new[None])
-        outputs.extend([weight_new, mom_new, sec_new])
-        if index < 6:
-            outputs.append(weight_new.astype(LOW))
+        outputs.extend([weight_new[None], mom_new[None], sec_new[None]])
+        if index < 4:
+            outputs.append(weight_new.astype(LOW)[None])
     return tuple(outputs)
 
 

time: 1490 us -> 1090 us (0.73)
  Pallas kernels: 193 us -> 599 us
  waiting for transfers between devices: 331 us -> 98.9 us
  other arithmetic: 331 us -> 134 us
  local copies, waits for them, and re-layouts: 223 us -> 121 us
  starting transfers between devices: 141 us -> 41.1 us
  matrix products: 163 us -> 78.4 us
  blocking collectives: 72.3 us -> 0 us
    pallas_call x0 -> x9, Pallas kernels: none -> 416 us  [the longest x1 154 us: exchange(): pl.pallas_call(functools.partial(exchange_kernel, planes), out_shape=outs...]
    convert_element_type x16 -> x9, other arithmetic: 205 us -> 35.9 us  [the longest x4 22.5 us: per_device(): outputs.append(weight_new.astype(LOW)[None])]
    ppermute x61 -> x25, waiting for transfers between devices: 205 us -> 79.7 us  [swap(): return lax.ppermute(block, axis, [(i, i ^ mask) for i in range(count)])]
    ppermute x30 -> x12, waiting for transfers between devices: 126 us -> 19.2 us  [shift(): lax.ppermute(block, axis, [(i, (i + distance) % count) for i in range(cou...]
    ppermute x30 -> x12, starting transfers between devices: 81.6 us -> 16 us  [shift(): lax.ppermute(block, axis, [(i, (i + distance) % count) for i in range(cou...]
    psum x2 -> x0, blocking collectives: 60.4 us -> none  [the longest x1 39.9 us: per_device(): lax.psum(jnp.stack([squares, loss_part / planes]), ('section', 'dp', 'fsd...]
    ppermute x61 -> x25, starting transfers between devices: 59.8 us -> 25.1 us  [swap(): return lax.ppermute(block, axis, [(i, i ^ mask) for i in range(count)])]
    dot_general x9 -> x8, matrix products: 57.9 us -> 29.7 us  [contract_cols(): lax.dot_general(left, right, (((1,), (1,)), ((), ())), preferred_element_...]
  transfers between devices with their start and end apart: 92 -> 37, of which waited for: 32 -> 8; matrix products, arithmetic and copies ran while one was open for 35% -> 20% of each run, Pallas kernels for 13% -> 36%
where the time goes in v2:
time: 1090 us
  Pallas kernels  599 us (55%)
  other arithmetic  134 us (12%)
  local copies, waits for them, and re-layouts  121 us (11%)
  waiting for transfers between devices  98.9 us (9%)
  matrix products  78.4 us (7%)
  starting transfers between devices  41.1 us (4%)
  between operations  12.9 us (1%)
    pallas_call x1, Pallas kernels, gather_weights(): pl.pallas_call(functools.partial(weights_kernel, planes, replicas, units,...  183 us
    pallas_call x1, Pallas kernels, exchange(): pl.pallas_call(functools.partial(exchange_kernel, planes), out_shape=outs...  154 us
    ppermute x25, waiting for transfers between devices, swap(): return lax.ppermute(block, axis, [(i, i ^ mask) for i in range(count)])  79.7 us
    pallas_call x1, Pallas kernels, table_adam(): pl.pallas_call(functools.partial(table_adam_kernel, lists, length, steps,...  74.3 us
    pallas_call x1, Pallas kernels, head_adam(): pl.pallas_call(functools.partial(head_adam_kernel, rate, decay), grid_spe...  66.1 us
    pallas_call x1, Pallas kernels, head_grads(): pl.pallas_call(functools.partial(head_grads_kernel, vocab), grid_spec=plt...  53.4 us
    pallas_call x3, Pallas kernels, small_gather(): pl.pallas_call(functools.partial(small_gather_kernel, axes, sizes), out_s...  33 us
    dot_general x8, matrix products, contract_cols(): lax.dot_general(left, right, (((1,), (1,)), ((), ())), preferred_element_...  29.7 us
  transfers between devices with their start and end apart: 37, of which 8 were waited for; matrix products, arithmetic and copies ran while one was open for 20% of the time, Pallas kernels for 36%

profile of v2, /device:TPU:0, one launch (start us, length us, event | category | flops | bytes accessed | tf_op | source)
XLA Modules:
  0.0 1085.2 jit_solution(12057708390959323391)
XLA Ops:
  3.3 11.9 %small_gather_3.1 = (s32[16,2,256]{2,1,0:T(2,128)}, f32[16,3,192]{2,1,0:T(4,128)}) custom-call(s32[2,256]{1,0:T(2,128)} %pad_add_fusion.2.refs_0_, f32[3,192]{1,0:T(4,128)} %bitcast.413), custom_call_target="tpu_custom_call" | custom-call | tf_op jit(solution)/shard_map/small_gather_3/pallas_call | solution.py:893
  16.1 13.6 %gather_fusion = bf16[1024,768]{1,0:T(8,128)(2,1)} fusion(f32[8000,768]{1,0:T(8,128)} %w.1, s32[1024]{0:T(1024)S(1)} %broadcast_clamp_fusion), kind=kCustom, calls=%fused_computation | custom fusion | bytes 3149824 | tf_op jit(solution)/shard_map/jit(_take)/gather | solution.py:950
  47.9 182.7 %gather_weights.1 = (bf16[768,2304]{1,0:T(8,128)(2,1)}, bf16[768,768]{1,0:T(8,128)(2,1)}, bf16[768,6144]{1,0:T(8,128)(2,1)}, bf16[3072,768]{1,0:T(8,128)(2,1)}) custom-call(bf16[192,2304]{1,0:T(8,128)(2,1)} %convert_bitcast_fusion.2.refs_0_, bf16[192,768]{1,0:T(8,128)(2,1)} %convert_bitcast_fusion.3.refs_1_, bf16[192,6144]{1,0:T(8,128)(2,1)} %convert_bitcast_fusion.refs_2_, ...), custom_call_target="tpu_custom_call" | custom-call | tf_op jit(solution)/shard_map/gather_weights/pallas_call | solution.py:122
  318.0 15.2 %collective-permute-done.7 = bf16[256,768]{1,0:T(8,128)(2,1)} collective-permute-done((bf16[256,768]{1,0:T(8,128)(2,1)}, bf16[256,768]{1,0:T(8,128)(2,1)}, u32[]{:S(2)}, u32[]{:S(2)}) %collective-permute-start.7) | collective-permute-done | bytes 393248 | tf_op jit(solution)/shard_map/ppermute | solution.py:177
  334.6 27.0 %head_stats.1 = f32[8,1024]{1,0:T(8,128)S(1)} custom-call(f32[8000,768]{1,0:T(8,128)} %bitcast.354, bf16[1024,768]{1,0:T(8,128)(2,1)S(1)} %pad_maximum_fusion.1.rows_ref, s32[1,1024]{1,0:T(1,128)S(1)} %and_select_fusion.target_ref), custom_call_target="tpu_custom_call" | custom-call | flops 12582912000 | bytes 24576000 | tf_op jit(solution)/shard_map/head_stats/pallas_call | solution.py:388
  379.1 53.4 %head_grads.1 = (bf16[8192,768]{1,0:T(8,128)(2,1)}, f32[768,1024]{1,0:T(8,128)}) custom-call(s32[16]{0:T(128)} %stack.154.order, f32[8000,768]{1,0:T(8,128)} %bitcast.355, bf16[1024,768]{1,0:T(8,128)(2,1)} %copy-done, s32[1,1024]{1,0:T(1,128)} %copy-done.1, f32[1,1024]{1,0:T(1,128)} %bitcast.418, f32[1,1024]{1,0:T(1,128)} %bitcast.417), custom_call_target="tpu_custom_call" | custom-call | flops 37748736000 | bytes 49152000 | tf_op jit(solution)/shard_map/head_grads/pallas_call | solution.py:428
  449.1 14.3 %select_reduce_fusion = s32[20,32,32]{2,1,0:T(8,128)S(1)} fusion(s32[32,256]{1,0:T(8,128)S(1)} %select_reduce_fusion.1, s32[20,32,32]{2,1,0:T(8,128)S(1)} %iota_add_fusion), kind=kLoop, calls=%fused_computation.3 | loop fusion | flops 15708160 | bytes 196608 | tf_op jit(solution)/shard_map/reduce_sum | solution.py:741
  472.7 5.9 slice.334
  492.2 11.8 %collective-permute-done.18 = bf16[256,3072]{1,0:T(8,128)(2,1)} collective-permute-done((bf16[256,3072]{1,0:T(8,128)(2,1)}, bf16[256,3072]{1,0:T(8,128)(2,1)}, u32[]{:S(2)}, u32[]{:S(2)}) %collective-permute-start.18) | collective-permute-done | bytes 1572896 | tf_op jit(solution)/shard_map/ppermute | solution.py:182
  507.5 9.0 fusion.160
  516.6 6.4 multiply_reduce_fusion.12
  536.8 9.0 add_convert_fusion
  552.3 6.6 fusion.159
  595.5 11.8 %small_gather_4.1 = f32[16,3,768]{2,1,0:T(4,128)} custom-call(f32[3,768]{1,0:T(4,128)} %pad_maximum_fusion.26.refs_0_), custom_call_target="tpu_custom_call" | custom-call | tf_op jit(solution)/shard_map/small_gather_4/pallas_call | solution.py:893
  627.1 44.8 %collective-permute-done.33 = bf16[256,768]{0,1:T(8,128)(2,1)S(1)} collective-permute-done((bf16[256,768]{0,1:T(8,128)(2,1)S(1)}, bf16[256,768]{0,1:T(8,128)(2,1)S(1)}, u32[]{:S(2)}, u32[]{:S(2)}) %collective-permute-start.33) | collective-permute-done | bytes 393248 | tf_op jit(solution)/shard_map/ppermute | solution.py:182
  677.9 13.3 %collective-permute-done.27 = bf16[256,1536]{1,0:T(8,128)(2,1)S(1)} collective-permute-done((bf16[256,1536]{1,0:T(8,128)(2,1)S(1)}, bf16[256,1536]{1,0:T(8,128)(2,1)S(1)}, u32[]{:S(2)}, u32[]{:S(2)}) %collective-permute-start.27) | collective-permute-done | bytes 786464 | tf_op jit(solution)/shard_map/ppermute | solution.py:182
  701.8 9.4 collective-permute-done.23
  714.9 153.9 %exchange.1 = (bf16[2,4,4,256,768]{4,3,2,1,0:T(8,128)(2,1)}, bf16[8192,768]{1,0:T(8,128)(2,1)}, bf16[3,192,1536]{2,1,0:T(8,128)(2,1)}, bf16[3,192,768]{2,1,0:T(8...) custom-call(bf16[256,768]{1,0:T(8,128)(2,1)} %convolution_convert_fusion.3.rows_ref, ...), custom_call_target="tpu_custom_call" | custom-call | tf_op jit(solution)/shard_map/exchange/pallas_call | solution.py:607
  868.9 8.4 table_square.1
  892.4 9.3 small_gather_5.1
  909.8 66.1 %head_adam.1 = (f32[8000,768]{1,0:T(8,128)}, f32[8000,768]{1,0:T(8,128)}, f32[8000,768]{1,0:T(8,128)}, bf16[8000,768]{1,0:T(8,128)(2,1)}) custom-call(f32[1]{0:T(128)} %bitcast.90.clip, bf16[8192,768]{1,0:T(8,128)(2,1)} %get-tuple-element.93.grad, f32[8000,768]{1,0:T(8,128)} %bitcast.356, f32[8000,768]{1,0:T(8,128)} %bitcast.357, f32[8000,768]{1,0:T(8,128)} %bitcast.358), custom_call_target="tpu_custom_call" | custom-call | flops 122880000 | bytes 172032000 | tf_op jit(solution)/shard_map/head_adam/pallas_call | solution.py:834
  977.1 74.3 %table_adam.1 = (f32[8000,768]{1,0:T(8,128)}, f32[8000,768]{1,0:T(8,128)}, f32[8000,768]{1,0:T(8,128)}, bf16[8000,768]{1,0:T(8,128)(2,1)}) custom-call(s32[640]{0:T(1024)} %reshape.1213.starts, s32[20]{0:T(128)} %broadcast_maximum_fusion.passes, s32[20]{0:T(128)} %copy-done.107, f32[1]{0:T(128)} %bitcast.90.clip, bf16[8192,768]{1,0:T(8,128)(2,1)} %bitcast.341, ...), custom_call_target="tpu_custom_call" | custom-call | flops 12582912000 | bytes 159744000 | tf_op jit(solution)/shard_map/table_adam/pallas_call | solution.py:789
  1055.5 5.7 fusion.167
  1065.9 11.0 %fusion.163 = (bf16[1,192,6144]{2,1,0:T(8,128)(2,1)}, f32[1,192,6144]{2,1,0:T(8,128)}, f32[1,192,6144]{2,1,0:T(8,128)}, f32[1,192,6144]{2,1,0:T(8,128)}) fusion(f32[1,192,6144]{2,1,0:T(8,128)} %param.39, f32[]{:T(128)} %div.401, bf16[1,192,1536]{2,1,0:T(8,128)(2,1)S(1)} %get-tuple-element.293, bf16[1,192,1536]{2,1,0:T(8,128)(2,1)S(1)} %get-tuple-element.292, ...), kind=kLoop, calls=%fused_computation.477 | loop fusion | flops 29491200 | bytes 33030148 | tf_op jit(solution)/shard_map/convert_element_type | solution.py:1118
  (606 shorter events, 297.4 us)
Async XLA Ops:
  32.5 198.8 %collective-permute-start.2 = (bf16[256,768]{1,0:T(8,128)(2,1)}, bf16[256,768]{1,0:T(8,128)(2,1)}, u32[]{:S(2)}, u32[]{:S(2)}) collective-permute-start(bf16[256,768]{1,0:T(8,128)(2,1)} %get-tuple-element.322), channel_id=1, source_target_pairs={{0,1},{1,2},{2,3},{3,0},{4,5},{5,6},{6,7},{7,4},{8,9},{9,10},{10,1... | collective-permute-start | bytes 1179656 | tf_op jit(solution)/shard_map/ppermute | solution.py:177
  33.7 197.6 %collective-permute-start.1 = (bf16[256,768]{1,0:T(8,128)(2,1)}, bf16[256,768]{1,0:T(8,128)(2,1)}, u32[]{:S(2)}, u32[]{:S(2)}) collective-permute-start(bf16[256,768]{1,0:T(8,128)(2,1)} %get-tuple-element.323), channel_id=1, source_target_pairs={{0,2},{1,3},{2,0},{3,1},{4,6},{5,7},{6,4},{7,5},{8,10},{9,11},{10,... | collective-permute-start | bytes 1179656 | tf_op jit(solution)/shard_map/ppermute | solution.py:177
  36.1 195.2 %collective-permute-start = (bf16[256,768]{1,0:T(8,128)(2,1)}, bf16[256,768]{1,0:T(8,128)(2,1)}, u32[]{:S(2)}, u32[]{:S(2)}) collective-permute-start(bf16[256,768]{1,0:T(8,128)(2,1)} %get-tuple-element.321), channel_id=1, source_target_pairs={{0,3},{1,0},{2,1},{3,2},{4,7},{5,4},{6,5},{7,6},{8,11},{9,8},{10,9... | collective-permute-start | bytes 1179656 | tf_op jit(solution)/shard_map/ppermute | solution.py:177
  259.1 31.5 %collective-permute-start.5 = (bf16[256,768]{1,0:T(8,128)(2,1)}, bf16[256,768]{1,0:T(8,128)(2,1)}, u32[]{:S(2)}, u32[]{:S(2)}) collective-permute-start(bf16[256,768]{1,0:T(8,128)(2,1)} %get-tuple-element.276), channel_id=1, source_target_pairs={{0,16},{16,0},{1,17},{17,1},{2,18},{18,2},{3,19},{19,3},{4,20},{20... | collective-permute-start | bytes 1179656 | tf_op jit(solution)/shard_map/ppermute | solution.py:182
  294.6 38.5 %collective-permute-start.7 = (bf16[256,768]{1,0:T(8,128)(2,1)}, bf16[256,768]{1,0:T(8,128)(2,1)}, u32[]{:S(2)}, u32[]{:S(2)}) collective-permute-start(bf16[256,768]{1,0:T(8,128)(2,1)} %multiply_convert_fusion.3), channel_id=1, source_target_pairs={{0,2},{1,3},{2,0},{3,1},{4,6},{5,7},{6,4},{7,5},{8,10},{9,11},{10,... | collective-permute-start | bytes 1179656 | tf_op jit(solution)/shard_map/ppermute | solution.py:177
  298.3 34.8 %collective-permute-start.6 = (bf16[256,768]{1,0:T(8,128)(2,1)}, bf16[256,768]{1,0:T(8,128)(2,1)}, u32[]{:S(2)}, u32[]{:S(2)}) collective-permute-start(bf16[256,768]{1,0:T(8,128)(2,1)} %multiply_convert_fusion.3), channel_id=1, source_target_pairs={{0,1},{1,2},{2,3},{3,0},{4,5},{5,6},{6,7},{7,4},{8,9},{9,10},{10,1... | collective-permute-start | bytes 1179656 | tf_op jit(solution)/shard_map/ppermute | solution.py:177
  365.8 121.0 %collective-permute-start.16 = (bf16[256,3072]{1,0:T(8,128)(2,1)}, bf16[256,3072]{1,0:T(8,128)(2,1)}, u32[]{:S(2)}, u32[]{:S(2)}) collective-permute-start(bf16[256,3072]{1,0:T(8,128)(2,1)} %get-tuple-element.329), channel_id=1, source_target_pairs={{0,4},{4,0},{8,12},{12,8},{1,5},{5,1},{9,13},{13,9},{2,6},{6,2},{1... | collective-permute-start | bytes 4718600 | tf_op jit(solution)/shard_map/ppermute | solution.py:182
  366.3 123.3 %collective-permute-start.17 = (bf16[256,3072]{1,0:T(8,128)(2,1)}, bf16[256,3072]{1,0:T(8,128)(2,1)}, u32[]{:S(2)}, u32[]{:S(2)}) collective-permute-start(bf16[256,3072]{1,0:T(8,128)(2,1)} %get-tuple-element.330), channel_id=1, source_target_pairs={{0,8},{4,12},{8,0},{12,4},{1,9},{5,13},{9,1},{13,5},{2,10},{6,14},... | collective-permute-start | bytes 4718600 | tf_op jit(solution)/shard_map/ppermute | solution.py:182
  439.6 43.0 %collective-permute-start.13 = (bf16[256,768]{1,0:T(8,128)(2,1)}, bf16[256,768]{1,0:T(8,128)(2,1)}, u32[]{:S(2)}, u32[]{:S(2)}) collective-permute-start(bf16[256,768]{1,0:T(8,128)(2,1)} %get-tuple-element.320), channel_id=1, source_target_pairs={{0,2},{1,3},{2,0},{3,1},{4,6},{5,7},{6,4},{7,5},{8,10},{9,11},{10,... | collective-permute-start | bytes 1179656 | tf_op jit(solution)/shard_map/ppermute | solution.py:177
  441.6 41.1 %collective-permute-start.12 = (bf16[256,768]{1,0:T(8,128)(2,1)}, bf16[256,768]{1,0:T(8,128)(2,1)}, u32[]{:S(2)}, u32[]{:S(2)}) collective-permute-start(bf16[256,768]{1,0:T(8,128)(2,1)} %get-tuple-element.318), channel_id=1, source_target_pairs={{0,3},{1,0},{2,1},{3,2},{4,7},{5,4},{6,5},{7,6},{8,11},{9,8},{10,9... | collective-permute-start | bytes 1179656 | tf_op jit(solution)/shard_map/ppermute | solution.py:177
  469.5 34.5 %collective-permute-start.18 = (bf16[256,3072]{1,0:T(8,128)(2,1)}, bf16[256,3072]{1,0:T(8,128)(2,1)}, u32[]{:S(2)}, u32[]{:S(2)}) collective-permute-start(bf16[256,3072]{1,0:T(8,128)(2,1)} %get-tuple-element.328), channel_id=1, source_target_pairs={{0,12},{4,8},{8,4},{12,0},{1,13},{5,9},{9,5},{13,1},{2,14},{6,10},... | collective-permute-start | bytes 4718600 | tf_op jit(solution)/shard_map/ppermute | solution.py:182
  482.7 54.1 %collective-permute-start.19 = (bf16[4096,768]{1,0:T(8,128)(2,1)}, bf16[4096,768]{1,0:T(8,128)(2,1)}, u32[]{:S(2)}, u32[]{:S(2)}) collective-permute-start(bf16[4096,768]{1,0:T(8,128)(2,1)} %slice.334), channel_id=1, source_target_pairs={{0,16},{16,0},{1,17},{17,1},{2,18},{18,2},{3,19},{19,3},{4,20},{20... | collective-permute-start | bytes 18874376 | tf_op jit(solution)/shard_map/ppermute | solution.py:182
  550.3 140.9 %collective-permute-start.22 = (bf16[1024,768]{1,0:T(8,128)(2,1)}, bf16[1024,768]{1,0:T(8,128)(2,1)}, u32[]{:S(2)}, u32[]{:S(2)}) collective-permute-start(bf16[1024,768]{1,0:T(8,128)(2,1)} %get-tuple-element.288), channel_id=1, source_target_pairs={{0,8},{4,12},{8,0},{12,4},{1,9},{5,13},{9,1},{13,5},{2,10},{6,14},... | collective-permute-start | bytes 4718600 | tf_op jit(solution)/shard_map/ppermute | solution.py:182
  570.9 38.7 %collective-permute-start.28 = (bf16[256,768]{1,0:T(8,128)(2,1)}, bf16[256,768]{1,0:T(8,128)(2,1)}, u32[]{:S(2)}, u32[]{:S(2)}) collective-permute-start(bf16[256,768]{1,0:T(8,128)(2,1)} %fusion.56), channel_id=1, source_target_pairs={{0,4},{4,0},{8,12},{12,8},{1,5},{5,1},{9,13},{13,9},{2,6},{6,2},{1... | collective-permute-start | bytes 1179656 | tf_op jit(solution)/shard_map/ppermute | solution.py:182
  572.0 41.3 %collective-permute-start.29 = (bf16[256,768]{1,0:T(8,128)(2,1)}, bf16[256,768]{1,0:T(8,128)(2,1)}, u32[]{:S(2)}, u32[]{:S(2)}) collective-permute-start(bf16[256,768]{1,0:T(8,128)(2,1)} %fusion.56), channel_id=1, source_target_pairs={{0,8},{4,12},{8,0},{12,4},{1,9},{5,13},{9,1},{13,5},{2,10},{6,14},... | collective-permute-start | bytes 1179656 | tf_op jit(solution)/shard_map/ppermute | solution.py:182
  573.5 41.9 %collective-permute-start.30 = (bf16[256,768]{1,0:T(8,128)(2,1)}, bf16[256,768]{1,0:T(8,128)(2,1)}, u32[]{:S(2)}, u32[]{:S(2)}) collective-permute-start(bf16[256,768]{1,0:T(8,128)(2,1)} %fusion.56), channel_id=1, source_target_pairs={{0,12},{4,8},{8,4},{12,0},{1,13},{5,9},{9,5},{13,1},{2,14},{6,10},... | collective-permute-start | bytes 1179656 | tf_op jit(solution)/shard_map/ppermute | solution.py:182
  583.9 34.4 %collective-permute-start.31 = (bf16[256,768]{0,1:T(8,128)(2,1)}, bf16[256,768]{0,1:T(8,128)(2,1)}, u32[]{:S(2)}, u32[]{:S(2)}) collective-permute-start(bf16[256,768]{0,1:T(8,128)(2,1)} %pad_maximum_fusion.16), channel_id=1, source_target_pairs={{0,4},{4,0},{8,12},{12,8},{1,5},{5,1},{9,13},{13,9},{2,6},{6,2},{1... | collective-permute-start | bytes 1179656 | tf_op jit(solution)/shard_map/ppermute | solution.py:182
  609.6 81.6 %collective-permute-start.21 = (bf16[1024,768]{1,0:T(8,128)(2,1)}, bf16[1024,768]{1,0:T(8,128)(2,1)S(1)}, u32[]{:S(2)}, u32[]{:S(2)}) collective-permute-start(bf16[1024,768]{1,0:T(8,128)(2,1)} %get-tuple-element.289), channel_id=1, source_target_pairs={{0,4},{4,0},{8,12},{12,8},{1,5},{5,1},{9,13},{13,9},{2,6},{6,2},{1... | collective-permute-start | bytes 4718600 | tf_op jit(solution)/shard_map/ppermute | solution.py:182
  613.3 64.5 %collective-permute-start.25 = (bf16[256,1536]{1,0:T(8,128)(2,1)}, bf16[256,1536]{1,0:T(8,128)(2,1)S(1)}, u32[]{:S(2)}, u32[]{:S(2)}) collective-permute-start(bf16[256,1536]{1,0:T(8,128)(2,1)} %get-tuple-element.308), channel_id=1, source_target_pairs={{0,4},{4,0},{8,12},{12,8},{1,5},{5,1},{9,13},{13,9},{2,6},{6,2},{1... | collective-permute-start | bytes 2359304 | tf_op jit(solution)/shard_map/ppermute | solution.py:182
  618.3 53.6 %collective-permute-start.33 = (bf16[256,768]{0,1:T(8,128)(2,1)S(1)}, bf16[256,768]{0,1:T(8,128)(2,1)S(1)}, u32[]{:S(2)}, u32[]{:S(2)}) collective-permute-start(bf16[256,768]{0,1:T(8,128)(2,1)S(1)} %copy-done.62), channel_id=1, source_target_pairs={{0,12},{4,8},{8,4},{12,0},{1,13},{5,9},{9,5},{13,1},{2,14},{6,10},... | collective-permute-start | bytes 1179656 | tf_op jit(solution)/shard_map/ppermute | solution.py:182
  625.9 51.9 %collective-permute-start.26 = (bf16[256,1536]{1,0:T(8,128)(2,1)S(1)}, bf16[256,1536]{1,0:T(8,128)(2,1)S(1)}, u32[]{:S(2)}, u32[]{:S(2)}) collective-permute-start(bf16[256,1536]{1,0:T(8,128)(2,1)S(1)} %copy-done.54), channel_id=1, source_target_pairs={{0,8},{4,12},{8,0},{12,4},{1,9},{5,13},{9,1},{13,5},{2,10},{6,14},... | collective-permute-start | bytes 2359304 | tf_op jit(solution)/shard_map/ppermute | solution.py:182
  905.6 145.8 %collective-permute-start.34 = (bf16[192,3072]{1,0:T(8,128)(2,1)}, bf16[192,3072]{1,0:T(8,128)(2,1)}, u32[]{:S(2)}, u32[]{:S(2)}) collective-permute-start(bf16[192,3072]{1,0:T(8,128)(2,1)} %concatenate.205), channel_id=1, source_target_pairs={{0,4},{4,0},{8,12},{12,8},{1,5},{5,1},{9,13},{13,9},{2,6},{6,2},{1... | collective-permute-start | bytes 3538952 | tf_op jit(solution)/shard_map/ppermute | solution.py:182
  907.0 144.4 %collective-permute-start.35 = (bf16[192,3072]{1,0:T(8,128)(2,1)}, bf16[192,3072]{1,0:T(8,128)(2,1)}, u32[]{:S(2)}, u32[]{:S(2)}) collective-permute-start(bf16[192,3072]{1,0:T(8,128)(2,1)} %concatenate.205), channel_id=1, source_target_pairs={{0,8},{4,12},{8,0},{12,4},{1,9},{5,13},{9,1},{13,5},{2,10},{6,14},... | collective-permute-start | bytes 3538952 | tf_op jit(solution)/shard_map/ppermute | solution.py:182
  907.6 143.8 %collective-permute-start.36 = (bf16[192,3072]{1,0:T(8,128)(2,1)}, bf16[192,3072]{1,0:T(8,128)(2,1)}, u32[]{:S(2)}, u32[]{:S(2)}) collective-permute-start(bf16[192,3072]{1,0:T(8,128)(2,1)} %concatenate.205), channel_id=1, source_target_pairs={{0,12},{4,8},{8,4},{12,0},{1,13},{5,9},{9,5},{13,1},{2,14},{6,10},... | collective-permute-start | bytes 3538952 | tf_op jit(solution)/shard_map/ppermute | solution.py:182
  (142 other events, 3520.7 us)

commit v3 on v2

--- a/solution.py
+++ b/solution.py
@@ -27,89 +27,114 @@
 LOW = jnp.bfloat16
 WIDE = jnp.float32
 
+AHEAD = 2
 MESH = pl.DeviceIdType.MESH
 
-def weights_kernel(planes, replicas, units, rows, *refs):
+def weights_kernel(planes, units, rows, *refs):
     n = len(rows)
-    own, full = refs[:n], refs[n:2*n]
-    send, recv, local = refs[2*n:]
+    own, full = refs[:n], refs[n : 2 * n]
+    send, recv, local = refs[2 * n :]
     z = lax.axis_index("fsdp")
     i = lax.axis_index("dp")
-    half = replicas // 2
-    low, top = i % 2, i // half
-    q = top * 2 + low
-    xn = i + 1 - 2 * low
-    yn = (i + half) % replicas
-    qx = top * 2 + 1 - low
-    qy = (1 - top) * 2 + low
+    x, y = i % 2, i // 2
+    q = i
+    xn, yn = i + 1 - 2 * x, (i + 2) % 4
+    near, far = z + 1 - 2 * (z % 2), planes - 1 - z
+    beyond = planes - 1 - near
+    to_x, to_y, to_near, to_far = {"dp": xn}, {"dp": yn}, {"fsdp": near}, {"fsdp": far}
     barrier = pltpu.get_barrier_semaphore()
-    for step in range(1, planes):
-        pl.semaphore_signal(barrier, inc=1, device_id={"fsdp": (z + step) % planes}, device_id_type=MESH)
-    pl.semaphore_signal(barrier, inc=1, device_id={"dp": xn}, device_id_type=MESH)
-    pl.semaphore_signal(barrier, inc=1, device_id={"dp": yn}, device_id_type=MESH)
-    pl.semaphore_wait(barrier, planes + 1)
+    for device in (to_x, to_y, to_near, to_far):
+        pl.semaphore_signal(barrier, inc=1, device_id=device, device_id_type=MESH)
+    pl.semaphore_wait(barrier, 4)
     keep = []
     for m in range(n):
-        c = pltpu.make_async_copy(own[m], full[m].at[pl.ds(pl.multiple_of(z * rows[m], 16), rows[m]), :], local.at[m])
+        c = pltpu.make_async_copy(
+            own[m], full[m].at[pl.ds(pl.multiple_of(z * rows[m], 16), rows[m]), :], local.at[m]
+        )
         c.start()
         keep.append(c)
-    per = 3 * (planes - 1) + (planes - 1)
-    def cp(src, dst, k, dev):
-        return pltpu.make_async_remote_copy(src_ref=src, dst_ref=dst, send_sem=send.at[k], recv_sem=recv.at[k], device_id=dev, device_id_type=MESH)
-    def block(m, plane, quarter, cols):
+    started = []
+
+    def put(src, dst, k, device):
+        copy = pltpu.make_async_remote_copy(
+            src_ref=src,
+            dst_ref=dst,
+            send_sem=send.at[k],
+            recv_sem=recv.at[k],
+            device_id=device,
+            device_id_type=MESH,
+        )
+        copy.start()
+        started.append(copy)
+        return copy
+
+    def block(u, plane, part):
+        m, cols, _ = units[u]
         r = rows[m] // 4
-        return full[m].at[pl.ds(pl.multiple_of(plane * rows[m] + quarter * r, 16), r), pl.ds(cols[0], cols[1])]
-    first, second, third = [], [], []
-    for u, (m, cols, order) in enumerate(units):
+        return full[m].at[pl.ds(pl.multiple_of(plane * rows[m] + part * r, 16), r), pl.ds(*cols)]
+
+    sources = (near, far, beyond)
+    zs, seconds, thirds = {}, {}, []
+    total = len(units)
+
+    def first(u):
+        m, cols, _ = units[u]
         r = rows[m] // 4
-        group = []
-        for step in range(1, planes):
-            src = own[m].at[pl.ds(pl.multiple_of(q * r, 16), r), pl.ds(cols[0], cols[1])]
-            c = cp(src, block(m, z, q, cols), u * per + step - 1, {"fsdp": (z + step) % planes})
-            c.start()
-            group.append(c)
-        first.append(group)
-    def phase2(u):
-        m, cols, order = units[u]
-        base = u * per + planes - 1
-        group = []
-        for step in range(1, planes):
-            first[u][step - 1].wait_recv()
-            b = block(m, (z + planes - step) % planes, q, cols)
-            c = cp(b, b, base + step - 1, {"dp": xn if order == 0 else yn})
-            c.start()
-            group.append(c)
-        second.append(group)
-    def phase3(u):
-        m, cols, order = units[u]
-        base = u * per + 2 * (planes - 1)
-        group = []
-        for step in range(1, planes):
-            second[u][step - 1].wait_recv()
-            for w, quarter in enumerate((q, qx if order == 0 else qy)):
-                b = block(m, (z + planes - step) % planes, quarter, cols)
-                c = cp(b, b, base + 2 * (step - 1) + w, {"dp": yn if order == 0 else xn})
-                c.start()
-                group.append(c)
-        third.append(group)
-    total = len(units)
-    for u in range(total):
-        phase2(u)
-        if u >= 1:
-            phase3(u - 1)
-    phase3(total - 1)
-    for u in range(total):
-        for c in third[u]:
-            c.wait_recv()
-    for u in range(total):
-        for c in first[u] + second[u] + third[u]:
-            c.wait_send()
+        src = own[m].at[pl.ds(pl.multiple_of(q * r, 16), r), pl.ds(*cols)]
+        zs[u, 0] = put(src, block(u, z, q), 12 * u, to_near)
+        zs[u, 1] = put(src, block(u, z, q), 12 * u + 1, to_far)
+
+    def onward(u):
+        zs[u, 1].wait_recv()
+        zs[u, 2] = put(block(u, far, q), block(u, far, q), 12 * u + 2, to_near)
+
+    def second(u, j):
+        if j != 1:
+            zs[u, j].wait_recv()
+        b = block(u, sources[j], q)
+        seconds[u, j] = put(b, b, 12 * u + 3 + j, to_y if units[u][2] else to_x)
+
+    def third(u, j):
+        seconds[u, j].wait_recv()
+        order = units[u][2]
+        for w, part in enumerate((q, yn if order else xn)):
+            b = block(u, sources[j], part)
+            thirds.append(put(b, b, 12 * u + 6 + 2 * j + w, to_x if order else to_y))
+
+    pairs = [(u, u + 1) for u in range(0, total, 2)]
+    for ahead in range(AHEAD):
+        for u in pairs[ahead]:
+            first(u)
+    for t in range(len(pairs) + 2):
+        if t < len(pairs):
+            for u in pairs[t]:
+                onward(u)
+            if t + AHEAD < len(pairs):
+                for u in pairs[t + AHEAD]:
+                    first(u)
+            for j in (0, 1):
+                for u in pairs[t]:
+                    second(u, j)
+        if 1 <= t <= len(pairs):
+            for u in pairs[t - 1]:
+                second(u, 2)
+            for j in (0, 1):
+                for u in pairs[t - 1]:
+                    third(u, j)
+        if t >= 2:
+            for u in pairs[t - 2]:
+                third(u, 2)
+    for c in thirds:
+        c.wait_recv()
+    for c in started:
+        c.wait_send()
     for c in keep:
         c.wait()
 
+
 def gather_weights(planes, replicas, shards):
     rows = [w.shape[0] for w in shards]
-    if any(r % (SHARE * 16) for r in rows):
+    if planes != 4 or replicas != 4 or any(r % (SHARE * 16) for r in rows):
         return [lax.all_gather(w, "fsdp", axis=0, tiled=True) for w in shards]
     units = []
     for m, w in enumerate(shards):
@@ -118,11 +143,11 @@
         step = width // parts
         for p in range(parts):
             units.append((m, (p * step, step), p % 2))
-    copies = len(units) * 4 * (planes - 1)
+    copies = len(units) * 12
     return pl.pallas_call(
-        functools.partial(weights_kernel, planes, replicas, units, rows),
+        functools.partial(weights_kernel, planes, units, rows),
         out_shape=[jax.ShapeDtypeStruct((planes * w.shape[0], w.shape[1]), w.dtype) for w in shards],
-        in_specs=[pl.BlockSpec(memory_space=pl.ANY)] * len(shards),
+        in_specs=[pl.BlockSpec(memory_space=pltpu.VMEM)] * len(shards),
         out_specs=[pl.BlockSpec(memory_space=pl.ANY)] * len(shards),
         scratch_shapes=[pltpu.SemaphoreType.DMA((copies,)), pltpu.SemaphoreType.DMA((copies,)), pltpu.SemaphoreType.DMA((len(shards),))],
         compiler_params=pltpu.CompilerParams(collective_id=1, has_side_effects=True),
@@ -500,14 +525,17 @@
 
 
 def exchange_kernel(planes, rows_ref, pa, pb, *refs):
-    n = (len(refs) - 7) // 2
+    paired = planes == 4
+    n = (len(refs) - 7) // (4 if paired else 2)
     parts, rows_all, head, slots = refs[:n], refs[n], refs[n + 1], refs[n + 2 : 2 * n + 2]
-    send, recv, core_send, core_recv, local = refs[2 * n + 2 :]
+    send, recv, core_send, core_recv, local = refs[2 * n + 2 : 2 * n + 7]
+    totals, extras = refs[2 * n + 7 : 3 * n + 7], refs[3 * n + 7 :]
     s = lax.axis_index("section")
     i = lax.axis_index("dp")
     z = lax.axis_index("fsdp")
     x, y = i % 2, i // 2
     xn, yn, diag = i + 1 - 2 * x, (i + 2) % 4, 3 - i
+    partner = z + 1 - 2 * (z % 2)
     to_x, to_y, to_core = {"dp": xn}, {"dp": yn}, {"section": 1 - s}
     barrier = pltpu.get_barrier_semaphore()
     for device in [to_x, to_y, to_core] + [{"fsdp": (z + k) % planes} for k in range(1, planes)]:
@@ -554,23 +582,45 @@
         copy = pltpu.make_async_copy(src, dst, local.at[k])
         copy.start()
         own.append(copy)
+    reduce = []
+
+    def part_of(m, plane):
+        height = slots[m].shape[1]
+        return parts[m].at[pl.ds(pl.multiple_of(plane * height, 16), height)]
+
+    fetched, passed = [], []
+    if paired:
+        for m in range(n):
+            copy = pltpu.make_async_copy(part_of(m, planes - 1 - z), totals[m], local.at[3 + m])
+            copy.start()
+            fetched.append(copy)
     near = [put(rows_ref, rows_all.at[s, i, z], {"fsdp": (z + k) % planes}) for k in range(1, planes)]
     head1 = [put(pa, head_a(x, y, piece), to_y), put(pb, head_b(x, y, piece), to_x)]
-    reduce = []
-    for m in range(n):
-        height = slots[m].shape[1]
-        for k in range(1, planes):
-            target = (z + k) % planes
-            block = parts[m].at[pl.ds(pl.multiple_of(target * height, 16), height)]
-            reduce.append(put(block, slots[m].at[k - 1], {"fsdp": target}))
+    if not paired:
+        for m in range(n):
+            for k in range(1, planes):
+                target = (z + k) % planes
+                reduce.append(put(part_of(m, target), slots[m].at[k - 1], {"fsdp": target}))
     for copy in own:
         copy.wait()
     take(*near)
+    if paired:
+        for m in range(n):
+            passed.append(put(part_of(m, planes - 1 - partner), extras[m], {"fsdp": partner}))
     mid = planes // 2
     early, late = pl.ds(0, mid), pl.ds(mid, planes - mid)
     a1 = put(rows_all.at[s, i, early], rows_all.at[s, i, early], to_x)
     b1 = put(rows_all.at[s, i, late], rows_all.at[s, i, late], to_y)
     core = [put(rows_all.at[s, i], rows_all.at[s, i], to_core)]
+    if paired:
+        for copy in fetched:
+            copy.wait()
+        for m in range(n):
+            passed[m].wait_recv()
+            held = totals[m][...].astype(WIDE) + extras[m][...].astype(WIDE)
+            totals[m][...] = held.astype(LOW)
+            reduce.append(put(totals[m], slots[m].at[1], {"fsdp": planes - 1 - z}))
+            reduce.append(put(part_of(m, partner), slots[m].at[0], {"fsdp": partner}))
     take(*head1)
     block = head_a(x, 0, 2 * piece)
     ha = put(block, block, to_x)
@@ -601,18 +651,23 @@
     piece, vocab = pieces[0].shape
     shape = jax.ShapeDtypeStruct
     outs = [shape((2, 4, planes) + row_grads.shape, LOW), shape((16 * piece, vocab), LOW)]
-    outs += [shape((planes - 1, p.shape[0] // planes, p.shape[1]), LOW) for p in parts]
+    blocks = [(p.shape[0] // planes, p.shape[1]) for p in parts]
+    paired = planes == 4
+    outs += [shape((2 if paired else planes - 1,) + b, LOW) for b in blocks]
     copies = (planes - 1) * (1 + len(parts)) + 2 + 2 + 2 + 4
     anywhere = pl.BlockSpec(memory_space=pl.ANY)
     result = pl.pallas_call(
         functools.partial(exchange_kernel, planes),
         out_shape=outs,
-        in_specs=[anywhere] * (3 + len(parts)),
+        in_specs=[pl.BlockSpec(memory_space=pltpu.VMEM)] * 3 + [anywhere] * len(parts),
         out_specs=[anywhere] * len(outs),
         scratch_shapes=[pltpu.SemaphoreType.DMA((copies,))] * 2
         + [pltpu.SemaphoreType.DMA((8,))] * 2
-        + [pltpu.SemaphoreType.DMA((3,))],
-        compiler_params=pltpu.CompilerParams(collective_id=2, has_side_effects=True),
+        + [pltpu.SemaphoreType.DMA((3 + len(parts),))]
+        + ([pltpu.VMEM(b, LOW) for b in blocks] * 2 if paired else []),
+        compiler_params=pltpu.CompilerParams(
+            collective_id=2, has_side_effects=True, vmem_limit_bytes=16 << 20
+        ),
         name="exchange",
     )(row_grads, *pieces, *parts)
     return result[0], result[1], result[2:]
@@ -735,16 +790,20 @@
     starts = jnp.sum((ids_sorted[:, None, :] < edges).astype(jnp.int32), axis=-1)
     ends = jnp.sum((ids_sorted[:, None, :] < edges + VOCAB_BLOCK).astype(jnp.int32), axis=-1)
     passes = jnp.max((ends - starts // 16 * 16 + chunk - 1) // chunk, axis=0)
-    length = ids_sorted.shape[1]
-    begin = (starts // 16 * 16).T[:, :, None]
-    at = jnp.minimum(begin, length - chunk) + jnp.arange(chunk)[None, None, :]
-    near = jnp.sum(
-        jnp.where(
-            at[..., None] == jnp.arange(length)[None, None, None, :], ids_sorted[None, :, None, :], 0
-        ),
-        axis=-1,
-    )
-    near = jnp.where(at >= begin, near, -(1 << 30)).reshape(near.shape[0], 1, -1)
+    lists, length = ids_sorted.shape
+    groups = length // 16
+    begin = (starts // 16).T
+    at = jnp.minimum(begin, groups - chunk // 16)
+    by_group = ids_sorted.reshape(lists, groups, 16).transpose(1, 0, 2).reshape(groups, -1)
+    pieces = []
+    for k in range(chunk // 16):
+        wanted = jnp.repeat(at + k, 16, axis=1)
+        found = jnp.zeros(wanted.shape, jnp.int32)
+        for g in range(groups):
+            found = jnp.where(wanted == g, by_group[g][None], found)
+        found = jnp.where(wanted >= jnp.repeat(begin, 16, axis=1), found, -(1 << 30))
+        pieces.append(found.reshape(-1, lists, 16))
+    near = jnp.stack(pieces, axis=2).reshape(begin.shape[0], 1, -1)
     return starts.reshape(-1), jnp.maximum(passes, 1), near
 
 
@@ -1012,15 +1071,15 @@
     top_grad, top_gain = norm_back(layer_out, head_gain, grad_in + sent)
     head_gain_grad = jnp.where(first, mtp_gain, top_gain)
     half = add_low(mine, swap(theirs, "section", 1))
-    top_grad, left_all = lax.optimization_barrier((top_grad, left_all))
+    top_grad, left_all, half = lax.optimization_barrier((top_grad, left_all, half))
     below, _, _ = layer_back(layer_in, layer_weights, saved, top_grad)
-    below, half = lax.optimization_barrier((below.astype(LOW), half))
     side = half.shape[0] // 2
     piece_a, piece_b = keep_half(half[:side], 1), keep_half(half[side:], 2)
+    below, piece_a, piece_b = lax.optimization_barrier((below.astype(LOW), piece_a, piece_b))
     upstream = jnp.where(first, swap(below, "section", 1).astype(WIDE), top_grad)
     grad_inputs, right, gain_parts = layer_back(layer_in, layer_weights, saved, upstream)
+    piece_a, piece_b = keep_half(piece_a, 2), keep_half(piece_b, 1)
     grad_inputs, piece_a, piece_b = lax.optimization_barrier((grad_inputs, piece_a, piece_b))
-    piece_a, piece_b = keep_half(piece_a, 2), keep_half(piece_b, 1)
 
     grad_packed, after_low, grad_gu, upstream_low = right
     tops = spread(lambda index: upstream_low)

time: 1090 us -> 1090 us (level)
  Pallas kernels: 599 us -> 565 us
  other arithmetic: 134 us -> 147 us
  waiting for transfers between devices: 98.9 us -> 111 us
    select_n x2 -> x4, other arithmetic: 3.02 us -> 31.1 us  [chunk_scalars(): jnp.where(wanted >= jnp.repeat(begin, 16, axis=1), found, -(1 << 30))]
    pallas_call x1, Pallas kernels: 183 us -> 155 us  [gather_weights(): pl.pallas_call(functools.partial(weights_kernel, planes, units, rows), ou...]
    reduce_sum x2 -> x0, other arithmetic: 16.6 us -> none  [chunk_scalars(): jnp.sum(jnp.where(at[..., None] == jnp.arange(length)[None, None, None, :...]
    pallas_call x1, Pallas kernels: 154 us -> 140 us  [exchange(): pl.pallas_call(functools.partial(exchange_kernel, planes), out_shape=outs...]
    ppermute x25, waiting for transfers between devices: 79.7 us -> 93.1 us  [swap(): return lax.ppermute(block, axis, [(i, i ^ mask) for i in range(count)])]
  transfers between devices with their start and end apart: 37 -> 37, of which waited for: 8 -> 9; matrix products, arithmetic and copies ran while one was open for 20% -> 19% of each run, Pallas kernels for 36% -> 33%
where the time goes in v3:
time: 1090 us; the launch traced here: 1080 us
  Pallas kernels  565 us (52%)
  other arithmetic  147 us (13%)
  local copies, waits for them, and re-layouts  128 us (12%)
  waiting for transfers between devices  111 us (10%)
  matrix products  79.6 us (7%)
  starting transfers between devices  37.5 us (3%)
  between operations  13.1 us (1%)
    pallas_call x1, Pallas kernels, gather_weights(): pl.pallas_call(functools.partial(weights_kernel, planes, units, rows), ou...  155 us
    pallas_call x1, Pallas kernels, exchange(): pl.pallas_call(functools.partial(exchange_kernel, planes), out_shape=outs...  140 us
    ppermute x25, waiting for transfers between devices, swap(): return lax.ppermute(block, axis, [(i, i ^ mask) for i in range(count)])  93.1 us
    pallas_call x1, Pallas kernels, table_adam(): pl.pallas_call(functools.partial(table_adam_kernel, lists, length, steps,...  74.2 us
    pallas_call x1, Pallas kernels, head_adam(): pl.pallas_call(functools.partial(head_adam_kernel, rate, decay), grid_spe...  66.1 us
    pallas_call x1, Pallas kernels, head_grads(): pl.pallas_call(functools.partial(head_grads_kernel, vocab), grid_spec=plt...  53.4 us
    pallas_call x3, Pallas kernels, small_gather(): pl.pallas_call(functools.partial(small_gather_kernel, axes, sizes), out_s...  41 us
    dot_general x8, matrix products, contract_cols(): lax.dot_general(left, right, (((1,), (1,)), ((), ())), preferred_element_...  34.2 us
  transfers between devices with their start and end apart: 37, of which 9 were waited for; matrix products, arithmetic and copies ran while one was open for 19% of the time, Pallas kernels for 33%

profile of v3, /device:TPU:0, one launch (start us, length us, event | category | flops | bytes accessed | tf_op | source)
XLA Modules:
  0.0 1081.2 jit_solution(11156632236518457082)
XLA Ops:
  3.3 11.9 %small_gather_3.1 = (s32[16,2,256]{2,1,0:T(2,128)}, f32[16,3,192]{2,1,0:T(4,128)}) custom-call(s32[2,256]{1,0:T(2,128)} %pad_add_fusion.4.refs_0_, f32[3,192]{1,0:T(4,128)} %bitcast.446), custom_call_target="tpu_custom_call" | custom-call | tf_op jit(solution)/shard_map/small_gather_3/pallas_call | solution.py:952
  16.1 13.6 %gather_fusion = bf16[1024,768]{1,0:T(8,128)(2,1)} fusion(f32[8000,768]{1,0:T(8,128)} %w.1, s32[1024]{0:T(1024)S(1)} %broadcast_clamp_fusion), kind=kCustom, calls=%fused_computation | custom fusion | bytes 3149824 | tf_op jit(solution)/shard_map/jit(_take)/gather | solution.py:1009
  46.7 154.6 %gather_weights.1 = (bf16[768,2304]{1,0:T(8,128)(2,1)}, bf16[768,768]{1,0:T(8,128)(2,1)}, bf16[768,6144]{1,0:T(8,128)(2,1)}, bf16[3072,768]{1,0:T(8,128)(2,1)}) custom-call(bf16[192,2304]{1,0:T(8,128)(2,1)} %convert_bitcast_fusion.2.refs_0_, bf16[192,768]{1,0:T(8,128)(2,1)} %convert_bitcast_fusion.3.refs_1_, bf16[192,6144]{1,0:T(8,128)(2,1)} %convert_bitcast_fusion.refs_2_, ...), custom_call_target="tpu_custom_call" | custom-call | tf_op jit(solution)/shard_map/gather_weights/pallas_call | solution.py:147
  246.4 6.0 fusion.194
  281.9 14.8 %collective-permute-done.7 = bf16[256,768]{1,0:T(8,128)(2,1)} collective-permute-done((bf16[256,768]{1,0:T(8,128)(2,1)}, bf16[256,768]{1,0:T(8,128)(2,1)}, u32[]{:S(2)}, u32[]{:S(2)}) %collective-permute-start.7) | collective-permute-done | bytes 393248 | tf_op jit(solution)/shard_map/ppermute | solution.py:202
  298.2 27.0 %head_stats.1 = f32[8,1024]{1,0:T(8,128)S(1)} custom-call(f32[8000,768]{1,0:T(8,128)} %bitcast.390, bf16[1024,768]{1,0:T(8,128)(2,1)S(1)} %pad_maximum_fusion.1.rows_ref, s32[1,1024]{1,0:T(1,128)S(1)} %and_select_fusion.target_ref), custom_call_target="tpu_custom_call" | custom-call | flops 12582912000 | bytes 24576000 | tf_op jit(solution)/shard_map/head_stats/pallas_call | solution.py:413
  344.6 53.4 %head_grads.1 = (bf16[8192,768]{1,0:T(8,128)(2,1)}, f32[768,1024]{1,0:T(8,128)}) custom-call(s32[16]{0:T(128)} %stack.160.order, f32[8000,768]{1,0:T(8,128)} %bitcast.391, bf16[1024,768]{1,0:T(8,128)(2,1)} %copy-done.2, s32[1,1024]{1,0:T(1,128)} %copy-done.12, f32[1,1024]{1,0:T(1,128)} %bitcast.451, f32[1,1024]{1,0:T(1,128)} %bitcast.450), custom_call_target="tpu_custom_call" | custom-call | flops 37748736000 | bytes 49152000 | tf_op jit(solution)/shard_map/head_grads/pallas_call | solution.py:453
  414.2 12.2 %broadcast_select_fusion.16 = s32[20,32,1,16]{3,2,1,0:T(1,128)S(1)} fusion(pred[20,32]{1,0:T(8,128)(4,1)S(1)} %get-tuple-element.415, pred[20,32]{1,0:T(8,128)(4,1)S(1)} %get-tuple-element.414, pred[20,32]{1,0:T(8,128)(4,1)S(1)} %get-tuple-element.413, pred[20,32]{1,0:T(8,128)(4,1)S(1)} %get-tuple-element.386, pred[20,32]{1,0:T(8,128)(4,1)S(1)} %get-tuple-element.387, ...), kind=kLoop, calls=%fused_computation.175 | loop fusion | flops 174080 | bytes 84608 | tf_op jit(solution)/shard_map/jit(_where)/select_n | solution.py:804
  426.5 12.2 %broadcast_select_fusion.33 = s32[20,32,1,16]{3,2,1,0:T(1,128)S(1)} fusion(pred[20,32]{1,0:T(8,128)(4,1)S(1)} %get-tuple-element.416, pred[20,32]{1,0:T(8,128)(4,1)S(1)} %get-tuple-element.417, pred[20,32]{1,0:T(8,128)(4,1)S(1)} %get-tuple-element.400, pred[20,32]{1,0:T(8,128)(4,1)S(1)} %get-tuple-element.401, pred[20,32]{1,0:T(8,128)(4,1)S(1)} %get-tuple-element.402, ...), kind=kLoop, calls=%fused_computation.192 | loop fusion | flops 174080 | bytes 84608 | tf_op jit(solution)/shard_map/jit(_where)/select_n | solution.py:804
  467.0 21.0 %collective-permute-done.18 = bf16[256,3072]{1,0:T(8,128)(2,1)} collective-permute-done((bf16[256,3072]{1,0:T(8,128)(2,1)}, bf16[256,3072]{1,0:T(8,128)(2,1)}, u32[]{:S(2)}, u32[]{:S(2)}) %collective-permute-start.18) | collective-permute-done | bytes 1572896 | tf_op jit(solution)/shard_map/ppermute | solution.py:207
  492.1 9.1 add_convert_fusion
  501.1 9.3 fusion.162
  510.5 8.8 multiply_reduce_fusion.12
  538.0 28.4 %collective-permute-done.21 = bf16[1024,768]{1,0:T(8,128)(2,1)S(1)} collective-permute-done((bf16[1024,768]{1,0:T(8,128)(2,1)S(1)}, bf16[1024,768]{1,0:T(8,128)(2,1)S(1)}, u32[]{:S(2)}, u32[]{:S(2)}) %collective-permute-start.21) | collective-permute-done | bytes 1572896 | tf_op jit(solution)/shard_map/ppermute | solution.py:207
  573.7 7.6 fusion.161
  618.1 10.2 small_gather_4.1
  642.4 17.5 %collective-permute-done.31 = bf16[256,768]{0,1:T(8,128)(2,1)S(1)} collective-permute-done((bf16[256,768]{0,1:T(8,128)(2,1)}, bf16[256,768]{0,1:T(8,128)(2,1)S(1)}, u32[]{:S(2)}, u32[]{:S(2)}) %collective-permute-start.31) | collective-permute-done | bytes 393248 | tf_op jit(solution)/shard_map/ppermute | solution.py:207
  664.4 24.7 %collective-permute-done.32 = bf16[256,768]{0,1:T(8,128)(2,1)S(1)} collective-permute-done((bf16[256,768]{0,1:T(8,128)(2,1)S(1)}, bf16[256,768]{0,1:T(8,128)(2,1)S(1)}, u32[]{:S(2)}, u32[]{:S(2)}) %collective-permute-start.32) | collective-permute-done | bytes 393248 | tf_op jit(solution)/shard_map/ppermute | solution.py:207
  700.1 140.0 %exchange.1 = (bf16[2,4,4,256,768]{4,3,2,1,0:T(8,128)(2,1)S(1)}, bf16[8192,768]{1,0:T(8,128)(2,1)S(1)}, bf16[2,192,1536]{2,1,0:T(8,128)(2,1)S(1)}, bf16[2,192,76...) custom-call(bf16[256,768]{1,0:T(8,128)(2,1)S(1)} %convolution_convert_fusion.3.rows_ref, ...), custom_call_target="tpu_custom_call" | custom-call | tf_op jit(solution)/shard_map/exchange/pallas_call | solution.py:659
  852.7 8.3 table_square.1
  878.9 18.9 %small_gather_5.1 = f32[32,2,128]{2,1,0:T(2,128)} custom-call(f32[2,128]{1,0:T(2,128)} %mul.1635.refs_0_), custom_call_target="tpu_custom_call" | custom-call | tf_op jit(solution)/shard_map/small_gather_5/pallas_call | solution.py:952
  905.8 66.1 %head_adam.1 = (f32[8000,768]{1,0:T(8,128)}, f32[8000,768]{1,0:T(8,128)}, f32[8000,768]{1,0:T(8,128)}, bf16[8000,768]{1,0:T(8,128)(2,1)}) custom-call(f32[1]{0:T(128)} %bitcast.109.clip, bf16[8192,768]{1,0:T(8,128)(2,1)} %copy-done.1, f32[8000,768]{1,0:T(8,128)} %bitcast.392, f32[8000,768]{1,0:T(8,128)} %bitcast.393, f32[8000,768]{1,0:T(8,128)} %bitcast.394), custom_call_target="tpu_custom_call" | custom-call | flops 122880000 | bytes 172032000 | tf_op jit(solution)/shard_map/head_adam/pallas_call | solution.py:893
  973.1 74.2 %table_adam.1 = (f32[8000,768]{1,0:T(8,128)}, f32[8000,768]{1,0:T(8,128)}, f32[8000,768]{1,0:T(8,128)}, bf16[8000,768]{1,0:T(8,128)(2,1)}) custom-call(s32[640]{0:T(1024)} %reshape.2012.starts, s32[20]{0:T(128)} %broadcast_maximum_fusion.passes, s32[20]{0:T(128)} %copy-done.109, f32[1]{0:T(128)} %bitcast.109.clip, bf16[8192,768]{1,0:T(8,128)(2,1)} %bitcast.375, ...), custom_call_target="tpu_custom_call" | custom-call | flops 12582912000 | bytes 159744000 | tf_op jit(solution)/shard_map/table_adam/pallas_call | solution.py:848
  1061.9 11.0 %fusion.165 = (bf16[1,192,6144]{2,1,0:T(8,128)(2,1)}, f32[1,192,6144]{2,1,0:T(8,128)}, f32[1,192,6144]{2,1,0:T(8,128)}, f32[1,192,6144]{2,1,0:T(8,128)}) fusion(f32[1,192,6144]{2,1,0:T(8,128)} %param.39, f32[]{:T(128)} %div.401, bf16[1,192,1536]{2,1,0:T(8,128)(2,1)S(1)} %get-tuple-element.295, bf16[1,192,1536]{2,1,0:T(8,128)(2,1)S(1)} %get-tuple-element.294, ...), kind=kLoop, calls=%fused_computation.623 | loop fusion | flops 29491200 | bytes 33030148 | tf_op jit(solution)/shard_map/convert_element_type | solution.py:1177
  (617 shorter events, 307.2 us)
Async XLA Ops:
  32.5 169.0 %collective-permute-start.2 = (bf16[256,768]{1,0:T(8,128)(2,1)}, bf16[256,768]{1,0:T(8,128)(2,1)}, u32[]{:S(2)}, u32[]{:S(2)}) collective-permute-start(bf16[256,768]{1,0:T(8,128)(2,1)} %get-tuple-element.324), channel_id=1, source_target_pairs={{0,1},{1,2},{2,3},{3,0},{4,5},{5,6},{6,7},{7,4},{8,9},{9,10},{10,1... | collective-permute-start | bytes 1179656 | tf_op jit(solution)/shard_map/ppermute | solution.py:202
  33.7 167.8 %collective-permute-start.1 = (bf16[256,768]{1,0:T(8,128)(2,1)}, bf16[256,768]{1,0:T(8,128)(2,1)}, u32[]{:S(2)}, u32[]{:S(2)}) collective-permute-start(bf16[256,768]{1,0:T(8,128)(2,1)} %get-tuple-element.325), channel_id=1, source_target_pairs={{0,2},{1,3},{2,0},{3,1},{4,6},{5,7},{6,4},{7,5},{8,10},{9,11},{10,... | collective-permute-start | bytes 1179656 | tf_op jit(solution)/shard_map/ppermute | solution.py:202
  36.1 165.4 %collective-permute-start = (bf16[256,768]{1,0:T(8,128)(2,1)}, bf16[256,768]{1,0:T(8,128)(2,1)}, u32[]{:S(2)}, u32[]{:S(2)}) collective-permute-start(bf16[256,768]{1,0:T(8,128)(2,1)} %get-tuple-element.323), channel_id=1, source_target_pairs={{0,3},{1,0},{2,1},{3,2},{4,7},{5,4},{6,5},{7,6},{8,11},{9,8},{10,9... | collective-permute-start | bytes 1179656 | tf_op jit(solution)/shard_map/ppermute | solution.py:202
  260.8 36.0 %collective-permute-start.7 = (bf16[256,768]{1,0:T(8,128)(2,1)}, bf16[256,768]{1,0:T(8,128)(2,1)}, u32[]{:S(2)}, u32[]{:S(2)}) collective-permute-start(bf16[256,768]{1,0:T(8,128)(2,1)} %multiply_convert_fusion.3), channel_id=1, source_target_pairs={{0,2},{1,3},{2,0},{3,1},{4,6},{5,7},{6,4},{7,5},{8,10},{9,11},{10,... | collective-permute-start | bytes 1179656 | tf_op jit(solution)/shard_map/ppermute | solution.py:202
  261.9 34.8 %collective-permute-start.6 = (bf16[256,768]{1,0:T(8,128)(2,1)}, bf16[256,768]{1,0:T(8,128)(2,1)}, u32[]{:S(2)}, u32[]{:S(2)}) collective-permute-start(bf16[256,768]{1,0:T(8,128)(2,1)} %multiply_convert_fusion.3), channel_id=1, source_target_pairs={{0,1},{1,2},{2,3},{3,0},{4,5},{5,6},{6,7},{7,4},{8,9},{9,10},{10,1... | collective-permute-start | bytes 1179656 | tf_op jit(solution)/shard_map/ppermute | solution.py:202
  329.3 132.3 %collective-permute-start.16 = (bf16[256,3072]{1,0:T(8,128)(2,1)}, bf16[256,3072]{1,0:T(8,128)(2,1)}, u32[]{:S(2)}, u32[]{:S(2)}) collective-permute-start(bf16[256,3072]{1,0:T(8,128)(2,1)} %get-tuple-element.331), channel_id=1, source_target_pairs={{0,4},{4,0},{8,12},{12,8},{1,5},{5,1},{9,13},{13,9},{2,6},{6,2},{1... | collective-permute-start | bytes 4718600 | tf_op jit(solution)/shard_map/ppermute | solution.py:207
  330.8 133.5 %collective-permute-start.17 = (bf16[256,3072]{1,0:T(8,128)(2,1)}, bf16[256,3072]{1,0:T(8,128)(2,1)}, u32[]{:S(2)}, u32[]{:S(2)}) collective-permute-start(bf16[256,3072]{1,0:T(8,128)(2,1)} %get-tuple-element.332), channel_id=1, source_target_pairs={{0,8},{4,12},{8,0},{12,4},{1,9},{5,13},{9,1},{13,5},{2,10},{6,14},... | collective-permute-start | bytes 4718600 | tf_op jit(solution)/shard_map/ppermute | solution.py:207
  404.6 39.3 %collective-permute-start.14 = (bf16[256,768]{1,0:T(8,128)(2,1)}, bf16[256,768]{1,0:T(8,128)(2,1)}, u32[]{:S(2)}, u32[]{:S(2)}) collective-permute-start(bf16[256,768]{1,0:T(8,128)(2,1)} %get-tuple-element.321), channel_id=1, source_target_pairs={{0,1},{1,2},{2,3},{3,0},{4,5},{5,6},{6,7},{7,4},{8,9},{9,10},{10,1... | collective-permute-start | bytes 1179656 | tf_op jit(solution)/shard_map/ppermute | solution.py:202
  404.8 45.3 %collective-permute-start.13 = (bf16[256,768]{1,0:T(8,128)(2,1)}, bf16[256,768]{1,0:T(8,128)(2,1)}, u32[]{:S(2)}, u32[]{:S(2)}) collective-permute-start(bf16[256,768]{1,0:T(8,128)(2,1)} %get-tuple-element.322), channel_id=1, source_target_pairs={{0,2},{1,3},{2,0},{3,1},{4,6},{5,7},{6,4},{7,5},{8,10},{9,11},{10,... | collective-permute-start | bytes 1179656 | tf_op jit(solution)/shard_map/ppermute | solution.py:202
  411.6 80.4 %collective-permute-start.19 = (bf16[4096,768]{1,0:T(8,128)(2,1)}, bf16[4096,768]{1,0:T(8,128)(2,1)}, u32[]{:S(2)}, u32[]{:S(2)}) collective-permute-start(bf16[4096,768]{1,0:T(8,128)(2,1)} %slice.442), channel_id=1, source_target_pairs={{0,16},{16,0},{1,17},{17,1},{2,18},{18,2},{3,19},{19,3},{4,20},{20... | collective-permute-start | bytes 18874376 | tf_op jit(solution)/shard_map/ppermute | solution.py:207
  450.2 37.8 %collective-permute-start.18 = (bf16[256,3072]{1,0:T(8,128)(2,1)}, bf16[256,3072]{1,0:T(8,128)(2,1)}, u32[]{:S(2)}, u32[]{:S(2)}) collective-permute-start(bf16[256,3072]{1,0:T(8,128)(2,1)} %get-tuple-element.330), channel_id=1, source_target_pairs={{0,12},{4,8},{8,4},{12,0},{1,13},{5,9},{9,5},{13,1},{2,14},{6,10},... | collective-permute-start | bytes 4718600 | tf_op jit(solution)/shard_map/ppermute | solution.py:207
  530.7 35.8 %collective-permute-start.21 = (bf16[1024,768]{1,0:T(8,128)(2,1)S(1)}, bf16[1024,768]{1,0:T(8,128)(2,1)S(1)}, u32[]{:S(2)}, u32[]{:S(2)}) collective-permute-start(bf16[1024,768]{1,0:T(8,128)(2,1)S(1)} %get-tuple-element.290), channel_id=1, source_target_pairs={{0,8},{4,12},{8,0},{12,4},{1,9},{5,13},{9,1},{13,5},{2,10},{6,14},... | collective-permute-start | bytes 4718600 | tf_op jit(solution)/shard_map/ppermute | solution.py:207
  532.2 35.4 %collective-permute-start.20 = (bf16[1024,768]{1,0:T(8,128)(2,1)S(1)}, bf16[1024,768]{1,0:T(8,128)(2,1)S(1)}, u32[]{:S(2)}, u32[]{:S(2)}) collective-permute-start(bf16[1024,768]{1,0:T(8,128)(2,1)S(1)} %get-tuple-element.291), channel_id=1, source_target_pairs={{0,4},{4,0},{8,12},{12,8},{1,5},{5,1},{9,13},{13,9},{2,6},{6,2},{1... | collective-permute-start | bytes 4718600 | tf_op jit(solution)/shard_map/ppermute | solution.py:207
  570.7 68.6 %collective-permute-start.23 = (bf16[512,768]{1,0:T(8,128)(2,1)}, bf16[512,768]{1,0:T(8,128)(2,1)}, u32[]{:S(2)}, u32[]{:S(2)}) collective-permute-start(bf16[512,768]{1,0:T(8,128)(2,1)} %slice.456), channel_id=1, source_target_pairs={{0,8},{4,12},{8,0},{12,4},{1,9},{5,13},{9,1},{13,5},{2,10},{6,14},... | collective-permute-start | bytes 2359304 | tf_op jit(solution)/shard_map/ppermute | solution.py:207
  572.2 88.8 %collective-permute-start.24 = (bf16[512,768]{1,0:T(8,128)(2,1)}, bf16[512,768]{1,0:T(8,128)(2,1)}, u32[]{:S(2)}, u32[]{:S(2)}) collective-permute-start(bf16[512,768]{1,0:T(8,128)(2,1)} %slice.458), channel_id=1, source_target_pairs={{0,4},{4,0},{8,12},{12,8},{1,5},{5,1},{9,13},{13,9},{2,6},{6,2},{1... | collective-permute-start | bytes 2359304 | tf_op jit(solution)/shard_map/ppermute | solution.py:207
  594.8 35.8 %collective-permute-start.28 = (bf16[256,768]{1,0:T(8,128)(2,1)}, bf16[256,768]{1,0:T(8,128)(2,1)}, u32[]{:S(2)}, u32[]{:S(2)}) collective-permute-start(bf16[256,768]{1,0:T(8,128)(2,1)} %fusion.56), channel_id=1, source_target_pairs={{0,4},{4,0},{8,12},{12,8},{1,5},{5,1},{9,13},{13,9},{2,6},{6,2},{1... | collective-permute-start | bytes 1179656 | tf_op jit(solution)/shard_map/ppermute | solution.py:207
  596.3 37.7 %collective-permute-start.29 = (bf16[256,768]{1,0:T(8,128)(2,1)}, bf16[256,768]{1,0:T(8,128)(2,1)}, u32[]{:S(2)}, u32[]{:S(2)}) collective-permute-start(bf16[256,768]{1,0:T(8,128)(2,1)} %fusion.56), channel_id=1, source_target_pairs={{0,8},{4,12},{8,0},{12,4},{1,9},{5,13},{9,1},{13,5},{2,10},{6,14},... | collective-permute-start | bytes 1179656 | tf_op jit(solution)/shard_map/ppermute | solution.py:207
  597.8 39.5 %collective-permute-start.30 = (bf16[256,768]{1,0:T(8,128)(2,1)}, bf16[256,768]{1,0:T(8,128)(2,1)}, u32[]{:S(2)}, u32[]{:S(2)}) collective-permute-start(bf16[256,768]{1,0:T(8,128)(2,1)} %fusion.56), channel_id=1, source_target_pairs={{0,12},{4,8},{8,4},{12,0},{1,13},{5,9},{9,5},{13,1},{2,14},{6,10},... | collective-permute-start | bytes 1179656 | tf_op jit(solution)/shard_map/ppermute | solution.py:207
  630.6 66.1 %collective-permute-start.25 = (bf16[256,1536]{1,0:T(8,128)(2,1)}, bf16[256,1536]{1,0:T(8,128)(2,1)S(1)}, u32[]{:S(2)}, u32[]{:S(2)}) collective-permute-start(bf16[256,1536]{1,0:T(8,128)(2,1)} %get-tuple-element.310), channel_id=1, source_target_pairs={{0,4},{4,0},{8,12},{12,8},{1,5},{5,1},{9,13},{13,9},{2,6},{6,2},{1... | collective-permute-start | bytes 2359304 | tf_op jit(solution)/shard_map/ppermute | solution.py:207
  633.9 63.1 %collective-permute-start.26 = (bf16[256,1536]{1,0:T(8,128)(2,1)}, bf16[256,1536]{1,0:T(8,128)(2,1)S(1)}, u32[]{:S(2)}, u32[]{:S(2)}) collective-permute-start(bf16[256,1536]{1,0:T(8,128)(2,1)} %get-tuple-element.309), channel_id=1, source_target_pairs={{0,8},{4,12},{8,0},{12,4},{1,9},{5,13},{9,1},{13,5},{2,10},{6,14},... | collective-permute-start | bytes 2359304 | tf_op jit(solution)/shard_map/ppermute | solution.py:207
  639.3 57.8 %collective-permute-start.27 = (bf16[256,1536]{1,0:T(8,128)(2,1)}, bf16[256,1536]{1,0:T(8,128)(2,1)S(1)}, u32[]{:S(2)}, u32[]{:S(2)}) collective-permute-start(bf16[256,1536]{1,0:T(8,128)(2,1)} %get-tuple-element.308), channel_id=1, source_target_pairs={{0,12},{4,8},{8,4},{12,0},{1,13},{5,9},{9,5},{13,1},{2,14},{6,10},... | collective-permute-start | bytes 2359304 | tf_op jit(solution)/shard_map/ppermute | solution.py:207
  901.6 145.7 %collective-permute-start.34 = (bf16[192,3072]{1,0:T(8,128)(2,1)}, bf16[192,3072]{1,0:T(8,128)(2,1)}, u32[]{:S(2)}, u32[]{:S(2)}) collective-permute-start(bf16[192,3072]{1,0:T(8,128)(2,1)} %concatenate.205), channel_id=1, source_target_pairs={{0,4},{4,0},{8,12},{12,8},{1,5},{5,1},{9,13},{13,9},{2,6},{6,2},{1... | collective-permute-start | bytes 3538952 | tf_op jit(solution)/shard_map/ppermute | solution.py:207
  902.7 144.7 %collective-permute-start.35 = (bf16[192,3072]{1,0:T(8,128)(2,1)}, bf16[192,3072]{1,0:T(8,128)(2,1)}, u32[]{:S(2)}, u32[]{:S(2)}) collective-permute-start(bf16[192,3072]{1,0:T(8,128)(2,1)} %concatenate.205), channel_id=1, source_target_pairs={{0,8},{4,12},{8,0},{12,4},{1,9},{5,13},{9,1},{13,5},{2,10},{6,14},... | collective-permute-start | bytes 3538952 | tf_op jit(solution)/shard_map/ppermute | solution.py:207
  903.7 143.7 %collective-permute-start.36 = (bf16[192,3072]{1,0:T(8,128)(2,1)}, bf16[192,3072]{1,0:T(8,128)(2,1)}, u32[]{:S(2)}, u32[]{:S(2)}) collective-permute-start(bf16[192,3072]{1,0:T(8,128)(2,1)} %concatenate.205), channel_id=1, source_target_pairs={{0,12},{4,8},{8,4},{12,0},{1,13},{5,9},{9,5},{13,1},{2,14},{6,10},... | collective-permute-start | bytes 3538952 | tf_op jit(solution)/shard_map/ppermute | solution.py:207
  (142 other events, 2140.2 us)

commit v4 on v3

--- a/solution.py
+++ b/solution.py
@@ -612,15 +612,6 @@
     a1 = put(rows_all.at[s, i, early], rows_all.at[s, i, early], to_x)
     b1 = put(rows_all.at[s, i, late], rows_all.at[s, i, late], to_y)
     core = [put(rows_all.at[s, i], rows_all.at[s, i], to_core)]
-    if paired:
-        for copy in fetched:
-            copy.wait()
-        for m in range(n):
-            passed[m].wait_recv()
-            held = totals[m][...].astype(WIDE) + extras[m][...].astype(WIDE)
-            totals[m][...] = held.astype(LOW)
-            reduce.append(put(totals[m], slots[m].at[1], {"fsdp": planes - 1 - z}))
-            reduce.append(put(part_of(m, partner), slots[m].at[0], {"fsdp": partner}))
     take(*head1)
     block = head_a(x, 0, 2 * piece)
     ha = put(block, block, to_x)
@@ -634,6 +625,15 @@
     for who, span in ((xn, early), (yn, late)):
         block = rows_all.at[s, who, span]
         core.append(put(block, block, to_core))
+    if paired:
+        for copy in fetched:
+            copy.wait()
+        for m in range(n):
+            passed[m].wait_recv()
+            held = totals[m][...].astype(WIDE) + extras[m][...].astype(WIDE)
+            totals[m][...] = held.astype(LOW)
+            reduce.append(put(totals[m], slots[m].at[1], {"fsdp": planes - 1 - z}))
+            reduce.append(put(part_of(m, partner), slots[m].at[0], {"fsdp": partner}))
     take(ha, hb)
     block = head.at[pl.ds(pl.multiple_of(s * 2 * side, 16), 2 * side)]
     core.append(put(block, block, to_core))
@@ -673,19 +673,20 @@
     return result[0], result[1], result[2:]
 
 
-VOCAB_BLOCK = 400
+def block_of(vocab_rows):
+    return 800 if vocab_rows % 800 == 0 else 400
 
 
 def chunk_of(lists):
     return 32 if lists <= 64 else 16
 
 
-def start_chunks(lists, length, step, steps, starts, rows_hbm, buffer, sem):
+def start_chunks(lists, length, stride, step, steps, starts, rows_hbm, buffer, sem):
     chunk = chunk_of(lists)
 
     def one(k, carry):
         at = jnp.minimum(starts[k * steps + step] // 16 * 16, length - chunk)
-        src = rows_hbm.at[pl.ds(pl.multiple_of(k * length + at, 16), chunk)]
+        src = rows_hbm.at[pl.ds(pl.multiple_of(k * stride + at, 16), chunk)]
         pltpu.make_async_copy(src, buffer.at[pl.ds(pl.multiple_of(k * chunk, 16), chunk)], sem).start()
         return carry
 
@@ -698,18 +699,20 @@
     chunk = chunk_of(lists)
     slot = step % 2
     spare = buffers.at[2]
+    width = grad.shape[0]
+    stride = rows_hbm.shape[0] // lists
 
     @pl.when(step == 0)
     def _():
-        start_chunks(lists, length, 0, steps, starts, rows_hbm, buffers.at[0], sems.at[0])
+        start_chunks(lists, length, stride, 0, steps, starts, rows_hbm, buffers.at[0], sems.at[0])
 
     @pl.when(step + 1 < steps)
     def _():
-        start_chunks(lists, length, step + 1, steps, starts, rows_hbm, buffers.at[1 - slot], sems.at[1 - slot])
+        start_chunks(lists, length, stride, step + 1, steps, starts, rows_hbm, buffers.at[1 - slot], sems.at[1 - slot])
 
     pltpu.make_async_copy(buffers.at[slot], buffers.at[slot], sems.at[slot]).wait()
-    lanes = lax.broadcasted_iota(jnp.int32, (chunk, VOCAB_BLOCK), 1) + bases[step]
-    within = lax.broadcasted_iota(jnp.int32, (chunk, VOCAB_BLOCK), 0)
+    lanes = lax.broadcasted_iota(jnp.int32, (chunk, width), 1) + bases[step]
+    within = lax.broadcasted_iota(jnp.int32, (chunk, width), 0)
 
     def mark(shifted):
         def one(k, carry):
@@ -722,7 +725,7 @@
 
         lax.fori_loop(0, lists, one, 0)
 
-    down = lax.broadcasted_iota(jnp.int32, (VOCAB_BLOCK, lists * chunk), 0) + bases[step]
+    down = lax.broadcasted_iota(jnp.int32, (width, lists * chunk), 0) + bases[step]
     wide_hot[...] = (down == near_ref[0]).astype(WIDE).astype(LOW)
     grad[...] = jnp.dot(wide_hot[...], buffers[slot], preferred_element_type=WIDE)
 
@@ -732,7 +735,7 @@
         def one(k, inner):
             begin = starts[k * steps + step] // 16 * 16 + p * chunk
             at = jnp.minimum(begin, length - chunk)
-            src = rows_hbm.at[pl.ds(pl.multiple_of(k * length + at, 16), chunk)]
+            src = rows_hbm.at[pl.ds(pl.multiple_of(k * stride + at, 16), chunk)]
             pltpu.make_async_copy(
                 src, spare.at[pl.ds(pl.multiple_of(k * chunk, 16), chunk)], sems.at[2]
             ).start()
@@ -773,47 +776,53 @@
     low[...] = weight.astype(LOW)
 
 
-def table_scratch(lists):
+def table_scratch(lists, width):
     chunk = chunk_of(lists)
     return [
         pltpu.VMEM((3, lists * chunk, D), LOW),
-        pltpu.VMEM((lists * chunk, VOCAB_BLOCK), LOW),
-        pltpu.VMEM((VOCAB_BLOCK, lists * chunk), LOW),
-        pltpu.VMEM((VOCAB_BLOCK, D), WIDE),
+        pltpu.VMEM((lists * chunk, width), LOW),
+        pltpu.VMEM((width, lists * chunk), LOW),
+        pltpu.VMEM((width, D), WIDE),
         pltpu.SemaphoreType.DMA((3,)),
     ]
 
 
-def chunk_scalars(ids_sorted, bases):
+def chunk_scalars(ids_sorted, bases, width):
     chunk = chunk_of(ids_sorted.shape[0])
     edges = bases[None, :, None]
     starts = jnp.sum((ids_sorted[:, None, :] < edges).astype(jnp.int32), axis=-1)
-    ends = jnp.sum((ids_sorted[:, None, :] < edges + VOCAB_BLOCK).astype(jnp.int32), axis=-1)
+    ends = jnp.sum((ids_sorted[:, None, :] < edges + width).astype(jnp.int32), axis=-1)
     passes = jnp.max((ends - starts // 16 * 16 + chunk - 1) // chunk, axis=0)
     lists, length = ids_sorted.shape
     groups = length // 16
     begin = (starts // 16).T
     at = jnp.minimum(begin, groups - chunk // 16)
     by_group = ids_sorted.reshape(lists, groups, 16).transpose(1, 0, 2).reshape(groups, -1)
+    widen = jnp.arange(lists * 16)[None, :] // 16 == jnp.arange(lists)[:, None]
+    both = jnp.concatenate([at, begin], axis=0).astype(LOW)
+    both = jnp.dot(both, widen.astype(LOW), preferred_element_type=WIDE).astype(jnp.int32)
+    both = lax.optimization_barrier(both)
+    steps = begin.shape[0]
     pieces = []
     for k in range(chunk // 16):
-        wanted = jnp.repeat(at + k, 16, axis=1)
+        wanted = both[:steps] + k
         found = jnp.zeros(wanted.shape, jnp.int32)
         for g in range(groups):
             found = jnp.where(wanted == g, by_group[g][None], found)
-        found = jnp.where(wanted >= jnp.repeat(begin, 16, axis=1), found, -(1 << 30))
-        pieces.append(found.reshape(-1, lists, 16))
+        found = jnp.where(wanted >= both[steps:], found, -(1 << 30))
+        pieces.append(lax.optimization_barrier(found).reshape(-1, lists, 16))
     near = jnp.stack(pieces, axis=2).reshape(begin.shape[0], 1, -1)
     return starts.reshape(-1), jnp.maximum(passes, 1), near
 
 
 def table_square(ids_sorted, ids_column, rows_flat, rank, ranks, vocab_rows):
     lists, length = ids_sorted.shape
-    total = vocab_rows // VOCAB_BLOCK
+    width = block_of(vocab_rows)
+    total = vocab_rows // width
     steps = -(-total // ranks)
     blocks = rank + ranks * jnp.arange(steps, dtype=jnp.int32)
-    bases = blocks * VOCAB_BLOCK
-    starts, passes, near = chunk_scalars(ids_sorted, bases)
+    bases = blocks * width
+    starts, passes, near = chunk_scalars(ids_sorted, bases, width)
     passes = jnp.where(blocks < total, passes, 0)
     out = pl.pallas_call(
         functools.partial(table_square_kernel, lists, length, steps),
@@ -828,7 +837,7 @@
                 pl.BlockSpec((1, 1, near.shape[2]), lambda g, *_: (g, 0, 0)),
             ],
             out_specs=pl.BlockSpec((8, D), lambda g, *_: (0, 0)),
-            scratch_shapes=table_scratch(lists),
+            scratch_shapes=table_scratch(lists, width),
         ),
         out_shape=jax.ShapeDtypeStruct((8, D), WIDE),
         compiler_params=pltpu.CompilerParams(vmem_limit_bytes=56 << 20),
@@ -840,10 +849,11 @@
 def table_adam(ids_sorted, ids_column, rows_flat, clip_scale, table, mom, sec, rate, decay):
     lists, length = ids_sorted.shape
     vocab_rows = table.shape[0]
-    steps = vocab_rows // VOCAB_BLOCK
-    bases = jnp.arange(steps, dtype=jnp.int32) * VOCAB_BLOCK
-    starts, passes, near = chunk_scalars(ids_sorted, bases)
-    block = pl.BlockSpec((VOCAB_BLOCK, D), lambda g, *_: (g, 0))
+    width = block_of(vocab_rows)
+    steps = vocab_rows // width
+    bases = jnp.arange(steps, dtype=jnp.int32) * width
+    starts, passes, near = chunk_scalars(ids_sorted, bases, width)
+    block = pl.BlockSpec((width, D), lambda g, *_: (g, 0))
     wide = jax.ShapeDtypeStruct(table.shape, WIDE)
     return pl.pallas_call(
         functools.partial(table_adam_kernel, lists, length, steps, rate, decay),
@@ -861,12 +871,12 @@
                 block,
             ],
             out_specs=[block] * 4,
-            scratch_shapes=table_scratch(lists),
+            scratch_shapes=table_scratch(lists, width),
         ),
         out_shape=[wide, wide, wide, jax.ShapeDtypeStruct(table.shape, LOW)],
         compiler_params=pltpu.CompilerParams(vmem_limit_bytes=60 << 20),
         cost_estimate=pl.CostEstimate(
-            flops=steps * 2 * VOCAB_BLOCK * lists * chunk_of(lists) * D,
+            flops=steps * 2 * width * lists * chunk_of(lists) * D,
             bytes_accessed=table.size * 26,
             transcendentals=table.size,
         ),
@@ -874,7 +884,7 @@
     )(starts, passes, bases, clip_scale.reshape(1), rows_flat, ids_column, near, table, mom, sec)
 
 
-HEAD_BLOCK = 512
+HEAD_BLOCK = 800
 
 
 def head_adam_kernel(rate, decay, clip, grad, w, m, v, w_new, m_new, v_new, low):
@@ -1096,13 +1106,17 @@
     ]
     parts = [part.astype(LOW) for part in parts]
     gains_grad = jnp.stack([gain_parts[0], gain_parts[1], head_gain_grad])
-    gains_grad = jnp.sum(small_gather([gains_grad], ("dp", "fsdp"), 4)[0], axis=0)
-    gains_grad = lax.dynamic_slice_in_dim(gains_grad, me * (D // planes), D // planes, 1)
 
     row_grads = jnp.where(first, grad_inputs.astype(LOW), sent.astype(LOW))
     row_grads = jnp.dot(arrange, row_grads, preferred_element_type=WIDE).astype(LOW)
+    row_grads = jnp.concatenate(
+        [row_grads, gains_grad.astype(LOW), jnp.zeros((13, D), LOW)], axis=0
+    )
     rows_all, grad_head, slots = exchange(planes, row_grads, (piece_a, piece_b), parts)
     rows_flat = rows_all.reshape(-1, D)
+    gains_grad = pick(rows_all[:, :, :, tokens : tokens + 3], lax.axis_index("section"))
+    gains_grad = jnp.sum(gains_grad.astype(WIDE), axis=(0, 1))
+    gains_grad = lax.dynamic_slice_in_dim(gains_grad, me * (D // planes), D // planes, 1)
     ids_column = sorted_ids.reshape(-1, 1)
 
     def square(item):
@@ -1119,7 +1133,7 @@
         squares = squares + square(item)
     squares = squares + square(gains_grad) / replicas
     totals = jnp.stack([squares, loss_part / planes])[:, None] * jnp.ones((1, 128), WIDE)
-    totals = jnp.sum(small_gather([totals], ("section", "dp", "fsdp"), 5)[0], axis=0)[:, 0]
+    totals = jnp.sum(small_gather([totals], ("section", "dp", "fsdp"), 4)[0], axis=0)[:, 0]
     grad_norm = jnp.sqrt(totals[0])
     loss_total = totals[1]
     clip_scale = CLIP / jnp.maximum(grad_norm, CLIP)

time: 1090 us -> 1060 us (0.972)
  waiting for transfers between devices: 111 us -> 151 us
  other arithmetic: 147 us -> 109 us
  Pallas kernels: 565 us -> 530 us
    ppermute x12, waiting for transfers between devices: 18.3 us -> 56.5 us  [shift(): lax.ppermute(block, axis, [(i, (i + distance) % count) for i in range(cou...]
    select_n x5, other arithmetic: 31.1 us -> 0.74 us  [the longest x1 0.58 us: chunk_scalars(): widen = jnp.arange(lists * 16)[None, :] // 16 == jnp.arange(lists)[:, None]]
    pallas_call x3 -> x2, Pallas kernels: 41 us -> 29.6 us  [small_gather(): pl.pallas_call(functools.partial(small_gather_kernel, axes, sizes), out_s...]
    unnamed x270 -> x234, local copies, waits for them, and re-layouts: 26.8 us -> 21.1 us
  transfers between devices with their start and end apart: 37 -> 37, of which waited for: 9 -> 12; matrix products, arithmetic and copies ran while one was open for 19% -> 16% of each run, Pallas kernels for 33% -> 27%
where the time goes in v4:
time: 1060 us; the launch traced here: 1050 us
  Pallas kernels  530 us (50%)
  waiting for transfers between devices  151 us (14%)
  local copies, waits for them, and re-layouts  125 us (12%)
  other arithmetic  109 us (10%)
  matrix products  88 us (8%)
  starting transfers between devices  34.9 us (3%)
  between operations  13.2 us (1%)
    pallas_call x1, Pallas kernels, gather_weights(): pl.pallas_call(functools.partial(weights_kernel, planes, units, rows), ou...  154 us
    pallas_call x1, Pallas kernels, exchange(): pl.pallas_call(functools.partial(exchange_kernel, planes), out_shape=outs...  133 us
    ppermute x25, waiting for transfers between devices, swap(): return lax.ppermute(block, axis, [(i, i ^ mask) for i in range(count)])  94.7 us
    pallas_call x1, Pallas kernels, table_adam(): pl.pallas_call(functools.partial(table_adam_kernel, lists, length, steps,...  68.1 us
    pallas_call x1, Pallas kernels, head_adam(): pl.pallas_call(functools.partial(head_adam_kernel, rate, decay), grid_spe...  56.6 us
    ppermute x12, waiting for transfers between devices, shift(): lax.ppermute(block, axis, [(i, (i + distance) % count) for i in range(cou...  56.5 us
    pallas_call x1, Pallas kernels, head_grads(): pl.pallas_call(functools.partial(head_grads_kernel, vocab), grid_spec=plt...  53.8 us
    dot_general x8, matrix products, contract_cols(): lax.dot_general(left, right, (((1,), (1,)), ((), ())), preferred_element_...  34.3 us
  transfers between devices with their start and end apart: 37, of which 12 were waited for; matrix products, arithmetic and copies ran while one was open for 16% of the time, Pallas kernels for 27%

profile of v4, /device:TPU:0, one launch (start us, length us, event | category | flops | bytes accessed | tf_op | source)
XLA Modules:
  0.0 1051.7 jit_solution(759269397083003542)
XLA Ops:
  3.3 11.9 %small_gather_3.1 = (s32[16,2,256]{2,1,0:T(2,128)}, f32[16,3,192]{2,1,0:T(4,128)}) custom-call(s32[2,256]{1,0:T(2,128)} %pad_add_fusion.4.refs_0_, f32[3,192]{1,0:T(4,128)} %bitcast.406), custom_call_target="tpu_custom_call" | custom-call | tf_op jit(solution)/shard_map/small_gather_3/pallas_call | solution.py:962
  16.1 13.6 %gather_fusion = bf16[1024,768]{1,0:T(8,128)(2,1)} fusion(f32[8000,768]{1,0:T(8,128)} %w.1, s32[1024]{0:T(1024)S(1)} %broadcast_clamp_fusion), kind=kCustom, calls=%fused_computation | custom fusion | bytes 3149824 | tf_op jit(solution)/shard_map/jit(_take)/gather | solution.py:1019
  47.1 154.2 %gather_weights.1 = (bf16[768,2304]{1,0:T(8,128)(2,1)}, bf16[768,768]{1,0:T(8,128)(2,1)}, bf16[768,6144]{1,0:T(8,128)(2,1)}, bf16[3072,768]{1,0:T(8,128)(2,1)}) custom-call(bf16[192,2304]{1,0:T(8,128)(2,1)} %convert_bitcast_fusion.2.refs_0_, bf16[192,768]{1,0:T(8,128)(2,1)} %convert_bitcast_fusion.3.refs_1_, bf16[192,6144]{1,0:T(8,128)(2,1)} %convert_bitcast_fusion.refs_2_, ...), custom_call_target="tpu_custom_call" | custom-call | tf_op jit(solution)/shard_map/gather_weights/pallas_call | solution.py:147
  245.6 6.2 fusion.195
  276.2 24.4 %collective-permute-done.7 = bf16[256,768]{1,0:T(8,128)(2,1)S(1)} collective-permute-done((bf16[256,768]{1,0:T(8,128)(2,1)}, bf16[256,768]{1,0:T(8,128)(2,1)S(1)}, u32[]{:S(2)}, u32[]{:S(2)}) %collective-permute-start.7) | collective-permute-done | bytes 393248 | tf_op jit(solution)/shard_map/ppermute | solution.py:202
  301.8 27.0 %head_stats.1 = f32[8,1024]{1,0:T(8,128)S(1)} custom-call(f32[8000,768]{1,0:T(8,128)} %bitcast.353, bf16[1024,768]{1,0:T(8,128)(2,1)S(1)} %pad_maximum_fusion.1.rows_ref, s32[1,1024]{1,0:T(1,128)S(1)} %and_select_fusion.target_ref), custom_call_target="tpu_custom_call" | custom-call | flops 12582912000 | bytes 24576000 | tf_op jit(solution)/shard_map/head_stats/pallas_call | solution.py:413
  349.5 53.8 %head_grads.1 = (bf16[8192,768]{1,0:T(8,128)(2,1)}, f32[768,1024]{1,0:T(8,128)}) custom-call(s32[16]{0:T(128)} %stack.161.order, f32[8000,768]{1,0:T(8,128)} %bitcast.354, bf16[1024,768]{1,0:T(8,128)(2,1)} %copy-done.3, s32[1,1024]{1,0:T(1,128)} %copy-done.6, f32[1,1024]{1,0:T(1,128)} %bitcast.412, f32[1,1024]{1,0:T(1,128)} %bitcast.411), custom_call_target="tpu_custom_call" | custom-call | flops 37748736000 | bytes 49152000 | tf_op jit(solution)/shard_map/head_grads/pallas_call | solution.py:453
  403.3 6.0 slice.461
  429.8 8.6 collective-permute-done.14
  439.3 15.0 %collective-permute-done.13 = bf16[256,768]{1,0:T(8,128)(2,1)S(1)} collective-permute-done((bf16[256,768]{1,0:T(8,128)(2,1)}, bf16[256,768]{1,0:T(8,128)(2,1)S(1)}, u32[]{:S(2)}, u32[]{:S(2)}) %collective-permute-start.13) | collective-permute-done | bytes 393248 | tf_op jit(solution)/shard_map/ppermute | solution.py:202
  470.1 19.8 %collective-permute-done.18 = bf16[256,3072]{1,0:T(8,128)(2,1)} collective-permute-done((bf16[256,3072]{1,0:T(8,128)(2,1)}, bf16[256,3072]{1,0:T(8,128)(2,1)}, u32[]{:S(2)}, u32[]{:S(2)}) %collective-permute-start.18) | collective-permute-done | bytes 1572896 | tf_op jit(solution)/shard_map/ppermute | solution.py:207
  494.0 9.1 add_convert_fusion
  503.1 9.3 fusion.162
  512.5 9.0 multiply_reduce_fusion.12
  539.7 26.5 %collective-permute-done.21 = bf16[1024,768]{1,0:T(8,128)(2,1)S(1)} collective-permute-done((bf16[1024,768]{1,0:T(8,128)(2,1)S(1)}, bf16[1024,768]{1,0:T(8,128)(2,1)S(1)}, u32[]{:S(2)}, u32[]{:S(2)}) %collective-permute-start.21) | collective-permute-done | bytes 1572896 | tf_op jit(solution)/shard_map/ppermute | solution.py:207
  572.7 7.6 fusion.161
  626.9 19.4 %collective-permute-done.31 = bf16[256,768]{0,1:T(8,128)(2,1)S(1)} collective-permute-done((bf16[256,768]{0,1:T(8,128)(2,1)S(1)}, bf16[256,768]{0,1:T(8,128)(2,1)S(1)}, u32[]{:S(2)}, u32[]{:S(2)}) %collective-permute-start.31) | collective-permute-done | bytes 393248 | tf_op jit(solution)/shard_map/ppermute | solution.py:207
  650.8 27.2 %collective-permute-done.32 = bf16[256,768]{0,1:T(8,128)(2,1)S(1)} collective-permute-done((bf16[256,768]{0,1:T(8,128)(2,1)S(1)}, bf16[256,768]{0,1:T(8,128)(2,1)S(1)}, u32[]{:S(2)}, u32[]{:S(2)}) %collective-permute-start.32) | collective-permute-done | bytes 393248 | tf_op jit(solution)/shard_map/ppermute | solution.py:207
  701.0 132.7 %exchange.1 = (bf16[2,4,4,272,768]{4,3,2,1,0:T(8,128)(2,1)S(1)}, bf16[8192,768]{1,0:T(8,128)(2,1)S(1)}, bf16[2,192,1536]{2,1,0:T(8,128)(2,1)S(1)}, bf16[2,192,76...) custom-call(bf16[272,768]{1,0:T(8,128)(2,1)S(1)} %concatenate.213.rows_ref, ...), custom_call_target="tpu_custom_call" | custom-call | tf_op jit(solution)/shard_map/exchange/pallas_call | solution.py:659
  844.9 8.3 table_square.1
  866.1 17.7 %small_gather_4.1 = f32[32,2,128]{2,1,0:T(2,128)} custom-call(f32[2,128]{1,0:T(2,128)} %mul.1635.refs_0_), custom_call_target="tpu_custom_call" | custom-call | tf_op jit(solution)/shard_map/small_gather_4/pallas_call | solution.py:962
  891.8 56.6 %head_adam.1 = (f32[8000,768]{1,0:T(8,128)}, f32[8000,768]{1,0:T(8,128)}, f32[8000,768]{1,0:T(8,128)}, bf16[8000,768]{1,0:T(8,128)(2,1)}) custom-call(f32[1]{0:T(128)} %bitcast.93.clip, bf16[8192,768]{1,0:T(8,128)(2,1)} %copy-done.1, f32[8000,768]{1,0:T(8,128)} %bitcast.355, f32[8000,768]{1,0:T(8,128)} %bitcast.356, f32[8000,768]{1,0:T(8,128)} %bitcast.357), custom_call_target="tpu_custom_call" | custom-call | flops 122880000 | bytes 172032000 | tf_op jit(solution)/shard_map/head_adam/pallas_call | solution.py:903
  949.6 68.1 %table_adam.1 = (f32[8000,768]{1,0:T(8,128)}, f32[8000,768]{1,0:T(8,128)}, f32[8000,768]{1,0:T(8,128)}, bf16[8000,768]{1,0:T(8,128)(2,1)}) custom-call(s32[320]{0:T(512)} %reshape.1171.starts, s32[10]{0:T(128)} %broadcast_maximum_fusion.passes, s32[10]{0:T(128)} %get-tuple-element.456.bases, f32[1]{0:T(128)} %bitcast.93.clip, bf16[8704,768]{1,0:T(8,128)(2,1)} %bitcast.338, ...), custom_call_target="tpu_custom_call" | custom-call | flops 12582912000 | bytes 159744000 | tf_op jit(solution)/shard_map/table_adam/pallas_call | solution.py:858
  1032.1 11.0 %fusion.165 = (bf16[1,192,6144]{2,1,0:T(8,128)(2,1)}, f32[1,192,6144]{2,1,0:T(8,128)}, f32[1,192,6144]{2,1,0:T(8,128)}, f32[1,192,6144]{2,1,0:T(8,128)}) fusion(f32[1,192,6144]{2,1,0:T(8,128)} %param.39, f32[]{:T(128)} %div.415, bf16[1,192,1536]{2,1,0:T(8,128)(2,1)S(1)} %get-tuple-element.323, bf16[1,192,1536]{2,1,0:T(8,128)(2,1)S(1)} %get-tuple-element.322, ...), kind=kLoop, calls=%fused_computation.513 | loop fusion | flops 29491200 | bytes 33030148 | tf_op jit(solution)/shard_map/convert_element_type | solution.py:1191
  (605 shorter events, 295.4 us)
Async XLA Ops:
  32.5 169.1 %collective-permute-start.2 = (bf16[256,768]{1,0:T(8,128)(2,1)}, bf16[256,768]{1,0:T(8,128)(2,1)}, u32[]{:S(2)}, u32[]{:S(2)}) collective-permute-start(bf16[256,768]{1,0:T(8,128)(2,1)} %get-tuple-element.352), channel_id=1, source_target_pairs={{0,1},{1,2},{2,3},{3,0},{4,5},{5,6},{6,7},{7,4},{8,9},{9,10},{10,1... | collective-permute-start | bytes 1179656 | tf_op jit(solution)/shard_map/ppermute | solution.py:202
  33.6 167.9 %collective-permute-start.1 = (bf16[256,768]{1,0:T(8,128)(2,1)}, bf16[256,768]{1,0:T(8,128)(2,1)}, u32[]{:S(2)}, u32[]{:S(2)}) collective-permute-start(bf16[256,768]{1,0:T(8,128)(2,1)} %get-tuple-element.353), channel_id=1, source_target_pairs={{0,2},{1,3},{2,0},{3,1},{4,6},{5,7},{6,4},{7,5},{8,10},{9,11},{10,... | collective-permute-start | bytes 1179656 | tf_op jit(solution)/shard_map/ppermute | solution.py:202
  36.1 165.5 %collective-permute-start = (bf16[256,768]{1,0:T(8,128)(2,1)}, bf16[256,768]{1,0:T(8,128)(2,1)}, u32[]{:S(2)}, u32[]{:S(2)}) collective-permute-start(bf16[256,768]{1,0:T(8,128)(2,1)} %get-tuple-element.351), channel_id=1, source_target_pairs={{0,3},{1,0},{2,1},{3,2},{4,7},{5,4},{6,5},{7,6},{8,11},{9,8},{10,9... | collective-permute-start | bytes 1179656 | tf_op jit(solution)/shard_map/ppermute | solution.py:202
  224.5 37.6 %collective-permute-start.5 = (bf16[256,768]{1,0:T(8,128)(2,1)}, bf16[256,768]{1,0:T(8,128)(2,1)}, u32[]{:S(2)}, u32[]{:S(2)}) collective-permute-start(bf16[256,768]{1,0:T(8,128)(2,1)} %get-tuple-element.306), channel_id=1, source_target_pairs={{0,16},{16,0},{1,17},{17,1},{2,18},{18,2},{3,19},{19,3},{4,20},{20... | collective-permute-start | bytes 1179656 | tf_op jit(solution)/shard_map/ppermute | solution.py:207
  264.5 36.1 %collective-permute-start.7 = (bf16[256,768]{1,0:T(8,128)(2,1)}, bf16[256,768]{1,0:T(8,128)(2,1)S(1)}, u32[]{:S(2)}, u32[]{:S(2)}) collective-permute-start(bf16[256,768]{1,0:T(8,128)(2,1)} %multiply_convert_fusion.3), channel_id=1, source_target_pairs={{0,2},{1,3},{2,0},{3,1},{4,6},{5,7},{6,4},{7,5},{8,10},{9,11},{10,... | collective-permute-start | bytes 1179656 | tf_op jit(solution)/shard_map/ppermute | solution.py:202
  265.7 34.8 %collective-permute-start.6 = (bf16[256,768]{1,0:T(8,128)(2,1)}, bf16[256,768]{1,0:T(8,128)(2,1)S(1)}, u32[]{:S(2)}, u32[]{:S(2)}) collective-permute-start(bf16[256,768]{1,0:T(8,128)(2,1)} %multiply_convert_fusion.3), channel_id=1, source_target_pairs={{0,1},{1,2},{2,3},{3,0},{4,5},{5,6},{6,7},{7,4},{8,9},{9,10},{10,1... | collective-permute-start | bytes 1179656 | tf_op jit(solution)/shard_map/ppermute | solution.py:202
  409.3 84.7 %collective-permute-start.19 = (bf16[4096,768]{1,0:T(8,128)(2,1)}, bf16[4096,768]{1,0:T(8,128)(2,1)}, u32[]{:S(2)}, u32[]{:S(2)}) collective-permute-start(bf16[4096,768]{1,0:T(8,128)(2,1)} %slice.461), channel_id=1, source_target_pairs={{0,16},{16,0},{1,17},{17,1},{2,18},{18,2},{3,19},{19,3},{4,20},{20... | collective-permute-start | bytes 18874376 | tf_op jit(solution)/shard_map/ppermute | solution.py:207
  411.8 52.9 %collective-permute-start.16 = (bf16[256,3072]{1,0:T(8,128)(2,1)}, bf16[256,3072]{1,0:T(8,128)(2,1)}, u32[]{:S(2)}, u32[]{:S(2)}) collective-permute-start(bf16[256,3072]{1,0:T(8,128)(2,1)} %get-tuple-element.359), channel_id=1, source_target_pairs={{0,4},{4,0},{8,12},{12,8},{1,5},{5,1},{9,13},{13,9},{2,6},{6,2},{1... | collective-permute-start | bytes 4718600 | tf_op jit(solution)/shard_map/ppermute | solution.py:207
  413.6 53.8 %collective-permute-start.17 = (bf16[256,3072]{1,0:T(8,128)(2,1)}, bf16[256,3072]{1,0:T(8,128)(2,1)}, u32[]{:S(2)}, u32[]{:S(2)}) collective-permute-start(bf16[256,3072]{1,0:T(8,128)(2,1)} %get-tuple-element.360), channel_id=1, source_target_pairs={{0,8},{4,12},{8,0},{12,4},{1,9},{5,13},{9,1},{13,5},{2,10},{6,14},... | collective-permute-start | bytes 4718600 | tf_op jit(solution)/shard_map/ppermute | solution.py:207
  424.5 29.8 %collective-permute-start.13 = (bf16[256,768]{1,0:T(8,128)(2,1)}, bf16[256,768]{1,0:T(8,128)(2,1)S(1)}, u32[]{:S(2)}, u32[]{:S(2)}) collective-permute-start(bf16[256,768]{1,0:T(8,128)(2,1)} %get-tuple-element.350), channel_id=1, source_target_pairs={{0,2},{1,3},{2,0},{3,1},{4,6},{5,7},{6,4},{7,5},{8,10},{9,11},{10,... | collective-permute-start | bytes 1179656 | tf_op jit(solution)/shard_map/ppermute | solution.py:202
  454.3 35.6 %collective-permute-start.18 = (bf16[256,3072]{1,0:T(8,128)(2,1)}, bf16[256,3072]{1,0:T(8,128)(2,1)}, u32[]{:S(2)}, u32[]{:S(2)}) collective-permute-start(bf16[256,3072]{1,0:T(8,128)(2,1)} %get-tuple-element.358), channel_id=1, source_target_pairs={{0,12},{4,8},{8,4},{12,0},{1,13},{5,9},{9,5},{13,1},{2,14},{6,10},... | collective-permute-start | bytes 4718600 | tf_op jit(solution)/shard_map/ppermute | solution.py:207
  464.7 27.9 %collective-permute-start.15 = (bf16[256,768]{1,0:T(8,128)(2,1)S(1)}, bf16[256,768]{1,0:T(8,128)(2,1)S(1)}, u32[]{:S(2)}, u32[]{:S(2)}) collective-permute-start(bf16[256,768]{1,0:T(8,128)(2,1)S(1)} %fusion.44), channel_id=1, source_target_pairs={{0,16},{16,0},{1,17},{17,1},{2,18},{18,2},{3,19},{19,3},{4,20},{20... | collective-permute-start | bytes 1179656 | tf_op jit(solution)/shard_map/ppermute | solution.py:207
  532.7 33.5 %collective-permute-start.21 = (bf16[1024,768]{1,0:T(8,128)(2,1)S(1)}, bf16[1024,768]{1,0:T(8,128)(2,1)S(1)}, u32[]{:S(2)}, u32[]{:S(2)}) collective-permute-start(bf16[1024,768]{1,0:T(8,128)(2,1)S(1)} %get-tuple-element.318), channel_id=1, source_target_pairs={{0,8},{4,12},{8,0},{12,4},{1,9},{5,13},{9,1},{13,5},{2,10},{6,14},... | collective-permute-start | bytes 4718600 | tf_op jit(solution)/shard_map/ppermute | solution.py:207
  534.3 33.2 %collective-permute-start.20 = (bf16[1024,768]{1,0:T(8,128)(2,1)S(1)}, bf16[1024,768]{1,0:T(8,128)(2,1)S(1)}, u32[]{:S(2)}, u32[]{:S(2)}) collective-permute-start(bf16[1024,768]{1,0:T(8,128)(2,1)S(1)} %get-tuple-element.319), channel_id=1, source_target_pairs={{0,4},{4,0},{8,12},{12,8},{1,5},{5,1},{9,13},{13,9},{2,6},{6,2},{1... | collective-permute-start | bytes 4718600 | tf_op jit(solution)/shard_map/ppermute | solution.py:207
  569.9 54.0 %collective-permute-start.23 = (bf16[512,768]{1,0:T(8,128)(2,1)}, bf16[512,768]{1,0:T(8,128)(2,1)}, u32[]{:S(2)}, u32[]{:S(2)}) collective-permute-start(bf16[512,768]{1,0:T(8,128)(2,1)} %slice.475), channel_id=1, source_target_pairs={{0,8},{4,12},{8,0},{12,4},{1,9},{5,13},{9,1},{13,5},{2,10},{6,14},... | collective-permute-start | bytes 2359304 | tf_op jit(solution)/shard_map/ppermute | solution.py:207
  571.4 76.3 %collective-permute-start.24 = (bf16[512,768]{1,0:T(8,128)(2,1)}, bf16[512,768]{1,0:T(8,128)(2,1)}, u32[]{:S(2)}, u32[]{:S(2)}) collective-permute-start(bf16[512,768]{1,0:T(8,128)(2,1)} %slice.477), channel_id=1, source_target_pairs={{0,4},{4,0},{8,12},{12,8},{1,5},{5,1},{9,13},{13,9},{2,6},{6,2},{1... | collective-permute-start | bytes 2359304 | tf_op jit(solution)/shard_map/ppermute | solution.py:207
  617.2 75.5 %collective-permute-start.25 = (bf16[256,1536]{1,0:T(8,128)(2,1)}, bf16[256,1536]{1,0:T(8,128)(2,1)}, u32[]{:S(2)}, u32[]{:S(2)}) collective-permute-start(bf16[256,1536]{1,0:T(8,128)(2,1)} %get-tuple-element.338), channel_id=1, source_target_pairs={{0,4},{4,0},{8,12},{12,8},{1,5},{5,1},{9,13},{13,9},{2,6},{6,2},{1... | collective-permute-start | bytes 2359304 | tf_op jit(solution)/shard_map/ppermute | solution.py:207
  619.8 74.3 %collective-permute-start.26 = (bf16[256,1536]{1,0:T(8,128)(2,1)}, bf16[256,1536]{1,0:T(8,128)(2,1)}, u32[]{:S(2)}, u32[]{:S(2)}) collective-permute-start(bf16[256,1536]{1,0:T(8,128)(2,1)} %get-tuple-element.337), channel_id=1, source_target_pairs={{0,8},{4,12},{8,0},{12,4},{1,9},{5,13},{9,1},{13,5},{2,10},{6,14},... | collective-permute-start | bytes 2359304 | tf_op jit(solution)/shard_map/ppermute | solution.py:207
  623.9 71.4 %collective-permute-start.27 = (bf16[256,1536]{1,0:T(8,128)(2,1)}, bf16[256,1536]{1,0:T(8,128)(2,1)}, u32[]{:S(2)}, u32[]{:S(2)}) collective-permute-start(bf16[256,1536]{1,0:T(8,128)(2,1)} %get-tuple-element.336), channel_id=1, source_target_pairs={{0,12},{4,8},{8,4},{12,0},{1,13},{5,9},{9,5},{13,1},{2,14},{6,10},... | collective-permute-start | bytes 2359304 | tf_op jit(solution)/shard_map/ppermute | solution.py:207
  646.3 31.6 %collective-permute-start.32 = (bf16[256,768]{0,1:T(8,128)(2,1)S(1)}, bf16[256,768]{0,1:T(8,128)(2,1)S(1)}, u32[]{:S(2)}, u32[]{:S(2)}) collective-permute-start(bf16[256,768]{0,1:T(8,128)(2,1)S(1)} %pad_maximum_fusion.17), channel_id=1, source_target_pairs={{0,8},{4,12},{8,0},{12,4},{1,9},{5,13},{9,1},{13,5},{2,10},{6,14},... | collective-permute-start | bytes 1179656 | tf_op jit(solution)/shard_map/ppermute | solution.py:207
  647.7 33.2 %collective-permute-start.33 = (bf16[256,768]{0,1:T(8,128)(2,1)S(1)}, bf16[256,768]{0,1:T(8,128)(2,1)S(1)}, u32[]{:S(2)}, u32[]{:S(2)}) collective-permute-start(bf16[256,768]{0,1:T(8,128)(2,1)S(1)} %pad_maximum_fusion.18), channel_id=1, source_target_pairs={{0,12},{4,8},{8,4},{12,0},{1,13},{5,9},{9,5},{13,1},{2,14},{6,10},... | collective-permute-start | bytes 1179656 | tf_op jit(solution)/shard_map/ppermute | solution.py:207
  887.6 130.1 %collective-permute-start.34 = (bf16[192,3072]{1,0:T(8,128)(2,1)}, bf16[192,3072]{1,0:T(8,128)(2,1)}, u32[]{:S(2)}, u32[]{:S(2)}) collective-permute-start(bf16[192,3072]{1,0:T(8,128)(2,1)} %concatenate.220), channel_id=1, source_target_pairs={{0,4},{4,0},{8,12},{12,8},{1,5},{5,1},{9,13},{13,9},{2,6},{6,2},{1... | collective-permute-start | bytes 3538952 | tf_op jit(solution)/shard_map/ppermute | solution.py:207
  889.0 128.7 %collective-permute-start.35 = (bf16[192,3072]{1,0:T(8,128)(2,1)}, bf16[192,3072]{1,0:T(8,128)(2,1)}, u32[]{:S(2)}, u32[]{:S(2)}) collective-permute-start(bf16[192,3072]{1,0:T(8,128)(2,1)} %concatenate.220), channel_id=1, source_target_pairs={{0,8},{4,12},{8,0},{12,4},{1,9},{5,13},{9,1},{13,5},{2,10},{6,14},... | collective-permute-start | bytes 3538952 | tf_op jit(solution)/shard_map/ppermute | solution.py:207
  889.7 128.1 %collective-permute-start.36 = (bf16[192,3072]{1,0:T(8,128)(2,1)}, bf16[192,3072]{1,0:T(8,128)(2,1)}, u32[]{:S(2)}, u32[]{:S(2)}) collective-permute-start(bf16[192,3072]{1,0:T(8,128)(2,1)} %concatenate.220), channel_id=1, source_target_pairs={{0,12},{4,8},{8,4},{12,0},{1,13},{5,9},{9,5},{13,1},{2,14},{6,10},... | collective-permute-start | bytes 3538952 | tf_op jit(solution)/shard_map/ppermute | solution.py:207
  (124 other events, 1660.3 us)

commit v5 on v4

--- a/solution.py
+++ b/solution.py
@@ -970,6 +970,44 @@
     )(*blocks)
 
 
+def finish_kernel(n, me, *refs):
+    parts, slots, pieces = refs[:n], refs[n : 2 * n], refs[2 * n : 2 * n + 2]
+    shards, out = refs[2 * n + 2 : 3 * n + 2], refs[3 * n + 2]
+    total = jnp.zeros((), WIDE)
+    for m in range(n):
+        held = parts[m][...].astype(WIDE)
+        for k in range(slots[m].shape[0]):
+            held = held + slots[m][k].astype(WIDE)
+        low = held.astype(LOW)
+        shards[m][...] = low
+        held = low.astype(WIDE)
+        total = total + jnp.sum(held * held)
+    for piece in pieces:
+        held = piece[...].astype(WIDE)
+        total = total + jnp.sum(held * held)
+    out[...] = jnp.full(out.shape, total, WIDE)
+
+
+def finish(me, parts, slots, pieces):
+    blocks = [slot.shape[1:] for slot in slots]
+    whole = lambda shape: pl.BlockSpec(shape, lambda g, *_: (0,) * len(shape))
+    results = pl.pallas_call(
+        functools.partial(finish_kernel, len(parts)),
+        grid_spec=pltpu.PrefetchScalarGridSpec(
+            num_scalar_prefetch=1,
+            grid=(1,),
+            in_specs=[pl.BlockSpec(block, lambda g, me: (me[0], 0)) for block in blocks]
+            + [whole(item.shape) for item in list(slots) + list(pieces)],
+            out_specs=[whole(block) for block in blocks] + [whole((8, 128))],
+        ),
+        out_shape=[jax.ShapeDtypeStruct(block, LOW) for block in blocks]
+        + [jax.ShapeDtypeStruct((8, 128), WIDE)],
+        compiler_params=pltpu.CompilerParams(vmem_limit_bytes=40 << 20),
+        name="finish",
+    )(me.astype(jnp.int32).reshape(1), *parts, *slots, *pieces)
+    return list(results[:-1]), results[-1][0, 0]
+
+
 def per_device(
     token_ids,
     next_ids,
@@ -1081,15 +1119,15 @@
     top_grad, top_gain = norm_back(layer_out, head_gain, grad_in + sent)
     head_gain_grad = jnp.where(first, mtp_gain, top_gain)
     half = add_low(mine, swap(theirs, "section", 1))
-    top_grad, left_all, half = lax.optimization_barrier((top_grad, left_all, half))
+    top_grad, left_all = lax.optimization_barrier((top_grad, left_all))
     below, _, _ = layer_back(layer_in, layer_weights, saved, top_grad)
+    below, half = lax.optimization_barrier((below.astype(LOW), half))
     side = half.shape[0] // 2
     piece_a, piece_b = keep_half(half[:side], 1), keep_half(half[side:], 2)
-    below, piece_a, piece_b = lax.optimization_barrier((below.astype(LOW), piece_a, piece_b))
     upstream = jnp.where(first, swap(below, "section", 1).astype(WIDE), top_grad)
     grad_inputs, right, gain_parts = layer_back(layer_in, layer_weights, saved, upstream)
+    grad_inputs, piece_a, piece_b = lax.optimization_barrier((grad_inputs, piece_a, piece_b))
     piece_a, piece_b = keep_half(piece_a, 2), keep_half(piece_b, 1)
-    grad_inputs, piece_a, piece_b = lax.optimization_barrier((grad_inputs, piece_a, piece_b))
 
     grad_packed, after_low, grad_gu, upstream_low = right
     tops = spread(lambda index: upstream_low)
@@ -1119,19 +1157,10 @@
     gains_grad = lax.dynamic_slice_in_dim(gains_grad, me * (D // planes), D // planes, 1)
     ids_column = sorted_ids.reshape(-1, 1)
 
-    def square(item):
-        wide = item.astype(WIDE)
-        return jnp.sum(wide * wide)
-
-    shards = []
-    for part, slot in zip(parts, slots):
-        mine = pick(part.reshape((planes,) + slot.shape[1:]), me).astype(WIDE)
-        shards.append((mine + jnp.sum(slot.astype(WIDE), axis=0)).astype(LOW))
+    shards, shard_squares = finish(me, parts, slots, (piece_a, piece_b))
     group = lax.axis_index("section") * replicas + lax.axis_index("dp")
     squares = table_square(sorted_ids, ids_column, rows_flat, group, 2 * replicas, vocab_rows)
-    for item in shards + [piece_a, piece_b]:
-        squares = squares + square(item)
-    squares = squares + square(gains_grad) / replicas
+    squares = squares + shard_squares + jnp.sum(gains_grad * gains_grad) / replicas
     totals = jnp.stack([squares, loss_part / planes])[:, None] * jnp.ones((1, 128), WIDE)
     totals = jnp.sum(small_gather([totals], ("section", "dp", "fsdp"), 4)[0], axis=0)[:, 0]
     grad_norm = jnp.sqrt(totals[0])

time: 1060 us -> 1010 us (0.953)
  waiting for transfers between devices: 151 us -> 107 us
  matrix products: 88 us -> 77.2 us
    ppermute x12, waiting for transfers between devices: 56.5 us -> 25.5 us  [shift(): lax.ppermute(block, axis, [(i, (i + distance) % count) for i in range(cou...]
    ppermute x25, waiting for transfers between devices: 94.7 us -> 81.7 us  [swap(): return lax.ppermute(block, axis, [(i, i ^ mask) for i in range(count)])]
    reduce_sum x11 -> x1, other arithmetic: 11.7 us -> 0.67 us  [per_device(): jnp.sum(gains_grad * gains_grad) / replicas]
    unnamed x234 -> x304, local copies, waits for them, and re-layouts: 21.1 us -> 25.8 us
  transfers between devices with their start and end apart: 37 -> 37, of which waited for: 12 -> 12; matrix products, arithmetic and copies ran while one was open for 16% -> 20% of each run, Pallas kernels for 27% -> 33%
where the time goes in v5:
time: 1010 us; the launch traced here: 1000 us
  Pallas kernels  528 us (52%)
  local copies, waits for them, and re-layouts  132 us (13%)
  other arithmetic  108 us (11%)
  waiting for transfers between devices  107 us (11%)
  matrix products  77.2 us (8%)
  starting transfers between devices  37.7 us (4%)
    pallas_call x1, Pallas kernels, gather_weights(): pl.pallas_call(functools.partial(weights_kernel, planes, units, rows), ou...  153 us
    pallas_call x1, Pallas kernels, exchange(): pl.pallas_call(functools.partial(exchange_kernel, planes), out_shape=outs...  131 us
    ppermute x25, waiting for transfers between devices, swap(): return lax.ppermute(block, axis, [(i, i ^ mask) for i in range(count)])  81.7 us
    pallas_call x1, Pallas kernels, table_adam(): pl.pallas_call(functools.partial(table_adam_kernel, lists, length, steps,...  68.1 us
    pallas_call x1, Pallas kernels, head_adam(): pl.pallas_call(functools.partial(head_adam_kernel, rate, decay), grid_spe...  56.6 us
    pallas_call x1, Pallas kernels, head_grads(): pl.pallas_call(functools.partial(head_grads_kernel, vocab), grid_spec=plt...  53.4 us
    dot_general x8, matrix products, contract_cols(): lax.dot_general(left, right, (((1,), (1,)), ((), ())), preferred_element_...  29.8 us
    pallas_call x2, Pallas kernels, small_gather(): pl.pallas_call(functools.partial(small_gather_kernel, axes, sizes), out_s...  29.2 us
  transfers between devices with their start and end apart: 37, of which 12 were waited for; matrix products, arithmetic and copies ran while one was open for 20% of the time, Pallas kernels for 33%

profile of v5, /device:TPU:0, one launch (start us, length us, event | category | flops | bytes accessed | tf_op | source)
XLA Modules:
  0.0 1000.4 jit_solution(15751897976411842886)
XLA Ops:
  3.3 11.9 %small_gather_3.1 = (s32[16,2,256]{2,1,0:T(2,128)}, f32[16,3,192]{2,1,0:T(4,128)}) custom-call(s32[2,256]{1,0:T(2,128)} %pad_add_fusion.4.refs_0_, f32[3,192]{1,0:T(4,128)} %bitcast.389), custom_call_target="tpu_custom_call" | custom-call | tf_op jit(solution)/shard_map/small_gather_3/pallas_call | solution.py:962
  16.1 13.6 %gather_fusion = bf16[1024,768]{1,0:T(8,128)(2,1)} fusion(f32[8000,768]{1,0:T(8,128)} %w.1, s32[1024]{0:T(1024)S(1)} %broadcast_clamp_fusion), kind=kCustom, calls=%fused_computation | custom fusion | bytes 3149824 | tf_op jit(solution)/shard_map/jit(_take)/gather | solution.py:1057
  48.5 152.9 %gather_weights.1 = (bf16[768,2304]{1,0:T(8,128)(2,1)}, bf16[768,768]{1,0:T(8,128)(2,1)}, bf16[768,6144]{1,0:T(8,128)(2,1)}, bf16[3072,768]{1,0:T(8,128)(2,1)}) custom-call(bf16[192,2304]{1,0:T(8,128)(2,1)} %convert_bitcast_fusion.2.refs_0_, bf16[192,768]{1,0:T(8,128)(2,1)} %convert_bitcast_fusion.3.refs_1_, bf16[192,6144]{1,0:T(8,128)(2,1)} %convert_bitcast_fusion.refs_2_, ...), custom_call_target="tpu_custom_call" | custom-call | tf_op jit(solution)/shard_map/gather_weights/pallas_call | solution.py:147
  284.7 14.8 %collective-permute-done.7 = bf16[256,768]{1,0:T(8,128)(2,1)} collective-permute-done((bf16[256,768]{1,0:T(8,128)(2,1)}, bf16[256,768]{1,0:T(8,128)(2,1)}, u32[]{:S(2)}, u32[]{:S(2)}) %collective-permute-start.7) | collective-permute-done | bytes 393248 | tf_op jit(solution)/shard_map/ppermute | solution.py:202
  301.0 27.0 %head_stats.1 = f32[8,1024]{1,0:T(8,128)S(1)} custom-call(f32[8000,768]{1,0:T(8,128)} %bitcast.333, bf16[1024,768]{1,0:T(8,128)(2,1)S(1)} %pad_maximum_fusion.1.rows_ref, s32[1,1024]{1,0:T(1,128)S(1)} %and_select_fusion.target_ref), custom_call_target="tpu_custom_call" | custom-call | flops 12582912000 | bytes 24576000 | tf_op jit(solution)/shard_map/head_stats/pallas_call | solution.py:413
  353.3 53.4 %head_grads.1 = (bf16[8192,768]{1,0:T(8,128)(2,1)}, f32[768,1024]{1,0:T(8,128)}) custom-call(s32[16]{0:T(128)} %stack.161.order, f32[8000,768]{1,0:T(8,128)} %bitcast.334, bf16[1024,768]{1,0:T(8,128)(2,1)} %copy-done.10, s32[1,1024]{1,0:T(1,128)} %copy-done.15, f32[1,1024]{1,0:T(1,128)} %bitcast.394, f32[1,1024]{1,0:T(1,128)} %bitcast.393), custom_call_target="tpu_custom_call" | custom-call | flops 37748736000 | bytes 49152000 | tf_op jit(solution)/shard_map/head_grads/pallas_call | solution.py:453
  420.4 7.2 collective-permute-done.14
  429.7 5.9 slice.468
  452.5 7.1 collective-permute-done.18
  463.4 8.4 fusion.158
  471.9 6.4 multiply_reduce_fusion.9
  493.0 9.0 add_convert_fusion
  508.9 6.6 fusion.157
  554.5 6.0 collective-permute-done.29
  574.1 40.7 %collective-permute-done.33 = bf16[256,768]{0,1:T(8,128)(2,1)S(1)} collective-permute-done((bf16[256,768]{0,1:T(8,128)(2,1)S(1)}, bf16[256,768]{0,1:T(8,128)(2,1)S(1)}, u32[]{:S(2)}, u32[]{:S(2)}) %collective-permute-start.33) | collective-permute-done | bytes 393248 | tf_op jit(solution)/shard_map/ppermute | solution.py:207
  620.0 14.5 %collective-permute-done.27 = bf16[256,1536]{1,0:T(8,128)(2,1)S(1)} collective-permute-done((bf16[256,1536]{1,0:T(8,128)(2,1)S(1)}, bf16[256,1536]{1,0:T(8,128)(2,1)S(1)}, u32[]{:S(2)}, u32[]{:S(2)}) %collective-permute-start.27) | collective-permute-done | bytes 786464 | tf_op jit(solution)/shard_map/ppermute | solution.py:207
  646.5 9.6 collective-permute-done.23
  660.7 130.9 %exchange.1 = (bf16[2,4,4,272,768]{4,3,2,1,0:T(8,128)(2,1)S(1)}, bf16[8192,768]{1,0:T(8,128)(2,1)S(1)}, bf16[2,192,1536]{2,1,0:T(8,128)(2,1)S(1)}, bf16[2,192,76...) custom-call(bf16[272,768]{1,0:T(8,128)(2,1)S(1)} %concatenate.213.rows_ref, ...), custom_call_target="tpu_custom_call" | custom-call | tf_op jit(solution)/shard_map/exchange/pallas_call | solution.py:659
  803.0 8.4 table_square.1
  814.8 17.3 %small_gather_4.1 = f32[32,2,128]{2,1,0:T(2,128)} custom-call(f32[2,128]{1,0:T(2,128)} %mul.1611.refs_0_), custom_call_target="tpu_custom_call" | custom-call | tf_op jit(solution)/shard_map/small_gather_4/pallas_call | solution.py:962
  840.1 56.6 %head_adam.1 = (f32[8000,768]{1,0:T(8,128)}, f32[8000,768]{1,0:T(8,128)}, f32[8000,768]{1,0:T(8,128)}, bf16[8000,768]{1,0:T(8,128)(2,1)}) custom-call(f32[1]{0:T(128)} %bitcast.87.clip, bf16[8192,768]{1,0:T(8,128)(2,1)} %copy-done.1, f32[8000,768]{1,0:T(8,128)} %bitcast.335, f32[8000,768]{1,0:T(8,128)} %bitcast.336, f32[8000,768]{1,0:T(8,128)} %bitcast.337), custom_call_target="tpu_custom_call" | custom-call | flops 122880000 | bytes 172032000 | tf_op jit(solution)/shard_map/head_adam/pallas_call | solution.py:903
  897.9 68.1 %table_adam.1 = (f32[8000,768]{1,0:T(8,128)}, f32[8000,768]{1,0:T(8,128)}, f32[8000,768]{1,0:T(8,128)}, bf16[8000,768]{1,0:T(8,128)(2,1)}) custom-call(s32[320]{0:T(512)} %reshape.1151.starts, s32[10]{0:T(128)} %broadcast_maximum_fusion.passes, s32[10]{0:T(128)} %copy-done.124, f32[1]{0:T(128)} %bitcast.87.clip, bf16[8704,768]{1,0:T(8,128)(2,1)} %bitcast.320, ...), custom_call_target="tpu_custom_call" | custom-call | flops 12582912000 | bytes 159744000 | tf_op jit(solution)/shard_map/table_adam/pallas_call | solution.py:858
  970.4 6.0 fusion.165
  981.1 11.0 %fusion.161 = (bf16[1,192,6144]{2,1,0:T(8,128)(2,1)}, f32[1,192,6144]{2,1,0:T(8,128)}, f32[1,192,6144]{2,1,0:T(8,128)}, f32[1,192,6144]{2,1,0:T(8,128)}) fusion(f32[1,192,6144]{2,1,0:T(8,128)} %param.39, f32[]{:T(128)} %div.415, bf16[1,192,1536]{2,1,0:T(8,128)(2,1)S(1)} %get-tuple-element.321, bf16[1,192,1536]{2,1,0:T(8,128)(2,1)S(1)} %get-tuple-element.320, ...), kind=kLoop, calls=%fused_computation.495 | loop fusion | flops 29491200 | bytes 33030148 | tf_op jit(solution)/shard_map/convert_element_type | solution.py:1220
  (669 shorter events, 297.1 us)
Async XLA Ops:
  32.5 169.6 %collective-permute-start.2 = (bf16[256,768]{1,0:T(8,128)(2,1)}, bf16[256,768]{1,0:T(8,128)(2,1)}, u32[]{:S(2)}, u32[]{:S(2)}) collective-permute-start(bf16[256,768]{1,0:T(8,128)(2,1)} %get-tuple-element.350), channel_id=1, source_target_pairs={{0,1},{1,2},{2,3},{3,0},{4,5},{5,6},{6,7},{7,4},{8,9},{9,10},{10,1... | collective-permute-start | bytes 1179656 | tf_op jit(solution)/shard_map/ppermute | solution.py:202
  33.7 168.4 %collective-permute-start.1 = (bf16[256,768]{1,0:T(8,128)(2,1)}, bf16[256,768]{1,0:T(8,128)(2,1)}, u32[]{:S(2)}, u32[]{:S(2)}) collective-permute-start(bf16[256,768]{1,0:T(8,128)(2,1)} %get-tuple-element.351), channel_id=1, source_target_pairs={{0,2},{1,3},{2,0},{3,1},{4,6},{5,7},{6,4},{7,5},{8,10},{9,11},{10,... | collective-permute-start | bytes 1179656 | tf_op jit(solution)/shard_map/ppermute | solution.py:202
  36.1 166.0 %collective-permute-start = (bf16[256,768]{1,0:T(8,128)(2,1)}, bf16[256,768]{1,0:T(8,128)(2,1)}, u32[]{:S(2)}, u32[]{:S(2)}) collective-permute-start(bf16[256,768]{1,0:T(8,128)(2,1)} %get-tuple-element.349), channel_id=1, source_target_pairs={{0,3},{1,0},{2,1},{3,2},{4,7},{5,4},{6,5},{7,6},{8,11},{9,8},{10,9... | collective-permute-start | bytes 1179656 | tf_op jit(solution)/shard_map/ppermute | solution.py:202
  229.5 31.6 %collective-permute-start.5 = (bf16[256,768]{1,0:T(8,128)(2,1)}, bf16[256,768]{1,0:T(8,128)(2,1)}, u32[]{:S(2)}, u32[]{:S(2)}) collective-permute-start(bf16[256,768]{1,0:T(8,128)(2,1)} %get-tuple-element.304), channel_id=1, source_target_pairs={{0,16},{16,0},{1,17},{17,1},{2,18},{18,2},{3,19},{19,3},{4,20},{20... | collective-permute-start | bytes 1179656 | tf_op jit(solution)/shard_map/ppermute | solution.py:207
  263.5 36.0 %collective-permute-start.7 = (bf16[256,768]{1,0:T(8,128)(2,1)}, bf16[256,768]{1,0:T(8,128)(2,1)}, u32[]{:S(2)}, u32[]{:S(2)}) collective-permute-start(bf16[256,768]{1,0:T(8,128)(2,1)} %multiply_convert_fusion.3), channel_id=1, source_target_pairs={{0,2},{1,3},{2,0},{3,1},{4,6},{5,7},{6,4},{7,5},{8,10},{9,11},{10,... | collective-permute-start | bytes 1179656 | tf_op jit(solution)/shard_map/ppermute | solution.py:202
  264.7 34.8 %collective-permute-start.6 = (bf16[256,768]{1,0:T(8,128)(2,1)}, bf16[256,768]{1,0:T(8,128)(2,1)}, u32[]{:S(2)}, u32[]{:S(2)}) collective-permute-start(bf16[256,768]{1,0:T(8,128)(2,1)} %multiply_convert_fusion.3), channel_id=1, source_target_pairs={{0,1},{1,2},{2,3},{3,0},{4,5},{5,6},{6,7},{7,4},{8,9},{9,10},{10,1... | collective-permute-start | bytes 1179656 | tf_op jit(solution)/shard_map/ppermute | solution.py:202
  332.4 114.6 %collective-permute-start.16 = (bf16[256,3072]{1,0:T(8,128)(2,1)}, bf16[256,3072]{1,0:T(8,128)(2,1)}, u32[]{:S(2)}, u32[]{:S(2)}) collective-permute-start(bf16[256,3072]{1,0:T(8,128)(2,1)} %get-tuple-element.357), channel_id=1, source_target_pairs={{0,4},{4,0},{8,12},{12,8},{1,5},{5,1},{9,13},{13,9},{2,6},{6,2},{1... | collective-permute-start | bytes 4718600 | tf_op jit(solution)/shard_map/ppermute | solution.py:207
  333.8 116.0 %collective-permute-start.17 = (bf16[256,3072]{1,0:T(8,128)(2,1)}, bf16[256,3072]{1,0:T(8,128)(2,1)}, u32[]{:S(2)}, u32[]{:S(2)}) collective-permute-start(bf16[256,3072]{1,0:T(8,128)(2,1)} %get-tuple-element.358), channel_id=1, source_target_pairs={{0,8},{4,12},{8,0},{12,4},{1,9},{5,13},{9,1},{13,5},{2,10},{6,14},... | collective-permute-start | bytes 4718600 | tf_op jit(solution)/shard_map/ppermute | solution.py:207
  413.6 30.1 %collective-permute-start.13 = (bf16[256,768]{1,0:T(8,128)(2,1)}, bf16[256,768]{1,0:T(8,128)(2,1)}, u32[]{:S(2)}, u32[]{:S(2)}) collective-permute-start(bf16[256,768]{1,0:T(8,128)(2,1)} %get-tuple-element.348), channel_id=1, source_target_pairs={{0,2},{1,3},{2,0},{3,1},{4,6},{5,7},{6,4},{7,5},{8,10},{9,11},{10,... | collective-permute-start | bytes 1179656 | tf_op jit(solution)/shard_map/ppermute | solution.py:202
  414.5 29.2 %collective-permute-start.12 = (bf16[256,768]{1,0:T(8,128)(2,1)}, bf16[256,768]{1,0:T(8,128)(2,1)}, u32[]{:S(2)}, u32[]{:S(2)}) collective-permute-start(bf16[256,768]{1,0:T(8,128)(2,1)} %get-tuple-element.346), channel_id=1, source_target_pairs={{0,3},{1,0},{2,1},{3,2},{4,7},{5,4},{6,5},{7,6},{8,11},{9,8},{10,9... | collective-permute-start | bytes 1179656 | tf_op jit(solution)/shard_map/ppermute | solution.py:202
  427.6 31.9 %collective-permute-start.18 = (bf16[256,3072]{1,0:T(8,128)(2,1)}, bf16[256,3072]{1,0:T(8,128)(2,1)}, u32[]{:S(2)}, u32[]{:S(2)}) collective-permute-start(bf16[256,3072]{1,0:T(8,128)(2,1)} %get-tuple-element.356), channel_id=1, source_target_pairs={{0,12},{4,8},{8,4},{12,0},{1,13},{5,9},{9,5},{13,1},{2,14},{6,10},... | collective-permute-start | bytes 4718600 | tf_op jit(solution)/shard_map/ppermute | solution.py:207
  443.7 49.3 %collective-permute-start.19 = (bf16[4096,768]{1,0:T(8,128)(2,1)}, bf16[4096,768]{1,0:T(8,128)(2,1)}, u32[]{:S(2)}, u32[]{:S(2)}) collective-permute-start(bf16[4096,768]{1,0:T(8,128)(2,1)} %slice.468), channel_id=1, source_target_pairs={{0,16},{16,0},{1,17},{17,1},{2,18},{18,2},{3,19},{19,3},{4,20},{20... | collective-permute-start | bytes 18874376 | tf_op jit(solution)/shard_map/ppermute | solution.py:207
  506.6 128.0 %collective-permute-start.22 = (bf16[1024,768]{1,0:T(8,128)(2,1)}, bf16[1024,768]{1,0:T(8,128)(2,1)}, u32[]{:S(2)}, u32[]{:S(2)}) collective-permute-start(bf16[1024,768]{1,0:T(8,128)(2,1)} %get-tuple-element.316), channel_id=1, source_target_pairs={{0,8},{4,12},{8,0},{12,4},{1,9},{5,13},{9,1},{13,5},{2,10},{6,14},... | collective-permute-start | bytes 4718600 | tf_op jit(solution)/shard_map/ppermute | solution.py:207
  527.4 23.2 %collective-permute-start.28 = (bf16[256,768]{1,0:T(8,128)(2,1)}, bf16[256,768]{1,0:T(8,128)(2,1)}, u32[]{:S(2)}, u32[]{:S(2)}) collective-permute-start(bf16[256,768]{1,0:T(8,128)(2,1)} %fusion.54), channel_id=1, source_target_pairs={{0,4},{4,0},{8,12},{12,8},{1,5},{5,1},{9,13},{13,9},{2,6},{6,2},{1... | collective-permute-start | bytes 1179656 | tf_op jit(solution)/shard_map/ppermute | solution.py:207
  527.6 32.9 %collective-permute-start.29 = (bf16[256,768]{1,0:T(8,128)(2,1)}, bf16[256,768]{1,0:T(8,128)(2,1)}, u32[]{:S(2)}, u32[]{:S(2)}) collective-permute-start(bf16[256,768]{1,0:T(8,128)(2,1)} %fusion.54), channel_id=1, source_target_pairs={{0,8},{4,12},{8,0},{12,4},{1,9},{5,13},{9,1},{13,5},{2,10},{6,14},... | collective-permute-start | bytes 1179656 | tf_op jit(solution)/shard_map/ppermute | solution.py:207
  528.4 33.6 %collective-permute-start.30 = (bf16[256,768]{1,0:T(8,128)(2,1)}, bf16[256,768]{1,0:T(8,128)(2,1)}, u32[]{:S(2)}, u32[]{:S(2)}) collective-permute-start(bf16[256,768]{1,0:T(8,128)(2,1)} %fusion.54), channel_id=1, source_target_pairs={{0,12},{4,8},{8,4},{12,0},{1,13},{5,9},{9,5},{13,1},{2,14},{6,10},... | collective-permute-start | bytes 1179656 | tf_op jit(solution)/shard_map/ppermute | solution.py:207
  540.7 23.6 %collective-permute-start.31 = (bf16[256,768]{0,1:T(8,128)(2,1)}, bf16[256,768]{0,1:T(8,128)(2,1)}, u32[]{:S(2)}, u32[]{:S(2)}) collective-permute-start(bf16[256,768]{0,1:T(8,128)(2,1)} %pad_maximum_fusion.16), channel_id=1, source_target_pairs={{0,4},{4,0},{8,12},{12,8},{1,5},{5,1},{9,13},{13,9},{2,6},{6,2},{1... | collective-permute-start | bytes 1179656 | tf_op jit(solution)/shard_map/ppermute | solution.py:207
  551.7 82.8 %collective-permute-start.21 = (bf16[1024,768]{1,0:T(8,128)(2,1)S(1)}, bf16[1024,768]{1,0:T(8,128)(2,1)S(1)}, u32[]{:S(2)}, u32[]{:S(2)}) collective-permute-start(bf16[1024,768]{1,0:T(8,128)(2,1)S(1)} %copy-done.62), channel_id=1, source_target_pairs={{0,4},{4,0},{8,12},{12,8},{1,5},{5,1},{9,13},{13,9},{2,6},{6,2},{1... | collective-permute-start | bytes 4718600 | tf_op jit(solution)/shard_map/ppermute | solution.py:207
  560.5 59.3 %collective-permute-start.25 = (bf16[256,1536]{1,0:T(8,128)(2,1)S(1)}, bf16[256,1536]{1,0:T(8,128)(2,1)S(1)}, u32[]{:S(2)}, u32[]{:S(2)}) collective-permute-start(bf16[256,1536]{1,0:T(8,128)(2,1)S(1)} %copy-done.66), channel_id=1, source_target_pairs={{0,4},{4,0},{8,12},{12,8},{1,5},{5,1},{9,13},{13,9},{2,6},{6,2},{1... | collective-permute-start | bytes 2359304 | tf_op jit(solution)/shard_map/ppermute | solution.py:207
  564.3 50.5 %collective-permute-start.33 = (bf16[256,768]{0,1:T(8,128)(2,1)S(1)}, bf16[256,768]{0,1:T(8,128)(2,1)S(1)}, u32[]{:S(2)}, u32[]{:S(2)}) collective-permute-start(bf16[256,768]{0,1:T(8,128)(2,1)S(1)} %pad_maximum_fusion.18), channel_id=1, source_target_pairs={{0,12},{4,8},{8,4},{12,0},{1,13},{5,9},{9,5},{13,1},{2,14},{6,10},... | collective-permute-start | bytes 1179656 | tf_op jit(solution)/shard_map/ppermute | solution.py:207
  572.7 47.2 %collective-permute-start.26 = (bf16[256,1536]{1,0:T(8,128)(2,1)S(1)}, bf16[256,1536]{1,0:T(8,128)(2,1)S(1)}, u32[]{:S(2)}, u32[]{:S(2)}) collective-permute-start(bf16[256,1536]{1,0:T(8,128)(2,1)S(1)} %copy-done.65), channel_id=1, source_target_pairs={{0,8},{4,12},{8,0},{12,4},{1,9},{5,13},{9,1},{13,5},{2,10},{6,14},... | collective-permute-start | bytes 2359304 | tf_op jit(solution)/shard_map/ppermute | solution.py:207
  835.9 130.1 %collective-permute-start.34 = (bf16[192,3072]{1,0:T(8,128)(2,1)}, bf16[192,3072]{1,0:T(8,128)(2,1)}, u32[]{:S(2)}, u32[]{:S(2)}) collective-permute-start(bf16[192,3072]{1,0:T(8,128)(2,1)} %concatenate.220), channel_id=1, source_target_pairs={{0,4},{4,0},{8,12},{12,8},{1,5},{5,1},{9,13},{13,9},{2,6},{6,2},{1... | collective-permute-start | bytes 3538952 | tf_op jit(solution)/shard_map/ppermute | solution.py:207
  836.7 129.3 %collective-permute-start.35 = (bf16[192,3072]{1,0:T(8,128)(2,1)}, bf16[192,3072]{1,0:T(8,128)(2,1)}, u32[]{:S(2)}, u32[]{:S(2)}) collective-permute-start(bf16[192,3072]{1,0:T(8,128)(2,1)} %concatenate.220), channel_id=1, source_target_pairs={{0,8},{4,12},{8,0},{12,4},{1,9},{5,13},{9,1},{13,5},{2,10},{6,14},... | collective-permute-start | bytes 3538952 | tf_op jit(solution)/shard_map/ppermute | solution.py:207
  837.9 128.1 %collective-permute-start.36 = (bf16[192,3072]{1,0:T(8,128)(2,1)}, bf16[192,3072]{1,0:T(8,128)(2,1)}, u32[]{:S(2)}, u32[]{:S(2)}) collective-permute-start(bf16[192,3072]{1,0:T(8,128)(2,1)} %concatenate.220), channel_id=1, source_target_pairs={{0,12},{4,8},{8,4},{12,0},{1,13},{5,9},{9,5},{13,1},{2,14},{6,10},... | collective-permute-start | bytes 3538952 | tf_op jit(solution)/shard_map/ppermute | solution.py:207
  (159 other events, 3628.4 us)

commit v6 on v5

--- a/solution.py
+++ b/solution.py
@@ -1126,19 +1126,19 @@
     piece_a, piece_b = keep_half(half[:side], 1), keep_half(half[side:], 2)
     upstream = jnp.where(first, swap(below, "section", 1).astype(WIDE), top_grad)
     grad_inputs, right, gain_parts = layer_back(layer_in, layer_weights, saved, upstream)
-    grad_inputs, piece_a, piece_b = lax.optimization_barrier((grad_inputs, piece_a, piece_b))
+    grad_packed, after_low, grad_gu, upstream_low = right
+    after_low, piece_a, piece_b = lax.optimization_barrier((after_low, piece_a, piece_b))
     piece_a, piece_b = keep_half(piece_a, 2), keep_half(piece_b, 1)
-
-    grad_packed, after_low, grad_gu, upstream_low = right
-    tops = spread(lambda index: upstream_low)
-    early = spread(lambda index: quarter(grad_gu, index))
+    early = spread(
+        lambda index: jnp.concatenate([upstream_low, quarter(grad_gu, index)], axis=1)
+    )
     late = spread(
         lambda index: jnp.concatenate([quarter(after_low, index), quarter(grad_packed, index)], axis=1)
     )
     cut = D // SHARE
     parts = [
-        contract_rows(left_all[:, 2 * D : 3 * D], early),
-        contract_rows(left_all[:, 3 * D :], tops),
+        contract_rows(left_all[:, 2 * D : 3 * D], early[:, D:]),
+        contract_rows(left_all[:, 3 * D :], early[:, :D]),
         contract_rows(left_all[:, :D], late[:, cut:]),
         contract_rows(left_all[:, D : 2 * D], late[:, :cut]),
     ]

time: 1010 us -> 1010 us (level)
    ppermute x25 -> x22, waiting for transfers between devices: 81.7 us -> 73.8 us  [swap(): return lax.ppermute(block, axis, [(i, i ^ mask) for i in range(count)])]
    ppermute x25 -> x22, starting transfers between devices: 22.5 us -> 18.4 us  [swap(): return lax.ppermute(block, axis, [(i, i ^ mask) for i in range(count)])]
    unnamed x304 -> x288, local copies, waits for them, and re-layouts: 25.8 us -> 26.8 us
  transfers between devices with their start and end apart: 37 -> 34, of which waited for: 12 -> 10; matrix products, arithmetic and copies ran while one was open for 20% -> 21% of each run, Pallas kernels for 33% -> 33%
where the time goes in v6:
time: 1010 us; the launch traced here: 1000 us
  Pallas kernels  530 us (52%)
  local copies, waits for them, and re-layouts  142 us (14%)
  other arithmetic  106 us (10%)
  waiting for transfers between devices  99.3 us (10%)
  matrix products  80.5 us (8%)
  starting transfers between devices  33.6 us (3%)
    pallas_call x1, Pallas kernels, gather_weights(): pl.pallas_call(functools.partial(weights_kernel, planes, units, rows), ou...  153 us
    pallas_call x1, Pallas kernels, exchange(): pl.pallas_call(functools.partial(exchange_kernel, planes), out_shape=outs...  132 us
    ppermute x22, waiting for transfers between devices, swap(): return lax.ppermute(block, axis, [(i, i ^ mask) for i in range(count)])  73.8 us
    pallas_call x1, Pallas kernels, table_adam(): pl.pallas_call(functools.partial(table_adam_kernel, lists, length, steps,...  68 us
    pallas_call x1, Pallas kernels, head_adam(): pl.pallas_call(functools.partial(head_adam_kernel, rate, decay), grid_spe...  56.6 us
    pallas_call x1, Pallas kernels, head_grads(): pl.pallas_call(functools.partial(head_grads_kernel, vocab), grid_spec=plt...  53.4 us
    pallas_call x2, Pallas kernels, small_gather(): pl.pallas_call(functools.partial(small_gather_kernel, axes, sizes), out_s...  29.2 us
    dot_general x8, matrix products, contract_cols(): lax.dot_general(left, right, (((1,), (1,)), ((), ())), preferred_element_...  28 us
  transfers between devices with their start and end apart: 34, of which 10 were waited for; matrix products, arithmetic and copies ran while one was open for 21% of the time, Pallas kernels for 33%

profile of v6, /device:TPU:0, one launch (start us, length us, event | category | flops | bytes accessed | tf_op | source)
XLA Modules:
  0.0 1001.2 jit_solution(9490948304449372227)
XLA Ops:
  3.3 11.9 %small_gather_3.1 = (s32[16,2,256]{2,1,0:T(2,128)}, f32[16,3,192]{2,1,0:T(4,128)}) custom-call(s32[2,256]{1,0:T(2,128)} %pad_add_fusion.4.refs_0_, f32[3,192]{1,0:T(4,128)} %bitcast.385), custom_call_target="tpu_custom_call" | custom-call | tf_op jit(solution)/shard_map/small_gather_3/pallas_call | solution.py:962
  16.1 13.6 %gather_fusion = bf16[1024,768]{1,0:T(8,128)(2,1)} fusion(f32[8000,768]{1,0:T(8,128)} %w.1, s32[1024]{0:T(1024)S(1)} %broadcast_clamp_fusion), kind=kCustom, calls=%fused_computation | custom fusion | bytes 3149824 | tf_op jit(solution)/shard_map/jit(_take)/gather | solution.py:1057
  48.5 152.9 %gather_weights.1 = (bf16[768,2304]{1,0:T(8,128)(2,1)}, bf16[768,768]{1,0:T(8,128)(2,1)}, bf16[768,6144]{1,0:T(8,128)(2,1)}, bf16[3072,768]{1,0:T(8,128)(2,1)}) custom-call(bf16[192,2304]{1,0:T(8,128)(2,1)} %convert_bitcast_fusion.2.refs_0_, bf16[192,768]{1,0:T(8,128)(2,1)} %convert_bitcast_fusion.3.refs_1_, bf16[192,6144]{1,0:T(8,128)(2,1)} %convert_bitcast_fusion.refs_2_, ...), custom_call_target="tpu_custom_call" | custom-call | tf_op jit(solution)/shard_map/gather_weights/pallas_call | solution.py:147
  216.9 5.6 fusion.61
  284.8 14.8 %collective-permute-done.7 = bf16[256,768]{1,0:T(8,128)(2,1)} collective-permute-done((bf16[256,768]{1,0:T(8,128)(2,1)}, bf16[256,768]{1,0:T(8,128)(2,1)}, u32[]{:S(2)}, u32[]{:S(2)}) %collective-permute-start.7) | collective-permute-done | bytes 393248 | tf_op jit(solution)/shard_map/ppermute | solution.py:202
  301.1 27.0 %head_stats.1 = f32[8,1024]{1,0:T(8,128)S(1)} custom-call(f32[8000,768]{1,0:T(8,128)} %bitcast.331, bf16[1024,768]{1,0:T(8,128)(2,1)S(1)} %pad_maximum_fusion.5.rows_ref, s32[1,1024]{1,0:T(1,128)S(1)} %and_select_fusion.target_ref), custom_call_target="tpu_custom_call" | custom-call | flops 12582912000 | bytes 24576000 | tf_op jit(solution)/shard_map/head_stats/pallas_call | solution.py:413
  353.4 53.4 %head_grads.1 = (bf16[8192,768]{1,0:T(8,128)(2,1)}, f32[768,1024]{1,0:T(8,128)}) custom-call(s32[16]{0:T(128)} %stack.161.order, f32[8000,768]{1,0:T(8,128)} %bitcast.332, bf16[1024,768]{1,0:T(8,128)(2,1)} %copy-done.8, s32[1,1024]{1,0:T(1,128)} %copy-done.13, f32[1,1024]{1,0:T(1,128)} %bitcast.390, f32[1,1024]{1,0:T(1,128)} %bitcast.389), custom_call_target="tpu_custom_call" | custom-call | flops 37748736000 | bytes 49152000 | tf_op jit(solution)/shard_map/head_grads/pallas_call | solution.py:453
  420.5 7.2 collective-permute-done.14
  429.8 5.9 slice.474
  452.6 7.1 collective-permute-done.18
  463.5 8.4 fusion.166
  472.0 6.4 multiply_reduce_fusion.9
  493.3 9.0 add_convert_fusion
  549.7 21.5 %collective-permute-done.25 = bf16[256,2304]{1,0:T(8,128)(2,1)} collective-permute-done((bf16[256,2304]{1,0:T(8,128)(2,1)}, bf16[256,2304]{1,0:T(8,128)(2,1)}, u32[]{:S(2)}, u32[]{:S(2)}) %collective-permute-start.25) | collective-permute-done | bytes 1179680 | tf_op jit(solution)/shard_map/ppermute | solution.py:207
  575.8 19.8 %collective-permute-done.27 = bf16[256,2304]{1,0:T(8,128)(2,1)} collective-permute-done((bf16[256,2304]{1,0:T(8,128)(2,1)}, bf16[256,2304]{1,0:T(8,128)(2,1)}, u32[]{:S(2)}, u32[]{:S(2)}) %collective-permute-start.27) | collective-permute-done | bytes 1179680 | tf_op jit(solution)/shard_map/ppermute | solution.py:207
  625.7 18.7 %collective-permute-done.28 = bf16[256,768]{0,1:T(8,128)(2,1)S(1)} collective-permute-done((bf16[256,768]{0,1:T(8,128)(2,1)}, bf16[256,768]{0,1:T(8,128)(2,1)S(1)}, u32[]{:S(2)}, u32[]{:S(2)}) %collective-permute-start.28) | collective-permute-done | bytes 393248 | tf_op jit(solution)/shard_map/ppermute | solution.py:207
  644.5 6.4 collective-permute-done.30
  659.1 132.2 %exchange.1 = (bf16[2,4,4,272,768]{4,3,2,1,0:T(8,128)(2,1)S(1)}, bf16[8192,768]{1,0:T(8,128)(2,1)S(1)}, bf16[2,192,1536]{2,1,0:T(8,128)(2,1)S(1)}, bf16[2,192,76...) custom-call(bf16[272,768]{1,0:T(8,128)(2,1)S(1)} %concatenate.225.rows_ref, ...), custom_call_target="tpu_custom_call" | custom-call | tf_op jit(solution)/shard_map/exchange/pallas_call | solution.py:659
  803.3 8.6 table_square.1
  815.3 17.3 %small_gather_4.1 = f32[32,2,128]{2,1,0:T(2,128)} custom-call(f32[2,128]{1,0:T(2,128)} %mul.1611.refs_0_), custom_call_target="tpu_custom_call" | custom-call | tf_op jit(solution)/shard_map/small_gather_4/pallas_call | solution.py:962
  840.7 56.6 %head_adam.1 = (f32[8000,768]{1,0:T(8,128)}, f32[8000,768]{1,0:T(8,128)}, f32[8000,768]{1,0:T(8,128)}, bf16[8000,768]{1,0:T(8,128)(2,1)}) custom-call(f32[1]{0:T(128)} %bitcast.87.clip, bf16[8192,768]{1,0:T(8,128)(2,1)} %copy-done.1, f32[8000,768]{1,0:T(8,128)} %bitcast.333, f32[8000,768]{1,0:T(8,128)} %bitcast.334, f32[8000,768]{1,0:T(8,128)} %bitcast.335), custom_call_target="tpu_custom_call" | custom-call | flops 122880000 | bytes 172032000 | tf_op jit(solution)/shard_map/head_adam/pallas_call | solution.py:903
  898.5 68.0 %table_adam.1 = (f32[8000,768]{1,0:T(8,128)}, f32[8000,768]{1,0:T(8,128)}, f32[8000,768]{1,0:T(8,128)}, bf16[8000,768]{1,0:T(8,128)(2,1)}) custom-call(s32[320]{0:T(512)} %reshape.1151.starts, s32[10]{0:T(128)} %broadcast_maximum_fusion.passes, s32[10]{0:T(128)} %copy-done.118, f32[1]{0:T(128)} %bitcast.87.clip, bf16[8704,768]{1,0:T(8,128)(2,1)} %bitcast.318, ...), custom_call_target="tpu_custom_call" | custom-call | flops 12582912000 | bytes 159744000 | tf_op jit(solution)/shard_map/table_adam/pallas_call | solution.py:858
  971.2 6.0 fusion.173
  981.8 11.0 %fusion.169 = (bf16[1,192,6144]{2,1,0:T(8,128)(2,1)}, f32[1,192,6144]{2,1,0:T(8,128)}, f32[1,192,6144]{2,1,0:T(8,128)}, f32[1,192,6144]{2,1,0:T(8,128)}) fusion(f32[1,192,6144]{2,1,0:T(8,128)} %param.39, f32[]{:T(128)} %div.415, bf16[1,192,1536]{2,1,0:T(8,128)(2,1)S(1)} %get-tuple-element.321, bf16[1,192,1536]{2,1,0:T(8,128)(2,1)S(1)} %get-tuple-element.320, ...), kind=kLoop, calls=%fused_computation.501 | loop fusion | flops 29491200 | bytes 33030148 | tf_op jit(solution)/shard_map/convert_element_type | solution.py:1220
  (642 shorter events, 302.0 us)
Async XLA Ops:
  32.5 169.6 %collective-permute-start.2 = (bf16[256,768]{1,0:T(8,128)(2,1)}, bf16[256,768]{1,0:T(8,128)(2,1)}, u32[]{:S(2)}, u32[]{:S(2)}) collective-permute-start(bf16[256,768]{1,0:T(8,128)(2,1)} %get-tuple-element.350), channel_id=1, source_target_pairs={{0,1},{1,2},{2,3},{3,0},{4,5},{5,6},{6,7},{7,4},{8,9},{9,10},{10,1... | collective-permute-start | bytes 1179656 | tf_op jit(solution)/shard_map/ppermute | solution.py:202
  33.7 168.4 %collective-permute-start.1 = (bf16[256,768]{1,0:T(8,128)(2,1)}, bf16[256,768]{1,0:T(8,128)(2,1)}, u32[]{:S(2)}, u32[]{:S(2)}) collective-permute-start(bf16[256,768]{1,0:T(8,128)(2,1)} %get-tuple-element.351), channel_id=1, source_target_pairs={{0,2},{1,3},{2,0},{3,1},{4,6},{5,7},{6,4},{7,5},{8,10},{9,11},{10,... | collective-permute-start | bytes 1179656 | tf_op jit(solution)/shard_map/ppermute | solution.py:202
  36.1 166.0 %collective-permute-start = (bf16[256,768]{1,0:T(8,128)(2,1)}, bf16[256,768]{1,0:T(8,128)(2,1)}, u32[]{:S(2)}, u32[]{:S(2)}) collective-permute-start(bf16[256,768]{1,0:T(8,128)(2,1)} %get-tuple-element.349), channel_id=1, source_target_pairs={{0,3},{1,0},{2,1},{3,2},{4,7},{5,4},{6,5},{7,6},{8,11},{9,8},{10,9... | collective-permute-start | bytes 1179656 | tf_op jit(solution)/shard_map/ppermute | solution.py:202
  229.6 31.6 %collective-permute-start.5 = (bf16[256,768]{1,0:T(8,128)(2,1)}, bf16[256,768]{1,0:T(8,128)(2,1)}, u32[]{:S(2)}, u32[]{:S(2)}) collective-permute-start(bf16[256,768]{1,0:T(8,128)(2,1)} %get-tuple-element.304), channel_id=1, source_target_pairs={{0,16},{16,0},{1,17},{17,1},{2,18},{18,2},{3,19},{19,3},{4,20},{20... | collective-permute-start | bytes 1179656 | tf_op jit(solution)/shard_map/ppermute | solution.py:207
  263.6 36.0 %collective-permute-start.7 = (bf16[256,768]{1,0:T(8,128)(2,1)}, bf16[256,768]{1,0:T(8,128)(2,1)}, u32[]{:S(2)}, u32[]{:S(2)}) collective-permute-start(bf16[256,768]{1,0:T(8,128)(2,1)} %multiply_convert_fusion.3), channel_id=1, source_target_pairs={{0,2},{1,3},{2,0},{3,1},{4,6},{5,7},{6,4},{7,5},{8,10},{9,11},{10,... | collective-permute-start | bytes 1179656 | tf_op jit(solution)/shard_map/ppermute | solution.py:202
  264.8 34.8 %collective-permute-start.6 = (bf16[256,768]{1,0:T(8,128)(2,1)}, bf16[256,768]{1,0:T(8,128)(2,1)}, u32[]{:S(2)}, u32[]{:S(2)}) collective-permute-start(bf16[256,768]{1,0:T(8,128)(2,1)} %multiply_convert_fusion.3), channel_id=1, source_target_pairs={{0,1},{1,2},{2,3},{3,0},{4,5},{5,6},{6,7},{7,4},{8,9},{9,10},{10,1... | collective-permute-start | bytes 1179656 | tf_op jit(solution)/shard_map/ppermute | solution.py:202
  332.4 114.7 %collective-permute-start.16 = (bf16[256,3072]{1,0:T(8,128)(2,1)}, bf16[256,3072]{1,0:T(8,128)(2,1)}, u32[]{:S(2)}, u32[]{:S(2)}) collective-permute-start(bf16[256,3072]{1,0:T(8,128)(2,1)} %get-tuple-element.357), channel_id=1, source_target_pairs={{0,4},{4,0},{8,12},{12,8},{1,5},{5,1},{9,13},{13,9},{2,6},{6,2},{1... | collective-permute-start | bytes 4718600 | tf_op jit(solution)/shard_map/ppermute | solution.py:207
  333.9 116.0 %collective-permute-start.17 = (bf16[256,3072]{1,0:T(8,128)(2,1)}, bf16[256,3072]{1,0:T(8,128)(2,1)}, u32[]{:S(2)}, u32[]{:S(2)}) collective-permute-start(bf16[256,3072]{1,0:T(8,128)(2,1)} %get-tuple-element.358), channel_id=1, source_target_pairs={{0,8},{4,12},{8,0},{12,4},{1,9},{5,13},{9,1},{13,5},{2,10},{6,14},... | collective-permute-start | bytes 4718600 | tf_op jit(solution)/shard_map/ppermute | solution.py:207
  413.7 30.1 %collective-permute-start.13 = (bf16[256,768]{1,0:T(8,128)(2,1)}, bf16[256,768]{1,0:T(8,128)(2,1)}, u32[]{:S(2)}, u32[]{:S(2)}) collective-permute-start(bf16[256,768]{1,0:T(8,128)(2,1)} %get-tuple-element.348), channel_id=1, source_target_pairs={{0,2},{1,3},{2,0},{3,1},{4,6},{5,7},{6,4},{7,5},{8,10},{9,11},{10,... | collective-permute-start | bytes 1179656 | tf_op jit(solution)/shard_map/ppermute | solution.py:202
  414.6 29.2 %collective-permute-start.12 = (bf16[256,768]{1,0:T(8,128)(2,1)}, bf16[256,768]{1,0:T(8,128)(2,1)}, u32[]{:S(2)}, u32[]{:S(2)}) collective-permute-start(bf16[256,768]{1,0:T(8,128)(2,1)} %get-tuple-element.346), channel_id=1, source_target_pairs={{0,3},{1,0},{2,1},{3,2},{4,7},{5,4},{6,5},{7,6},{8,11},{9,8},{10,9... | collective-permute-start | bytes 1179656 | tf_op jit(solution)/shard_map/ppermute | solution.py:202
  427.7 31.9 %collective-permute-start.18 = (bf16[256,3072]{1,0:T(8,128)(2,1)}, bf16[256,3072]{1,0:T(8,128)(2,1)}, u32[]{:S(2)}, u32[]{:S(2)}) collective-permute-start(bf16[256,3072]{1,0:T(8,128)(2,1)} %get-tuple-element.356), channel_id=1, source_target_pairs={{0,12},{4,8},{8,4},{12,0},{1,13},{5,9},{9,5},{13,1},{2,14},{6,10},... | collective-permute-start | bytes 4718600 | tf_op jit(solution)/shard_map/ppermute | solution.py:207
  443.8 49.5 %collective-permute-start.19 = (bf16[4096,768]{1,0:T(8,128)(2,1)}, bf16[4096,768]{1,0:T(8,128)(2,1)}, u32[]{:S(2)}, u32[]{:S(2)}) collective-permute-start(bf16[4096,768]{1,0:T(8,128)(2,1)} %slice.474), channel_id=1, source_target_pairs={{0,16},{16,0},{1,17},{17,1},{2,18},{18,2},{3,19},{19,3},{4,20},{20... | collective-permute-start | bytes 18874376 | tf_op jit(solution)/shard_map/ppermute | solution.py:207
  506.8 101.2 %collective-permute-start.22 = (bf16[1024,768]{1,0:T(8,128)(2,1)}, bf16[1024,768]{1,0:T(8,128)(2,1)}, u32[]{:S(2)}, u32[]{:S(2)}) collective-permute-start(bf16[1024,768]{1,0:T(8,128)(2,1)} %get-tuple-element.316), channel_id=1, source_target_pairs={{0,8},{4,12},{8,0},{12,4},{1,9},{5,13},{9,1},{13,5},{2,10},{6,14},... | collective-permute-start | bytes 4718600 | tf_op jit(solution)/shard_map/ppermute | solution.py:207
  508.3 99.8 %collective-permute-start.21 = (bf16[1024,768]{1,0:T(8,128)(2,1)}, bf16[1024,768]{1,0:T(8,128)(2,1)}, u32[]{:S(2)}, u32[]{:S(2)}) collective-permute-start(bf16[1024,768]{1,0:T(8,128)(2,1)} %get-tuple-element.317), channel_id=1, source_target_pairs={{0,4},{4,0},{8,12},{12,8},{1,5},{5,1},{9,13},{13,9},{2,6},{6,2},{1... | collective-permute-start | bytes 4718600 | tf_op jit(solution)/shard_map/ppermute | solution.py:207
  535.2 35.9 %collective-permute-start.25 = (bf16[256,2304]{1,0:T(8,128)(2,1)}, bf16[256,2304]{1,0:T(8,128)(2,1)}, u32[]{:S(2)}, u32[]{:S(2)}) collective-permute-start(bf16[256,2304]{1,0:T(8,128)(2,1)} %get-tuple-element.381), channel_id=1, source_target_pairs={{0,4},{4,0},{8,12},{12,8},{1,5},{5,1},{9,13},{13,9},{2,6},{6,2},{1... | collective-permute-start | bytes 3538952 | tf_op jit(solution)/shard_map/ppermute | solution.py:207
  537.1 36.4 %collective-permute-start.26 = (bf16[256,2304]{1,0:T(8,128)(2,1)}, bf16[256,2304]{1,0:T(8,128)(2,1)}, u32[]{:S(2)}, u32[]{:S(2)}) collective-permute-start(bf16[256,2304]{1,0:T(8,128)(2,1)} %get-tuple-element.382), channel_id=1, source_target_pairs={{0,8},{4,12},{8,0},{12,4},{1,9},{5,13},{9,1},{13,5},{2,10},{6,14},... | collective-permute-start | bytes 3538952 | tf_op jit(solution)/shard_map/ppermute | solution.py:207
  544.2 51.5 %collective-permute-start.27 = (bf16[256,2304]{1,0:T(8,128)(2,1)}, bf16[256,2304]{1,0:T(8,128)(2,1)}, u32[]{:S(2)}, u32[]{:S(2)}) collective-permute-start(bf16[256,2304]{1,0:T(8,128)(2,1)} %get-tuple-element.380), channel_id=1, source_target_pairs={{0,12},{4,8},{8,4},{12,0},{1,13},{5,9},{9,5},{13,1},{2,14},{6,10},... | collective-permute-start | bytes 3538952 | tf_op jit(solution)/shard_map/ppermute | solution.py:207
  612.9 43.1 %collective-permute-start.23 = (bf16[512,768]{1,0:T(8,128)(2,1)}, bf16[512,768]{1,0:T(8,128)(2,1)}, u32[]{:S(2)}, u32[]{:S(2)}) collective-permute-start(bf16[512,768]{1,0:T(8,128)(2,1)} %slice.484), channel_id=1, source_target_pairs={{0,8},{4,12},{8,0},{12,4},{1,9},{5,13},{9,1},{13,5},{2,10},{6,14},... | collective-permute-start | bytes 2359304 | tf_op jit(solution)/shard_map/ppermute | solution.py:207
  615.3 42.4 %collective-permute-start.24 = (bf16[512,768]{1,0:T(8,128)(2,1)}, bf16[512,768]{1,0:T(8,128)(2,1)}, u32[]{:S(2)}, u32[]{:S(2)}) collective-permute-start(bf16[512,768]{1,0:T(8,128)(2,1)} %slice.486), channel_id=1, source_target_pairs={{0,4},{4,0},{8,12},{12,8},{1,5},{5,1},{9,13},{13,9},{2,6},{6,2},{1... | collective-permute-start | bytes 2359304 | tf_op jit(solution)/shard_map/ppermute | solution.py:207
  619.9 24.5 %collective-permute-start.28 = (bf16[256,768]{0,1:T(8,128)(2,1)}, bf16[256,768]{0,1:T(8,128)(2,1)S(1)}, u32[]{:S(2)}, u32[]{:S(2)}) collective-permute-start(bf16[256,768]{0,1:T(8,128)(2,1)} %pad_maximum_fusion.20), channel_id=1, source_target_pairs={{0,4},{4,0},{8,12},{12,8},{1,5},{5,1},{9,13},{13,9},{2,6},{6,2},{1... | collective-permute-start | bytes 1179656 | tf_op jit(solution)/shard_map/ppermute | solution.py:207
  623.3 27.7 %collective-permute-start.30 = (bf16[256,768]{0,1:T(8,128)(2,1)S(1)}, bf16[256,768]{0,1:T(8,128)(2,1)S(1)}, u32[]{:S(2)}, u32[]{:S(2)}) collective-permute-start(bf16[256,768]{0,1:T(8,128)(2,1)S(1)} %pad_maximum_fusion.22), channel_id=1, source_target_pairs={{0,12},{4,8},{8,4},{12,0},{1,13},{5,9},{9,5},{13,1},{2,14},{6,10},... | collective-permute-start | bytes 1179656 | tf_op jit(solution)/shard_map/ppermute | solution.py:207
  836.5 130.0 %collective-permute-start.31 = (bf16[192,3072]{1,0:T(8,128)(2,1)}, bf16[192,3072]{1,0:T(8,128)(2,1)}, u32[]{:S(2)}, u32[]{:S(2)}) collective-permute-start(bf16[192,3072]{1,0:T(8,128)(2,1)} %concatenate.236), channel_id=1, source_target_pairs={{0,4},{4,0},{8,12},{12,8},{1,5},{5,1},{9,13},{13,9},{2,6},{6,2},{1... | collective-permute-start | bytes 3538952 | tf_op jit(solution)/shard_map/ppermute | solution.py:207
  837.1 129.4 %collective-permute-start.32 = (bf16[192,3072]{1,0:T(8,128)(2,1)}, bf16[192,3072]{1,0:T(8,128)(2,1)}, u32[]{:S(2)}, u32[]{:S(2)}) collective-permute-start(bf16[192,3072]{1,0:T(8,128)(2,1)} %concatenate.236), channel_id=1, source_target_pairs={{0,8},{4,12},{8,0},{12,4},{1,9},{5,13},{9,1},{13,5},{2,10},{6,14},... | collective-permute-start | bytes 3538952 | tf_op jit(solution)/shard_map/ppermute | solution.py:207
  838.5 128.0 %collective-permute-start.33 = (bf16[192,3072]{1,0:T(8,128)(2,1)}, bf16[192,3072]{1,0:T(8,128)(2,1)}, u32[]{:S(2)}, u32[]{:S(2)}) collective-permute-start(bf16[192,3072]{1,0:T(8,128)(2,1)} %concatenate.236), channel_id=1, source_target_pairs={{0,12},{4,8},{8,4},{12,0},{1,13},{5,9},{9,5},{13,1},{2,14},{6,10},... | collective-permute-start | bytes 3538952 | tf_op jit(solution)/shard_map/ppermute | solution.py:207
  (148 other events, 3711.4 us)

commit v7 on v6

--- a/solution.py
+++ b/solution.py
@@ -424,7 +424,7 @@
     )(head, rows, targets)
 
 
-def head_grads_kernel(vocab, order, h_ref, rows_ref, target_ref, lse_ref, factor_ref, g_ref, c_ref, flipped, delta):
+def head_grads_kernel(vocab, order, h_ref, rows_ref, target_ref, lse_ref, factor_ref, mine_ref, theirs_ref, c_ref, flipped, delta):
     step = pl.program_id(0)
     base = order[step] * h_ref.shape[0]
     table = table_block(vocab, base, h_ref)
@@ -441,7 +441,16 @@
         delta[:, span] = (
             (jnp.exp(logits - lse_ref[:, span]) - onehot) * factor_ref[:, span]
         ).astype(LOW)
-    g_ref[...] = jnp.dot(delta[...], rows_ref[...], preferred_element_type=WIDE).astype(LOW)
+    block = jnp.dot(delta[...], rows_ref[...], preferred_element_type=WIDE).astype(LOW)
+
+    @pl.when(step < 8)
+    def _():
+        mine_ref[...] = block
+
+    @pl.when(step >= 8)
+    def _():
+        theirs_ref[...] = block
+
     for c in range(rows_ref.shape[0] // TOKENS):
         span = slice(c * TOKENS, (c + 1) * TOKENS)
         c_ref[:, span] += jnp.dot(flipped[...], delta[:, span], preferred_element_type=WIDE)
@@ -463,13 +472,15 @@
                 once((1, count)),
             ],
             out_specs=[
-                pl.BlockSpec((piece, D), lambda g, order: (g, 0)),
+                pl.BlockSpec((piece, D), lambda g, order: (jnp.minimum(g, 7), 0)),
+                pl.BlockSpec((piece, D), lambda g, order: (jnp.maximum(g - 8, 0), 0)),
                 pl.BlockSpec((D, count), lambda g, order: (0, 0)),
             ],
             scratch_shapes=[pltpu.VMEM((D, piece), LOW), pltpu.VMEM((piece, count), LOW)],
         ),
         out_shape=[
-            jax.ShapeDtypeStruct((16 * piece, D), LOW),
+            jax.ShapeDtypeStruct((8 * piece, D), LOW),
+            jax.ShapeDtypeStruct((8 * piece, D), LOW),
             jax.ShapeDtypeStruct((D, count), WIDE),
         ],
         compiler_params=pltpu.CompilerParams(vmem_limit_bytes=56 << 20),
@@ -497,13 +508,12 @@
     lse = (peak + jnp.log(total)).reshape(-1)
     loss_part = jnp.sum((lse - jnp.sum(parts[:, 2], axis=0).reshape(-1)) * weights_tok)
     factor = weights_tok / token_total
-    grad_head, partial = head_grads(head, gathered, local, lse[None, :], factor[None, :])
+    mine, theirs, partial = head_grads(head, gathered, local, lse[None, :], factor[None, :])
     partial = partial.T.reshape(planes, -1, D)
     grad_rows = partial[0]
     for step in range(1, planes):
         grad_rows = grad_rows + shift(partial[step].astype(LOW), "fsdp", planes - step).astype(WIDE)
-    middle = grad_head.shape[0] // 2
-    return (loss_part, grad_head[:middle], grad_head[middle:], grad_rows)
+    return (loss_part, mine, theirs, grad_rows)
 
 
 def add_low(one, other):

time: 1010 us -> 1020 us (level)
  Pallas kernels: 530 us -> 542 us
    pallas_call x1, Pallas kernels: 53.4 us -> 69.8 us  [head_grads(): pl.pallas_call(functools.partial(head_grads_kernel, vocab), grid_spec=plt...]
  transfers between devices with their start and end apart: 34 -> 34, of which waited for: 10 -> 11; matrix products, arithmetic and copies ran while one was open for 21% -> 20% of each run, Pallas kernels for 33% -> 34%
where the time goes in v7:
time: 1020 us; the launch traced here: 1010 us
  Pallas kernels  542 us (53%)
  local copies, waits for them, and re-layouts  136 us (13%)
  other arithmetic  106 us (10%)
  waiting for transfers between devices  105 us (10%)
  matrix products  80.5 us (8%)
  starting transfers between devices  33.6 us (3%)
    pallas_call x1, Pallas kernels, gather_weights(): pl.pallas_call(functools.partial(weights_kernel, planes, units, rows), ou...  153 us
    pallas_call x1, Pallas kernels, exchange(): pl.pallas_call(functools.partial(exchange_kernel, planes), out_shape=outs...  129 us
    ppermute x22, waiting for transfers between devices, swap(): return lax.ppermute(block, axis, [(i, i ^ mask) for i in range(count)])  75.7 us
    pallas_call x1, Pallas kernels, head_grads(): pl.pallas_call(functools.partial(head_grads_kernel, vocab), grid_spec=plt...  69.8 us
    pallas_call x1, Pallas kernels, table_adam(): pl.pallas_call(functools.partial(table_adam_kernel, lists, length, steps,...  68 us
    pallas_call x1, Pallas kernels, head_adam(): pl.pallas_call(functools.partial(head_adam_kernel, rate, decay), grid_spe...  56.6 us
    ppermute x12, waiting for transfers between devices, shift(): lax.ppermute(block, axis, [(i, (i + distance) % count) for i in range(cou...  29.4 us
    pallas_call x2, Pallas kernels, small_gather(): pl.pallas_call(functools.partial(small_gather_kernel, axes, sizes), out_s...  29.2 us
  transfers between devices with their start and end apart: 34, of which 11 were waited for; matrix products, arithmetic and copies ran while one was open for 20% of the time, Pallas kernels for 34%

profile of v7, /device:TPU:0, one launch (start us, length us, event | category | flops | bytes accessed | tf_op | source)
XLA Modules:
  0.0 1014.1 jit_solution(14481481852199095660)
XLA Ops:
  3.3 11.9 %small_gather_3.1 = (s32[16,2,256]{2,1,0:T(2,128)}, f32[16,3,192]{2,1,0:T(4,128)}) custom-call(s32[2,256]{1,0:T(2,128)} %pad_add_fusion.4.refs_0_, f32[3,192]{1,0:T(4,128)} %bitcast.385), custom_call_target="tpu_custom_call" | custom-call | tf_op jit(solution)/shard_map/small_gather_3/pallas_call | solution.py:972
  16.1 13.6 %gather_fusion = bf16[1024,768]{1,0:T(8,128)(2,1)} fusion(f32[8000,768]{1,0:T(8,128)} %w.1, s32[1024]{0:T(1024)S(1)} %broadcast_clamp_fusion), kind=kCustom, calls=%fused_computation | custom fusion | bytes 3149824 | tf_op jit(solution)/shard_map/jit(_take)/gather | solution.py:1067
  48.5 152.9 %gather_weights.1 = (bf16[768,2304]{1,0:T(8,128)(2,1)}, bf16[768,768]{1,0:T(8,128)(2,1)}, bf16[768,6144]{1,0:T(8,128)(2,1)}, bf16[3072,768]{1,0:T(8,128)(2,1)}) custom-call(bf16[192,2304]{1,0:T(8,128)(2,1)} %convert_bitcast_fusion.2.refs_0_, bf16[192,768]{1,0:T(8,128)(2,1)} %convert_bitcast_fusion.3.refs_1_, bf16[192,6144]{1,0:T(8,128)(2,1)} %convert_bitcast_fusion.refs_2_, ...), custom_call_target="tpu_custom_call" | custom-call | tf_op jit(solution)/shard_map/gather_weights/pallas_call | solution.py:147
  216.9 5.6 fusion.61
  284.8 14.8 %collective-permute-done.7 = bf16[256,768]{1,0:T(8,128)(2,1)} collective-permute-done((bf16[256,768]{1,0:T(8,128)(2,1)}, bf16[256,768]{1,0:T(8,128)(2,1)}, u32[]{:S(2)}, u32[]{:S(2)}) %collective-permute-start.7) | collective-permute-done | bytes 393248 | tf_op jit(solution)/shard_map/ppermute | solution.py:202
  301.1 27.0 %head_stats.1 = f32[8,1024]{1,0:T(8,128)S(1)} custom-call(f32[8000,768]{1,0:T(8,128)} %bitcast.331, bf16[1024,768]{1,0:T(8,128)(2,1)S(1)} %pad_maximum_fusion.5.rows_ref, s32[1,1024]{1,0:T(1,128)S(1)} %and_select_fusion.target_ref), custom_call_target="tpu_custom_call" | custom-call | flops 12582912000 | bytes 24576000 | tf_op jit(solution)/shard_map/head_stats/pallas_call | solution.py:413
  353.4 69.8 %head_grads.1 = (bf16[4096,768]{1,0:T(8,128)(2,1)}, bf16[4096,768]{1,0:T(8,128)(2,1)}, f32[768,1024]{1,0:T(8,128)}) custom-call(s32[16]{0:T(128)} %stack.161.order, f32[8000,768]{1,0:T(8,128)} %bitcast.332, bf16[1024,768]{1,0:T(8,128)(2,1)} %copy-done.8, s32[1,1024]{1,0:T(1,128)} %copy-done.13, f32[1,1024]{1,0:T(1,128)} %bitcast.390, f32[1,1024]{1,0:T(1,128)} %bitcast.389), custom_call_target="tpu_custom_call" | custom-call | flops 37748736000 | bytes 49152000 | tf_op jit(solution)/shard_map/head_grads/pallas_call | solution.py:462
  437.0 7.2 collective-permute-done.14
  467.1 9.0 collective-permute-done.18
  479.9 8.4 fusion.166
  488.4 6.4 multiply_reduce_fusion.9
  509.8 9.1 add_convert_fusion
  566.1 21.5 %collective-permute-done.25 = bf16[256,2304]{1,0:T(8,128)(2,1)} collective-permute-done((bf16[256,2304]{1,0:T(8,128)(2,1)}, bf16[256,2304]{1,0:T(8,128)(2,1)}, u32[]{:S(2)}, u32[]{:S(2)}) %collective-permute-start.25) | collective-permute-done | bytes 1179680 | tf_op jit(solution)/shard_map/ppermute | solution.py:207
  592.3 19.8 %collective-permute-done.27 = bf16[256,2304]{1,0:T(8,128)(2,1)} collective-permute-done((bf16[256,2304]{1,0:T(8,128)(2,1)}, bf16[256,2304]{1,0:T(8,128)(2,1)}, u32[]{:S(2)}, u32[]{:S(2)}) %collective-permute-start.27) | collective-permute-done | bytes 1179680 | tf_op jit(solution)/shard_map/ppermute | solution.py:207
  619.0 5.5 convolution_convert_fusion.refs_0_
  642.2 18.7 %collective-permute-done.28 = bf16[256,768]{0,1:T(8,128)(2,1)S(1)} collective-permute-done((bf16[256,768]{0,1:T(8,128)(2,1)}, bf16[256,768]{0,1:T(8,128)(2,1)S(1)}, u32[]{:S(2)}, u32[]{:S(2)}) %collective-permute-start.28) | collective-permute-done | bytes 393248 | tf_op jit(solution)/shard_map/ppermute | solution.py:207
  661.0 6.4 collective-permute-done.30
  675.6 128.6 %exchange.1 = (bf16[2,4,4,272,768]{4,3,2,1,0:T(8,128)(2,1)S(1)}, bf16[8192,768]{1,0:T(8,128)(2,1)S(1)}, bf16[2,192,1536]{2,1,0:T(8,128)(2,1)S(1)}, bf16[2,192,76...) custom-call(bf16[272,768]{1,0:T(8,128)(2,1)S(1)} %concatenate.225.rows_ref, ...), custom_call_target="tpu_custom_call" | custom-call | tf_op jit(solution)/shard_map/exchange/pallas_call | solution.py:669
  816.2 8.6 table_square.1
  828.3 17.3 %small_gather_4.1 = f32[32,2,128]{2,1,0:T(2,128)} custom-call(f32[2,128]{1,0:T(2,128)} %mul.1611.refs_0_), custom_call_target="tpu_custom_call" | custom-call | tf_op jit(solution)/shard_map/small_gather_4/pallas_call | solution.py:972
  853.6 56.6 %head_adam.1 = (f32[8000,768]{1,0:T(8,128)}, f32[8000,768]{1,0:T(8,128)}, f32[8000,768]{1,0:T(8,128)}, bf16[8000,768]{1,0:T(8,128)(2,1)}) custom-call(f32[1]{0:T(128)} %bitcast.87.clip, bf16[8192,768]{1,0:T(8,128)(2,1)} %copy-done.1, f32[8000,768]{1,0:T(8,128)} %bitcast.333, f32[8000,768]{1,0:T(8,128)} %bitcast.334, f32[8000,768]{1,0:T(8,128)} %bitcast.335), custom_call_target="tpu_custom_call" | custom-call | flops 122880000 | bytes 172032000 | tf_op jit(solution)/shard_map/head_adam/pallas_call | solution.py:913
  911.4 68.0 %table_adam.1 = (f32[8000,768]{1,0:T(8,128)}, f32[8000,768]{1,0:T(8,128)}, f32[8000,768]{1,0:T(8,128)}, bf16[8000,768]{1,0:T(8,128)(2,1)}) custom-call(s32[320]{0:T(512)} %reshape.1151.starts, s32[10]{0:T(128)} %broadcast_maximum_fusion.passes, s32[10]{0:T(128)} %copy-done.118, f32[1]{0:T(128)} %bitcast.87.clip, bf16[8704,768]{1,0:T(8,128)(2,1)} %bitcast.318, ...), custom_call_target="tpu_custom_call" | custom-call | flops 12582912000 | bytes 159744000 | tf_op jit(solution)/shard_map/table_adam/pallas_call | solution.py:868
  984.1 6.0 fusion.173
  994.7 11.0 %fusion.169 = (bf16[1,192,6144]{2,1,0:T(8,128)(2,1)}, f32[1,192,6144]{2,1,0:T(8,128)}, f32[1,192,6144]{2,1,0:T(8,128)}, f32[1,192,6144]{2,1,0:T(8,128)}) fusion(f32[1,192,6144]{2,1,0:T(8,128)} %param.39, f32[]{:T(128)} %div.415, bf16[1,192,1536]{2,1,0:T(8,128)(2,1)S(1)} %get-tuple-element.323, bf16[1,192,1536]{2,1,0:T(8,128)(2,1)S(1)} %get-tuple-element.322, ...), kind=kLoop, calls=%fused_computation.501 | loop fusion | flops 29491200 | bytes 33030148 | tf_op jit(solution)/shard_map/convert_element_type | solution.py:1230
  (641 shorter events, 300.4 us)
Async XLA Ops:
  32.5 169.6 %collective-permute-start.2 = (bf16[256,768]{1,0:T(8,128)(2,1)}, bf16[256,768]{1,0:T(8,128)(2,1)}, u32[]{:S(2)}, u32[]{:S(2)}) collective-permute-start(bf16[256,768]{1,0:T(8,128)(2,1)} %get-tuple-element.352), channel_id=1, source_target_pairs={{0,1},{1,2},{2,3},{3,0},{4,5},{5,6},{6,7},{7,4},{8,9},{9,10},{10,1... | collective-permute-start | bytes 1179656 | tf_op jit(solution)/shard_map/ppermute | solution.py:202
  33.7 168.4 %collective-permute-start.1 = (bf16[256,768]{1,0:T(8,128)(2,1)}, bf16[256,768]{1,0:T(8,128)(2,1)}, u32[]{:S(2)}, u32[]{:S(2)}) collective-permute-start(bf16[256,768]{1,0:T(8,128)(2,1)} %get-tuple-element.353), channel_id=1, source_target_pairs={{0,2},{1,3},{2,0},{3,1},{4,6},{5,7},{6,4},{7,5},{8,10},{9,11},{10,... | collective-permute-start | bytes 1179656 | tf_op jit(solution)/shard_map/ppermute | solution.py:202
  36.1 166.0 %collective-permute-start = (bf16[256,768]{1,0:T(8,128)(2,1)}, bf16[256,768]{1,0:T(8,128)(2,1)}, u32[]{:S(2)}, u32[]{:S(2)}) collective-permute-start(bf16[256,768]{1,0:T(8,128)(2,1)} %get-tuple-element.351), channel_id=1, source_target_pairs={{0,3},{1,0},{2,1},{3,2},{4,7},{5,4},{6,5},{7,6},{8,11},{9,8},{10,9... | collective-permute-start | bytes 1179656 | tf_op jit(solution)/shard_map/ppermute | solution.py:202
  229.6 31.6 %collective-permute-start.5 = (bf16[256,768]{1,0:T(8,128)(2,1)}, bf16[256,768]{1,0:T(8,128)(2,1)}, u32[]{:S(2)}, u32[]{:S(2)}) collective-permute-start(bf16[256,768]{1,0:T(8,128)(2,1)} %get-tuple-element.306), channel_id=1, source_target_pairs={{0,16},{16,0},{1,17},{17,1},{2,18},{18,2},{3,19},{19,3},{4,20},{20... | collective-permute-start | bytes 1179656 | tf_op jit(solution)/shard_map/ppermute | solution.py:207
  263.6 36.0 %collective-permute-start.7 = (bf16[256,768]{1,0:T(8,128)(2,1)}, bf16[256,768]{1,0:T(8,128)(2,1)}, u32[]{:S(2)}, u32[]{:S(2)}) collective-permute-start(bf16[256,768]{1,0:T(8,128)(2,1)} %multiply_convert_fusion.3), channel_id=1, source_target_pairs={{0,2},{1,3},{2,0},{3,1},{4,6},{5,7},{6,4},{7,5},{8,10},{9,11},{10,... | collective-permute-start | bytes 1179656 | tf_op jit(solution)/shard_map/ppermute | solution.py:202
  264.8 34.8 %collective-permute-start.6 = (bf16[256,768]{1,0:T(8,128)(2,1)}, bf16[256,768]{1,0:T(8,128)(2,1)}, u32[]{:S(2)}, u32[]{:S(2)}) collective-permute-start(bf16[256,768]{1,0:T(8,128)(2,1)} %multiply_convert_fusion.3), channel_id=1, source_target_pairs={{0,1},{1,2},{2,3},{3,0},{4,5},{5,6},{6,7},{7,4},{8,9},{9,10},{10,1... | collective-permute-start | bytes 1179656 | tf_op jit(solution)/shard_map/ppermute | solution.py:202
  332.4 129.1 %collective-permute-start.16 = (bf16[256,3072]{1,0:T(8,128)(2,1)}, bf16[256,3072]{1,0:T(8,128)(2,1)}, u32[]{:S(2)}, u32[]{:S(2)}) collective-permute-start(bf16[256,3072]{1,0:T(8,128)(2,1)} %get-tuple-element.359), channel_id=1, source_target_pairs={{0,4},{4,0},{8,12},{12,8},{1,5},{5,1},{9,13},{13,9},{2,6},{6,2},{1... | collective-permute-start | bytes 4718600 | tf_op jit(solution)/shard_map/ppermute | solution.py:207
  333.9 130.5 %collective-permute-start.17 = (bf16[256,3072]{1,0:T(8,128)(2,1)}, bf16[256,3072]{1,0:T(8,128)(2,1)}, u32[]{:S(2)}, u32[]{:S(2)}) collective-permute-start(bf16[256,3072]{1,0:T(8,128)(2,1)} %get-tuple-element.360), channel_id=1, source_target_pairs={{0,8},{4,12},{8,0},{12,4},{1,9},{5,13},{9,1},{13,5},{2,10},{6,14},... | collective-permute-start | bytes 4718600 | tf_op jit(solution)/shard_map/ppermute | solution.py:207
  430.1 28.2 %collective-permute-start.13 = (bf16[256,768]{1,0:T(8,128)(2,1)}, bf16[256,768]{1,0:T(8,128)(2,1)}, u32[]{:S(2)}, u32[]{:S(2)}) collective-permute-start(bf16[256,768]{1,0:T(8,128)(2,1)} %get-tuple-element.350), channel_id=1, source_target_pairs={{0,2},{1,3},{2,0},{3,1},{4,6},{5,7},{6,4},{7,5},{8,10},{9,11},{10,... | collective-permute-start | bytes 1179656 | tf_op jit(solution)/shard_map/ppermute | solution.py:202
  431.1 27.2 %collective-permute-start.12 = (bf16[256,768]{1,0:T(8,128)(2,1)}, bf16[256,768]{1,0:T(8,128)(2,1)}, u32[]{:S(2)}, u32[]{:S(2)}) collective-permute-start(bf16[256,768]{1,0:T(8,128)(2,1)} %get-tuple-element.348), channel_id=1, source_target_pairs={{0,3},{1,0},{2,1},{3,2},{4,7},{5,4},{6,5},{7,6},{8,11},{9,8},{10,9... | collective-permute-start | bytes 1179656 | tf_op jit(solution)/shard_map/ppermute | solution.py:202
  444.2 31.9 %collective-permute-start.18 = (bf16[256,3072]{1,0:T(8,128)(2,1)}, bf16[256,3072]{1,0:T(8,128)(2,1)}, u32[]{:S(2)}, u32[]{:S(2)}) collective-permute-start(bf16[256,3072]{1,0:T(8,128)(2,1)} %get-tuple-element.358), channel_id=1, source_target_pairs={{0,12},{4,8},{8,4},{12,0},{1,13},{5,9},{9,5},{13,1},{2,14},{6,10},... | collective-permute-start | bytes 4718600 | tf_op jit(solution)/shard_map/ppermute | solution.py:207
  458.3 51.4 %collective-permute-start.19 = (bf16[4096,768]{1,0:T(8,128)(2,1)}, bf16[4096,768]{1,0:T(8,128)(2,1)}, u32[]{:S(2)}, u32[]{:S(2)}) collective-permute-start(bf16[4096,768]{1,0:T(8,128)(2,1)} %get-tuple-element.82), channel_id=1, source_target_pairs={{0,16},{16,0},{1,17},{17,1},{2,18},{18,2},{3,19},{19,3},{4,20},{20... | collective-permute-start | bytes 18874376 | tf_op jit(solution)/shard_map/ppermute | solution.py:207
  523.3 101.2 %collective-permute-start.22 = (bf16[1024,768]{1,0:T(8,128)(2,1)}, bf16[1024,768]{1,0:T(8,128)(2,1)}, u32[]{:S(2)}, u32[]{:S(2)}) collective-permute-start(bf16[1024,768]{1,0:T(8,128)(2,1)} %get-tuple-element.318), channel_id=1, source_target_pairs={{0,8},{4,12},{8,0},{12,4},{1,9},{5,13},{9,1},{13,5},{2,10},{6,14},... | collective-permute-start | bytes 4718600 | tf_op jit(solution)/shard_map/ppermute | solution.py:207
  524.8 99.7 %collective-permute-start.21 = (bf16[1024,768]{1,0:T(8,128)(2,1)}, bf16[1024,768]{1,0:T(8,128)(2,1)}, u32[]{:S(2)}, u32[]{:S(2)}) collective-permute-start(bf16[1024,768]{1,0:T(8,128)(2,1)} %get-tuple-element.319), channel_id=1, source_target_pairs={{0,4},{4,0},{8,12},{12,8},{1,5},{5,1},{9,13},{13,9},{2,6},{6,2},{1... | collective-permute-start | bytes 4718600 | tf_op jit(solution)/shard_map/ppermute | solution.py:207
  551.7 35.9 %collective-permute-start.25 = (bf16[256,2304]{1,0:T(8,128)(2,1)}, bf16[256,2304]{1,0:T(8,128)(2,1)}, u32[]{:S(2)}, u32[]{:S(2)}) collective-permute-start(bf16[256,2304]{1,0:T(8,128)(2,1)} %get-tuple-element.383), channel_id=1, source_target_pairs={{0,4},{4,0},{8,12},{12,8},{1,5},{5,1},{9,13},{13,9},{2,6},{6,2},{1... | collective-permute-start | bytes 3538952 | tf_op jit(solution)/shard_map/ppermute | solution.py:207
  553.5 36.4 %collective-permute-start.26 = (bf16[256,2304]{1,0:T(8,128)(2,1)}, bf16[256,2304]{1,0:T(8,128)(2,1)}, u32[]{:S(2)}, u32[]{:S(2)}) collective-permute-start(bf16[256,2304]{1,0:T(8,128)(2,1)} %get-tuple-element.384), channel_id=1, source_target_pairs={{0,8},{4,12},{8,0},{12,4},{1,9},{5,13},{9,1},{13,5},{2,10},{6,14},... | collective-permute-start | bytes 3538952 | tf_op jit(solution)/shard_map/ppermute | solution.py:207
  560.7 51.5 %collective-permute-start.27 = (bf16[256,2304]{1,0:T(8,128)(2,1)}, bf16[256,2304]{1,0:T(8,128)(2,1)}, u32[]{:S(2)}, u32[]{:S(2)}) collective-permute-start(bf16[256,2304]{1,0:T(8,128)(2,1)} %get-tuple-element.382), channel_id=1, source_target_pairs={{0,12},{4,8},{8,4},{12,0},{1,13},{5,9},{9,5},{13,1},{2,14},{6,10},... | collective-permute-start | bytes 3538952 | tf_op jit(solution)/shard_map/ppermute | solution.py:207
  629.4 43.1 %collective-permute-start.23 = (bf16[512,768]{1,0:T(8,128)(2,1)}, bf16[512,768]{1,0:T(8,128)(2,1)}, u32[]{:S(2)}, u32[]{:S(2)}) collective-permute-start(bf16[512,768]{1,0:T(8,128)(2,1)} %slice.476), channel_id=1, source_target_pairs={{0,8},{4,12},{8,0},{12,4},{1,9},{5,13},{9,1},{13,5},{2,10},{6,14},... | collective-permute-start | bytes 2359304 | tf_op jit(solution)/shard_map/ppermute | solution.py:207
  631.8 42.4 %collective-permute-start.24 = (bf16[512,768]{1,0:T(8,128)(2,1)}, bf16[512,768]{1,0:T(8,128)(2,1)}, u32[]{:S(2)}, u32[]{:S(2)}) collective-permute-start(bf16[512,768]{1,0:T(8,128)(2,1)} %slice.478), channel_id=1, source_target_pairs={{0,4},{4,0},{8,12},{12,8},{1,5},{5,1},{9,13},{13,9},{2,6},{6,2},{1... | collective-permute-start | bytes 2359304 | tf_op jit(solution)/shard_map/ppermute | solution.py:207
  636.4 24.5 %collective-permute-start.28 = (bf16[256,768]{0,1:T(8,128)(2,1)}, bf16[256,768]{0,1:T(8,128)(2,1)S(1)}, u32[]{:S(2)}, u32[]{:S(2)}) collective-permute-start(bf16[256,768]{0,1:T(8,128)(2,1)} %pad_maximum_fusion.20), channel_id=1, source_target_pairs={{0,4},{4,0},{8,12},{12,8},{1,5},{5,1},{9,13},{13,9},{2,6},{6,2},{1... | collective-permute-start | bytes 1179656 | tf_op jit(solution)/shard_map/ppermute | solution.py:207
  639.7 27.7 %collective-permute-start.30 = (bf16[256,768]{0,1:T(8,128)(2,1)S(1)}, bf16[256,768]{0,1:T(8,128)(2,1)S(1)}, u32[]{:S(2)}, u32[]{:S(2)}) collective-permute-start(bf16[256,768]{0,1:T(8,128)(2,1)S(1)} %pad_maximum_fusion.22), channel_id=1, source_target_pairs={{0,12},{4,8},{8,4},{12,0},{1,13},{5,9},{9,5},{13,1},{2,14},{6,10},... | collective-permute-start | bytes 1179656 | tf_op jit(solution)/shard_map/ppermute | solution.py:207
  849.4 130.0 %collective-permute-start.31 = (bf16[192,3072]{1,0:T(8,128)(2,1)}, bf16[192,3072]{1,0:T(8,128)(2,1)}, u32[]{:S(2)}, u32[]{:S(2)}) collective-permute-start(bf16[192,3072]{1,0:T(8,128)(2,1)} %concatenate.236), channel_id=1, source_target_pairs={{0,4},{4,0},{8,12},{12,8},{1,5},{5,1},{9,13},{13,9},{2,6},{6,2},{1... | collective-permute-start | bytes 3538952 | tf_op jit(solution)/shard_map/ppermute | solution.py:207
  850.0 129.4 %collective-permute-start.32 = (bf16[192,3072]{1,0:T(8,128)(2,1)}, bf16[192,3072]{1,0:T(8,128)(2,1)}, u32[]{:S(2)}, u32[]{:S(2)}) collective-permute-start(bf16[192,3072]{1,0:T(8,128)(2,1)} %concatenate.236), channel_id=1, source_target_pairs={{0,8},{4,12},{8,0},{12,4},{1,9},{5,13},{9,1},{13,5},{2,10},{6,14},... | collective-permute-start | bytes 3538952 | tf_op jit(solution)/shard_map/ppermute | solution.py:207
  851.4 128.0 %collective-permute-start.33 = (bf16[192,3072]{1,0:T(8,128)(2,1)}, bf16[192,3072]{1,0:T(8,128)(2,1)}, u32[]{:S(2)}, u32[]{:S(2)}) collective-permute-start(bf16[192,3072]{1,0:T(8,128)(2,1)} %concatenate.236), channel_id=1, source_target_pairs={{0,12},{4,8},{8,4},{12,0},{1,13},{5,9},{9,5},{13,1},{2,14},{6,10},... | collective-permute-start | bytes 3538952 | tf_op jit(solution)/shard_map/ppermute | solution.py:207
  (148 other events, 3824.4 us)
